TPU v7x, 256 devices: a whole 4x4x8 slice. The times are simulated.
256 devices in a mesh: expert: 64 (over z, x, y_hi), replica: 4 (over y_lo, core).
Axes of the slice: x: 4, y: 4 (y_hi: 2, y_lo: 2; y = y_hi * 2 + y_lo), z: 8, core: 2. Of those that a mesh axis runs over, the one named last changes fastest.
Arguments:
- tokens: bfloat16 [32768, 1024], P(('expert', 'replica')), may hold values from -6 to 6
- upstream: bfloat16 [32768, 1024], P(('expert', 'replica')), may hold values from -2 to 2
- expert_ids: int32 [32768, 2], P(('expert', 'replica')), may hold values from 0 to 63, as said below
- slot_index: int32 [32768, 2], P(('expert', 'replica')), may hold values from -1 to 4, as said below
- gate_weights: float32 [32768, 2], P(('expert', 'replica')), may hold values from 0.2 to 1
- in_weight: bfloat16 [64, 1024, 4096], P('expert', None, 'replica'), may hold values from -0.1875 to 0.1875
- out_weight: bfloat16 [64, 4096, 1024], P('expert', 'replica'), may hold values from -0.09375 to 0.09375
Outputs:
- token_grad: bfloat16 [32768, 1024], P(('expert', 'replica'))
- grad_in: bfloat16 [64, 1024, 4096], P('expert', None, 'replica')
- grad_out: bfloat16 [64, 4096, 1024], P('expert', 'replica')
Inputs may be any that keep to these rules, and one draw needn't show every extreme that they name: `expert_ids`: each token names two different experts. `slot_index`: the number of earlier assignments of the same group to the same expert, counted in token order then in column order, or -1 where that number is 5 or more; in every group some expert has all 5 slots filled.
All inputs are finite; a program needn't handle non-finite values.
Results may differ from a plain program's by a relative error of at most 0.014.
Values may be sent and summed in bfloat16 or wider, within the bound.
No kernel may reach another device: no remote copies, remote signals or barrier semaphores. Data moves between devices by JAX's collectives and lax.ppermute only.
A program may use at most 128 MiB of HBM per device.

v0:
```python
import jax
import jax.numpy as jnp
from jax import lax
from jax.sharding import PartitionSpec as P


def smooth_gate(value):
    return jax.nn.gelu(value, approximate=True)


def hidden_step(input_rows, grad_rows, weight_in, weight_out):
    hidden = jnp.dot(input_rows, weight_in, preferred_element_type=jnp.float32)
    active, pullback = jax.vjp(smooth_gate, hidden)
    carried = lax.dot_general(
        grad_rows, weight_out, (((1,), (1,)), ((), ())), preferred_element_type=jnp.float32
    )
    grad_hidden = pullback(carried)[0].astype(jnp.bfloat16)
    return (active.astype(jnp.bfloat16), grad_hidden)


def shards(tokens, upstream, expert_ids, slot_index, gate_weights, in_weight, out_weight):
    token_count, feature_width = tokens.shape
    expert_count = lax.axis_size("expert")
    capacity = 5 * token_count // (2 * expert_count)
    columns = expert_count * capacity
    target = expert_ids * capacity + slot_index
    keep_mask = slot_index >= 0
    column_ids = lax.broadcasted_iota(jnp.int32, (1, 1, columns), 2)
    one_hot = jnp.where(
        (target[:, :, None] == column_ids) & keep_mask[:, :, None], 1.0, 0.0
    ).astype(jnp.float32)
    placing = jnp.sum(one_hot, axis=1)
    weighted = jnp.sum(one_hot * gate_weights[:, :, None], axis=1)
    place_half = placing.astype(jnp.bfloat16)
    sent_tokens = jnp.einsum(
        "tc,td->cd", place_half, tokens, preferred_element_type=jnp.float32
    ).astype(jnp.bfloat16)
    sent_grads = jnp.einsum(
        "tc,td->cd", weighted, upstream.astype(jnp.float32), precision=lax.Precision.HIGHEST
    ).astype(jnp.bfloat16)
    got_tokens, got_grads = (
        lax.all_to_all(
            sent_tokens.reshape(expert_count, capacity, feature_width),
            "expert",
            split_axis=0,
            concat_axis=0,
            tiled=True,
        ),
        lax.all_to_all(
            sent_grads.reshape(expert_count, capacity, feature_width),
            "expert",
            split_axis=0,
            concat_axis=0,
            tiled=True,
        ),
    )
    expert_rows = got_tokens.reshape(columns, feature_width)
    expert_grads = got_grads.reshape(columns, feature_width)
    local_in = in_weight[0]
    local_out = out_weight[0]
    full_in, full_out = (
        lax.all_gather(local_in, "replica", axis=1, tiled=True),
        lax.all_gather(local_out, "replica", axis=0, tiled=True),
    )
    active, grad_hidden = hidden_step(expert_rows, expert_grads, full_in, full_out)
    returned = lax.dot_general(
        grad_hidden, full_in, (((1,), (1,)), ((), ())), preferred_element_type=jnp.float32
    ).astype(jnp.bfloat16)
    grad_output = lax.psum_scatter(
        jnp.einsum("rf,rd->fd", active, expert_grads, preferred_element_type=jnp.float32).astype(
            jnp.bfloat16
        ),
        "replica",
        scatter_dimension=0,
        tiled=True,
    )
    grad_input = (
        lax.psum_scatter(
            jnp.einsum(
                "rf,rd->fd", grad_hidden, expert_rows, preferred_element_type=jnp.float32
            ).astype(jnp.bfloat16),
            "replica",
            scatter_dimension=0,
            tiled=True,
        )
        .astype(jnp.float32)
        .T
    )
    arrived = lax.all_to_all(
        returned.reshape(expert_count, capacity, feature_width),
        "expert",
        split_axis=0,
        concat_axis=0,
        tiled=True,
    )
    token_grad = jnp.einsum(
        "tc,cd->td",
        place_half,
        arrived.reshape(columns, feature_width),
        preferred_element_type=jnp.float32,
    ).astype(jnp.bfloat16)
    return (token_grad, grad_input.astype(jnp.bfloat16)[None], grad_output[None])


def solution(mesh):
    return jax.shard_map(
        shards,
        mesh=mesh,
        in_specs=(
            P(("expert", "replica"), None),
            P(("expert", "replica"), None),
            P(("expert", "replica"), None),
            P(("expert", "replica"), None),
            P(("expert", "replica"), None),
            P("expert", None, "replica"),
            P("expert", "replica", None),
        ),
        out_specs=(
            P(("expert", "replica"), None),
            P("expert", None, "replica"),
            P("expert", "replica", None),
        ),
        check_vma=False,
    )
```

profile of v0, /device:TPU:32, one launch (start us, length us, event | category | flops | bytes accessed | tf_op | source)
XLA Modules:
  0.0 411.7 jit_solution(12895841442688547127)
XLA Ops:
  7.2 0.0 copy-start
  7.2 0.0 copy-start.1
  7.2 0.0 all-gather.7.cloned.1.call-start
  7.2 0.7 all-gather.7.cloned.1.call-update
  7.9 0.0 all-gather.5.cloned.1.call-start
  8.0 0.7 all-gather.5.cloned.1.call-update
  8.7 0.7 broadcast_compare_fusion
  9.4 0.7 multiply_add_fusion
  10.1 0.8 fusion.22
  10.9 0.0 copy-done
  10.9 0.7 convolution_convert_fusion.3
  11.5 1.2 reshape.27
  12.8 14.2 %all-to-all-start = ((bf16[64,5,1024]{2,1,0:T(8,128)(2,1)}), bf16[64,5,1024]{2,1,0:T(8,128)(2,1)S(1)}, u32[]{:S(2)}, u32[]{:S(2)}) async-start(bf16[64,5,1024]{2,1,0:T(8,128)(2,1)} %reshape.27), calls=%async_computation | async-start | bytes 2097152 | tf_op jit(solution)/shard_map/all_to_all | solution.py:49
  27.0 0.0 copy-done.1
  27.0 0.3 convolution_convert_fusion.2
  27.3 1.2 reshape.29
  28.5 28.7 %all-to-all-done = bf16[64,5,1024]{2,1,0:T(8,128)(2,1)S(1)} async-done(((bf16[64,5,1024]{2,1,0:T(8,128)(2,1)}), bf16[64,5,1024]{2,1,0:T(8,128)(2,1)S(1)}, u32[]{:S(2)}, u32[]{:S(2)}) %all-to-all-start) | async-done | bytes 655392 | tf_op jit(solution)/shard_map/all_to_all | solution.py:49
  57.3 5.9 %all-to-all-start.1 = ((bf16[64,5,1024]{2,1,0:T(8,128)(2,1)}), bf16[64,5,1024]{2,1,0:T(8,128)(2,1)S(1)}, u32[]{:S(2)}, u32[]{:S(2)}) async-start(bf16[64,5,1024]{2,1,0:T(8,128)(2,1)} %reshape.29), calls=%async_computation.1 | async-start | bytes 2097152 | tf_op jit(solution)/shard_map/all_to_all | solution.py:42
  63.2 0.0 reduce-scatter.3.cloned.1.call-start
  63.3 0.3 reshape.28
  63.6 29.1 %all-to-all-done.1 = bf16[64,5,1024]{2,1,0:T(8,128)(2,1)S(1)} async-done(((bf16[64,5,1024]{2,1,0:T(8,128)(2,1)}), bf16[64,5,1024]{2,1,0:T(8,128)(2,1)S(1)}, u32[]{:S(2)}, u32[]{:S(2)}) %all-to-all-start.1) | async-done | bytes 655392 | tf_op jit(solution)/shard_map/all_to_all | solution.py:42
  92.6 0.3 reshape.30
  92.9 24.9 %all-gather.7.cloned.1.call-done = bf16[1,1024,4096]{2,1,0:T(8,128)(2,1)} async-done(((bf16[1,1024,1024]{2,1,0:T(8,128)(2,1)}), bf16[1,1024,4096]{2,1,0:T(8,128)(2,1)}) %all-gather.7.cloned.1.call-update) | async-done | bytes 8388624 | tf_op jit(solution)/shard_map/all_gather | solution.py:62
  117.8 8.1 %fusion.2 = f32[320,4096]{1,0:T(8,128)} fusion(bf16[320,1024]{1,0:T(8,128)(2,1)S(1)} %reshape.30, bf16[1,1024,4096]{2,1,0:T(8,128)(2,1)} %all-gather.7.cloned.1.call-done), kind=kOutput, calls=%fused_computation.2 | convolution fusion | flops 2684354560 | bytes 14286848 | tf_op jit(solution)/shard_map/dot_general | solution.py:12
  125.9 78.3 %all-gather.5.cloned.1.call-done = bf16[1,4096,1024]{2,1,0:T(8,128)(2,1)} async-done(((bf16[1,1024,1024]{2,1,0:T(8,128)(2,1)}), bf16[1,4096,1024]{2,1,0:T(8,128)(2,1)}) %all-gather.5.cloned.1.call-update) | async-done | bytes 8388624 | tf_op jit(solution)/shard_map/all_gather | solution.py:63
  204.2 12.0 %fusion.12 = bf16[320,4096]{1,0:T(8,128)(2,1)S(1)} fusion(f32[320,4096]{1,0:T(8,128)} %fusion.2, bf16[320,1024]{1,0:T(8,128)(2,1)S(1)} %reshape.28, bf16[1,4096,1024]{2,1,0:T(8,128)(2,1)} %all-gather.5.cloned.1.call-done), kind=kOutput, calls=%fused_computation.16 | convolution fusion | flops 2710568960 | bytes 16908288 | tf_op jit(solution)/shard_map/dot_general | solution.py:14
  216.1 0.0 copy-start.2
  216.1 1.5 copy-done.2
  217.6 6.7 %convolution_convert_fusion.1 = bf16[4096,1024]{1,0:T(8,128)(2,1)} fusion(bf16[320,4096]{1,0:T(8,128)(2,1)S(1)} %fusion.12, bf16[320,1024]{1,0:T(8,128)(2,1)S(1)} %reshape.30), kind=kOutput, calls=%fused_computation.7 | convolution fusion | flops 2688548864 | bytes 11665408 | tf_op jit(solution)/shard_map/rf,rd->fd/dot_general | solution.py:79
  224.3 0.0 reduce-scatter.3.cloned.1.call-update
  224.3 0.2 reduce-scatter.5.cloned.1.call-start
  224.6 10.3 %convolution_convert_fusion = bf16[4096,1024]{1,0:T(8,128)(2,1)} fusion(bf16[320,1024]{1,0:T(8,128)(2,1)S(1)} %reshape.28, f32[320,4096]{1,0:T(8,128)} %fusion.2), kind=kOutput, calls=%fused_computation.6 | convolution fusion | flops 2700345344 | bytes 14286848 | tf_op jit(solution)/shard_map/rf,rd->fd/dot_general | solution.py:70
  234.8 0.0 reduce-scatter.5.cloned.1.call-update
  234.9 7.8 %fusion.19 = bf16[320,1024]{1,0:T(8,128)(2,1)S(1)} fusion(bf16[320,4096]{1,0:T(8,128)(2,1)} %copy-done.2, bf16[1,1024,4096]{2,1,0:T(8,128)(2,1)} %all-gather.7.cloned.1.call-done), kind=kOutput, calls=%fused_computation.23 | convolution fusion | flops 2684682240 | bytes 11665408 | tf_op jit(solution)/shard_map/dot_general | solution.py:66
  242.7 0.3 reshape.31
  243.0 42.9 %all_to_all.15 = bf16[64,5,1024]{2,1,0:T(8,128)(2,1)S(1)} all-to-all(bf16[64,5,1024]{2,1,0:T(8,128)(2,1)S(1)} %reshape.31), channel_id=1, replica_groups=mesh['expert'=64,'replica'=4] {'expert'}, dimensions={0} | all-to-all | bytes 1310720 | tf_op jit(solution)/shard_map/all_to_all | solution.py:89
  285.9 0.3 reshape.32
  286.1 1.0 convolution_convert_fusion.4
  287.2 32.3 %reduce-scatter.3.cloned.1.call-done = bf16[1024,1024]{1,0:T(8,128)(2,1)} async-done(((bf16[4096,1024]{1,0:T(8,128)(2,1)}), bf16[1024,1024]{1,0:T(8,128)(2,1)}) %reduce-scatter.3.cloned.1.call-update) | async-done | bytes 2097168 | tf_op jit(solution)/shard_map/reduce_scatter | solution.py:78
  319.5 3.9 copy.18
  323.4 81.7 %reduce-scatter.5.cloned.1.call-done = bf16[1024,1024]{1,0:T(8,128)(2,1)} async-done(((bf16[4096,1024]{1,0:T(8,128)(2,1)}), bf16[1024,1024]{1,0:T(8,128)(2,1)}) %reduce-scatter.5.cloned.1.call-update) | async-done | bytes 2097168 | tf_op jit(solution)/shard_map/reduce_scatter | solution.py:69
Async XLA Ops:
  7.2 3.7 copy-start
  7.2 19.8 %copy-start.1 = (bf16[128,1024]{1,0:T(8,128)(2,1)S(1)}, bf16[128,1024]{1,0:T(8,128)(2,1)}, u32[]{:S(2)}) copy-start(bf16[128,1024]{1,0:T(8,128)(2,1)} %param.7) | copy-start | bytes 786436
  7.2 110.7 %all-gather.7.cloned.1.call-start = ((), (), s32[]{:S(2)}) async-start(), calls=%async_computation.8 | async-start | bytes 10485760 | tf_op jit(solution)/shard_map/all_gather | solution.py:62
  7.9 196.2 %all-gather.5.cloned.1.call-start = ((), (), s32[]{:S(2)}) async-start(), calls=%async_computation.7 | async-start | bytes 10485760 | tf_op jit(solution)/shard_map/all_gather | solution.py:63
  12.8 44.5 %all-to-all-start = ((bf16[64,5,1024]{2,1,0:T(8,128)(2,1)}), bf16[64,5,1024]{2,1,0:T(8,128)(2,1)S(1)}, u32[]{:S(2)}, u32[]{:S(2)}) async-start(bf16[64,5,1024]{2,1,0:T(8,128)(2,1)} %reshape.27), calls=%async_computation | async-start | bytes 2097152 | tf_op jit(solution)/shard_map/all_to_all | solution.py:49
  57.3 35.4 %all-to-all-start.1 = ((bf16[64,5,1024]{2,1,0:T(8,128)(2,1)}), bf16[64,5,1024]{2,1,0:T(8,128)(2,1)S(1)}, u32[]{:S(2)}, u32[]{:S(2)}) async-start(bf16[64,5,1024]{2,1,0:T(8,128)(2,1)} %reshape.29), calls=%async_computation.1 | async-start | bytes 2097152 | tf_op jit(solution)/shard_map/all_to_all | solution.py:42
  63.2 256.2 %reduce-scatter.3.cloned.1.call-start = ((), (), s32[]{:S(2)}) async-start(), calls=%async_computation.5 | async-start | bytes 10485760 | tf_op jit(solution)/shard_map/reduce_scatter | solution.py:78
  216.1 1.5 copy-start.2
  224.3 180.8 %reduce-scatter.5.cloned.1.call-start = ((), (), s32[]{:S(2)}) async-start(), calls=%async_computation.6 | async-start | bytes 10485760 | tf_op jit(solution)/shard_map/reduce_scatter | solution.py:69
Sparse Core Ops, SparseCore 0:
  9.8 107.9 all-gather.6
  119.7 84.4 all-gather.4
  224.5 94.9 reduce-scatter.2
  322.5 82.5 reduce-scatter.4
where the time goes:
time: 414 us; the launch traced here: 412 us
  waiting for transfers between devices  276 us (67%)
  matrix products  46.8 us (11%)
  blocking collectives  42.9 us (10%)
  starting transfers between devices  20.5 us (5%)
  between operations  13.9 us (3%)
  local copies, waits for them, and re-layouts  8.94 us (2%)
    reduce_scatter x1, waiting for transfers between devices, shards(): lax.psum_scatter(jnp.einsum('rf,rd->fd', active, expert_grads, preferred_...  81.7 us
    all_gather x1, waiting for transfers between devices, shards(): lax.all_gather(local_out, 'replica', axis=0, tiled=True)  78.3 us
    all_to_all x1, blocking collectives, shards(): lax.all_to_all(returned.reshape(expert_count, capacity, feature_width), '...  42.9 us
    reduce_scatter x1, waiting for transfers between devices, shards(): lax.psum_scatter(jnp.einsum('rf,rd->fd', grad_hidden, expert_rows, prefer...  32.3 us
    all_to_all x1, waiting for transfers between devices, shards(): lax.all_to_all(sent_tokens.reshape(expert_count, capacity, feature_width)...  29.1 us
    all_to_all x1, waiting for transfers between devices, shards(): lax.all_to_all(sent_grads.reshape(expert_count, capacity, feature_width),...  28.7 us
    all_gather x1, waiting for transfers between devices, shards(): lax.all_gather(local_in, 'replica', axis=1, tiled=True)  24.9 us
    all_to_all x1, starting transfers between devices, shards(): lax.all_to_all(sent_grads.reshape(expert_count, capacity, feature_width),...  14.2 us
  transfers between devices with their start and end apart: 6, of which 6 were waited for; matrix products, arithmetic and copies ran while one was open for 9% of the time, Pallas kernels for 0%

commit v1 on v0

v1 whole, which is shorter than its diff:
```python
import jax
import jax.numpy as jnp
from jax import lax
from jax.sharding import PartitionSpec as P

BF = jnp.bfloat16
F32 = jnp.float32
LANES = 128
TO_CORE = ((0, 1), (1, 0), (2, 3), (3, 2))
TO_CHIP = ((0, 2), (2, 0), (1, 3), (3, 1))


def smooth_gate(value):
    return jax.nn.gelu(value, approximate=True)


def dot(a, b, dims):
    return lax.dot_general(a, b, ((dims[0], dims[1]), ((), ())), preferred_element_type=F32)


def exchange(rows, experts):
    count, width = rows.shape
    blocks = rows.reshape(experts, count // experts * (width // LANES), LANES)
    moved = lax.all_to_all(blocks, "expert", split_axis=0, concat_axis=0, tiled=True)
    return moved.reshape(count, width)


def to_core(rows):
    return lax.ppermute(rows, "replica", TO_CORE)


def to_chip(rows):
    return lax.ppermute(rows, "replica", TO_CHIP)


def shards(tokens, upstream, expert_ids, slot_index, gate_weights, in_weight, out_weight):
    token_count, width = tokens.shape
    experts = lax.axis_size("expert")
    capacity = 5 * token_count // (2 * experts)
    columns = experts * capacity
    target = jnp.where(slot_index >= 0, expert_ids * capacity + slot_index, -1)
    column_ids = lax.broadcasted_iota(jnp.int32, (columns, 1), 0)
    first = column_ids == target[:, 0][None, :]
    second = column_ids == target[:, 1][None, :]
    place = (first | second).astype(BF)
    gates = jnp.where(first, gate_weights[:, 0][None, :], 0.0) + jnp.where(
        second, gate_weights[:, 1][None, :], 0.0
    )
    slot_gate = jnp.sum(gates, axis=1, keepdims=True)
    sent_tokens = dot(place, tokens, ((1,), (0,))).astype(BF)
    sent_grads = (slot_gate * dot(place, upstream, ((1,), (0,)))).astype(BF)
    if COMBINED:
        per = capacity * (width // LANES)
        both = jnp.concatenate([sent_tokens.reshape(experts, per, LANES), sent_grads.reshape(experts, per, LANES)], axis=1)
        both = lax.all_to_all(both, "expert", split_axis=0, concat_axis=0, tiled=True)
        x_own = both[:, :per].reshape(columns, width)
        g_own = both[:, per:].reshape(columns, width)
    else:
        x_own = exchange(sent_tokens, experts)
        g_own = exchange(sent_grads, experts)
    w_in = in_weight[0]
    w_out = out_weight[0]
    x_chip = to_chip(x_own)
    g_chip = to_chip(g_own)
    x_core = to_core(x_own)
    g_core = to_core(g_own)
    x_far = to_core(x_chip)
    g_far = to_core(g_chip)
    x_all = jnp.concatenate([x_own, x_core, x_chip, x_far], axis=0)
    g_all = jnp.concatenate([g_own, g_core, g_chip, g_far], axis=0)
    hidden = dot(x_all, w_in, ((1,), (0,)))
    active, pullback = jax.vjp(smooth_gate, hidden)
    carried = dot(g_all, w_out, ((1,), (1,)))
    grad_hidden = pullback(carried)[0].astype(BF)
    active = active.astype(BF)
    partial = dot(grad_hidden, w_in, ((1,), (1,)))
    n = columns
    away = jnp.concatenate([partial[n : 2 * n], partial[3 * n :]], axis=0).astype(BF)
    back = to_core(away)
    own = partial[:n] + back[:n].astype(F32)
    chip = (partial[2 * n : 3 * n] + back[n:].astype(F32)).astype(BF)
    returned = (own + to_chip(chip).astype(F32)).astype(BF)
    grad_out = dot(active, g_all, ((0,), (0,))).astype(BF)
    grad_in = dot(x_all, grad_hidden, ((0,), (0,))).astype(BF)
    arrived = exchange(returned, experts)
    token_grad = dot(place, arrived, ((0,), (0,))).astype(BF)
    return token_grad, grad_in[None], grad_out[None]


COMBINED = True


def solution(mesh):
    rows = P(("expert", "replica"), None)
    return jax.shard_map(
        shards,
        mesh=mesh,
        in_specs=(rows, rows, rows, rows, rows, P("expert", None, "replica"), P("expert", "replica", None)),
        out_specs=(rows, P("expert", None, "replica"), P("expert", "replica", None)),
        check_vma=False,
    )
```

time: 414 us -> 155 us (0.37)
  waiting for transfers between devices: 276 us -> 50.3 us
  matrix products: 46.8 us -> 30.5 us
  between operations: 13.9 us -> 0.91 us
  starting transfers between devices: 20.5 us -> 12.1 us
  blocking collectives: 42.9 us -> 49.8 us
    reduce_scatter x2 -> x0, waiting for transfers between devices: 114 us -> none  [the longest x1 81.7 us: shards(): lax.psum_scatter(jnp.einsum('rf,rd->fd', active, expert_grads, preferred_...]
    all_gather x2 -> x0, waiting for transfers between devices: 103 us -> none  [the longest x1 78.3 us: shards(): lax.all_gather(local_out, 'replica', axis=0, tiled=True)]
    all_to_all x2 -> x1, waiting for transfers between devices: 57.8 us -> 7.37 us  [exchange(): lax.all_to_all(blocks, 'expert', split_axis=0, concat_axis=0, tiled=True)]
    ppermute x0 -> x8, waiting for transfers between devices: none -> 42.9 us  [the longest x3 40.2 us: to_chip(): return lax.ppermute(rows, 'replica', TO_CHIP)]
    dot_general x8, matrix products: 46.8 us -> 30.5 us  [dot(): lax.dot_general(a, b, ((dims[0], dims[1]), ((), ())), preferred_element_t...]
    all_to_all x2 -> x1, starting transfers between devices: 20.2 us -> 8.13 us  [exchange(): lax.all_to_all(blocks, 'expert', split_axis=0, concat_axis=0, tiled=True)]
    all_to_all x1, blocking collectives: 42.9 us -> 49.8 us  [shards(): lax.all_to_all(both, 'expert', split_axis=0, concat_axis=0, tiled=True)]
  transfers between devices with their start and end apart: 6 -> 9, of which waited for: 6 -> 5; matrix products, arithmetic and copies ran while one was open for 9% -> 13% of each run, Pallas kernels for 0% -> 0%
where the time goes in v1:
time: 155 us
  waiting for transfers between devices  50.3 us (32%)
  blocking collectives  49.8 us (32%)
  matrix products  30.5 us (20%)
  starting transfers between devices  12.1 us (8%)
  local copies, waits for them, and re-layouts  9.61 us (6%)
  other arithmetic  1.74 us (1%)
    all_to_all x1, blocking collectives, shards(): lax.all_to_all(both, 'expert', split_axis=0, concat_axis=0, tiled=True)  49.8 us
    ppermute x3, waiting for transfers between devices, to_chip(): return lax.ppermute(rows, 'replica', TO_CHIP)  40.2 us
    dot_general x8, matrix products, dot(): lax.dot_general(a, b, ((dims[0], dims[1]), ((), ())), preferred_element_t...  30.5 us
    all_to_all x1, starting transfers between devices, exchange(): lax.all_to_all(blocks, 'expert', split_axis=0, concat_axis=0, tiled=True)  8.13 us
    all_to_all x1, waiting for transfers between devices, exchange(): lax.all_to_all(blocks, 'expert', split_axis=0, concat_axis=0, tiled=True)  7.37 us
    unnamed x20, local copies, waits for them, and re-layouts  4.1 us
  transfers between devices with their start and end apart: 9, of which 5 were waited for; matrix products, arithmetic and copies ran while one was open for 13% of the time, Pallas kernels for 0%

profile of v1, /device:TPU:32, one launch (start us, length us, event | category | flops | bytes accessed | tf_op | source)
XLA Modules:
  0.0 154.9 jit_solution(13305817476534678274)
XLA Ops:
  0.6 0.0 copy-start
  0.6 0.8 compare_select_fusion
  1.5 0.8 slice_bitcast_fusion.1
  2.3 0.1 add_reduce_fusion
  2.4 1.3 fusion.20
  3.7 0.3 reshape.30
  4.0 2.1 %convolution_convert_fusion = bf16[320,1024]{1,0:T(8,128)(2,1)} fusion(bf16[128,1024]{1,0:T(8,128)(2,1)} %param.7, s32[128]{0:T(128)S(1)} %get-tuple-element.8, s32[128]{0:T(128)S(1)} %get-tuple-element.7), kind=kOutput, calls=%fused_computation.24 | convolution fusion | flops 84336640 | bytes 918528 | tf_op jit(solution)/shard_map/dot_general | solution.py:18
  6.1 1.4 reshape.29
  7.5 0.1 pad_maximum_fusion
  7.6 49.8 %all_to_all.10 = bf16[64,80,128]{2,1,0:T(8,128)(2,1)S(1)} all-to-all(bf16[64,80,128]{2,1,0:T(8,128)(2,1)S(1)} %pad_maximum_fusion), channel_id=1, replica_groups=mesh['expert'=64,'replica'=4] {'expert'}, dimensions={0} | all-to-all | bytes 2621440 | tf_op jit(solution)/shard_map/all_to_all | solution.py:55
  57.4 0.1 fusion.39
  57.5 1.1 reshape.32
  58.6 0.7 collective-permute-start.4
  59.3 0.3 reshape.31
  59.6 1.4 collective-permute-start.1
  61.0 0.0 collective-permute-start.3
  61.0 0.5 collective-permute-start
  61.5 15.1 %collective-permute-done.4 = bf16[320,1024]{1,0:T(8,128)(2,1)} collective-permute-done((bf16[320,1024]{1,0:T(8,128)(2,1)}, bf16[320,1024]{1,0:T(8,128)(2,1)}, u32[]{:S(2)}, u32[]{:S(2)}) %collective-permute-start.4) | collective-permute-done | bytes 655392 | tf_op jit(solution)/shard_map/ppermute | solution.py:33
  76.6 0.0 collective-permute-start.5
  76.6 1.1 constant_dynamic-update-slice_fusion.7
  77.8 8.8 %collective-permute-done.1 = bf16[320,1024]{1,0:T(8,128)(2,1)S(1)} collective-permute-done((bf16[320,1024]{1,0:T(8,128)(2,1)S(1)}, bf16[320,1024]{1,0:T(8,128)(2,1)S(1)}, u32[]{:S(2)}, u32[]{:S(2)}) %collective-permute-start.1) | collective-permute-done | bytes 655392 | tf_op jit(solution)/shard_map/ppermute | solution.py:33
  86.6 0.0 collective-permute-start.2
  86.6 0.0 collective-permute-done.3
  86.7 1.1 constant_dynamic-update-slice_fusion.5
  87.8 0.0 collective-permute-done
  87.9 0.0 collective-permute-done.5
  88.0 0.0 copy-done
  88.0 0.0 copy-start.3
  88.0 0.0 copy-start.4
  88.0 2.9 %fusion.14 = f32[1280,1024]{1,0:T(8,128)S(1)} fusion(bf16[1280,1024]{1,0:T(8,128)(2,1)S(1)} %constant_dynamic-update-slice_fusion.4, bf16[1,1024,1024]{2,1,0:T(8,128)(2,1)S(1)} %copy-done), kind=kOutput, calls=%fused_computation.17 | convolution fusion | flops 2684354560 | bytes 9961472 | tf_op jit(solution)/shard_map/dot_general | solution.py:18
  90.9 0.0 copy-done.3
  90.9 0.0 copy-start.6
  91.0 0.0 collective-permute-done.2
  91.0 0.0 copy-start.1
  91.0 1.6 %copy-done.1 = bf16[1280,1024]{1,0:T(8,128)(2,1)} copy-done((bf16[1280,1024]{1,0:T(8,128)(2,1)}, bf16[1280,1024]{1,0:T(8,128)(2,1)S(1)}, u32[]{:S(2)}) %copy-start.1) | copy-done | bytes 2621464
  92.7 0.0 copy-done.4
  92.7 6.0 %fusion.6 = bf16[1280,1024]{1,0:T(8,128)(2,1)S(1)} fusion(f32[1280,1024]{1,0:T(8,128)S(1)} %fusion.14, bf16[1280,1024]{1,0:T(8,128)(2,1)S(1)} %constant_dynamic-update-slice_fusion, bf16[1,1024,1024]{2,1,0:T(8,128)(2,1)S(1)} %copy-done.4), kind=kOutput, calls=%fused_computation.8 | convolution fusion | flops 2710568960 | bytes 12582912 | tf_op jit(solution)/shard_map/dot_general | solution.py:18
  98.7 0.0 copy-done.6
  98.7 0.0 copy-start.5
  98.7 2.9 %fusion.40 = (bf16[1280,1024]{1,0:T(8,128)(2,1)S(1)}, f32[1280,1024]{1,0:T(8,128)S(1)}) fusion(bf16[1280,1024]{1,0:T(8,128)(2,1)S(1)} %fusion.6, bf16[1,1024,1024]{2,1,0:T(8,128)(2,1)S(1)} %copy-done), kind=kOutput, calls=%fused_computation.63 | convolution fusion | flops 2685665280 | bytes 12582912 | tf_op jit(solution)/shard_map/dot_general | solution.py:18
  101.6 0.0 copy-done.5
  101.6 0.1 fusion.38
  101.7 0.1 pad_maximum_fusion.1
  101.8 0.6 collective-permute-start.6
  102.4 2.7 %collective-permute-done.6 = bf16[640,1024]{1,0:T(8,128)(2,1)S(1)} collective-permute-done((bf16[640,1024]{1,0:T(8,128)(2,1)S(1)}, bf16[640,1024]{1,0:T(8,128)(2,1)S(1)}, u32[]{:S(2)}, u32[]{:S(2)}) %collective-permute-start.6) | collective-permute-done | bytes 1310752 | tf_op jit(solution)/shard_map/ppermute | solution.py:29
  105.1 0.2 fusion.21
  105.3 0.8 collective-permute-start.7
  106.1 16.3 %collective-permute-done.7 = bf16[320,1024]{1,0:T(8,128)(2,1)S(1)} collective-permute-done((bf16[320,1024]{1,0:T(8,128)(2,1)S(1)}, bf16[320,1024]{1,0:T(8,128)(2,1)S(1)}, u32[]{:S(2)}, u32[]{:S(2)}) %collective-permute-start.7) | collective-permute-done | bytes 655392 | tf_op jit(solution)/shard_map/ppermute | solution.py:33
  122.4 0.3 fusion.23
  122.7 1.1 reshape.33
  123.9 8.1 %all-to-all-start.1 = ((bf16[64,40,128]{2,1,0:T(8,128)(2,1)}), bf16[64,40,128]{2,1,0:T(8,128)(2,1)S(1)}, u32[]{:S(2)}, u32[]{:S(2)}) async-start(bf16[64,40,128]{2,1,0:T(8,128)(2,1)} %reshape.33), calls=%async_computation.1 | async-start | bytes 1310720 | tf_op jit(solution)/shard_map/all_to_all | solution.py:24
  132.0 0.0 copy-start.2
  132.0 6.9 %convert_bitcast_fusion.1 = bf16[1,1024,1024]{2,1,0:T(8,128)(2,1)} fusion(bf16[1280,1024]{1,0:T(8,128)(2,1)} %copy-done.3, bf16[1280,1024]{1,0:T(8,128)(2,1)} %copy-done.5), kind=kOutput, calls=%fused_computation.22 | convolution fusion | flops 2685403136 | bytes 7340032 | tf_op jit(solution)/shard_map/dot_general | solution.py:18
  139.0 0.0 copy-done.2
  139.0 7.3 %convert_bitcast_fusion = bf16[1,1024,1024]{2,1,0:T(8,128)(2,1)} fusion(bf16[1280,1024]{1,0:T(8,128)(2,1)S(1)} %copy-done.2, f32[1280,1024]{1,0:T(8,128)} %copy-done.6), kind=kOutput, calls=%fused_computation.21 | convolution fusion | flops 2697199616 | bytes 9961472 | tf_op jit(solution)/shard_map/dot_general | solution.py:18
  146.2 7.4 %all-to-all-done.1 = bf16[64,40,128]{2,1,0:T(8,128)(2,1)S(1)} async-done(((bf16[64,40,128]{2,1,0:T(8,128)(2,1)}), bf16[64,40,128]{2,1,0:T(8,128)(2,1)S(1)}, u32[]{:S(2)}, u32[]{:S(2)}) %all-to-all-start.1) | async-done | bytes 655392 | tf_op jit(solution)/shard_map/all_to_all | solution.py:24
  153.6 0.3 reshape.34
  153.9 1.1 convolution_convert_fusion.1
  (7 shorter events, 0.3 us)
Async XLA Ops:
  0.6 87.4 %copy-start = (bf16[1,1024,1024]{2,1,0:T(8,128)(2,1)S(1)}, bf16[1,1024,1024]{2,1,0:T(8,128)(2,1)}, u32[]{:S(2)}) copy-start(bf16[1,1024,1024]{2,1,0:T(8,128)(2,1)} %param.12) | copy-start | bytes 6291460
  58.6 18.0 %collective-permute-start.4 = (bf16[320,1024]{1,0:T(8,128)(2,1)}, bf16[320,1024]{1,0:T(8,128)(2,1)}, u32[]{:S(2)}, u32[]{:S(2)}) collective-permute-start(bf16[320,1024]{1,0:T(8,128)(2,1)} %reshape.32), channel_id=1, source_target_pairs={{0,2},{2,0},{1,3},{3,1},{4,6},{6,4},{5,7},{7,5},{8,10},{10,8},{9,1... | collective-permute-start | bytes 1966088 | tf_op jit(solution)/shard_map/ppermute | solution.py:33
  59.6 27.1 %collective-permute-start.1 = (bf16[320,1024]{1,0:T(8,128)(2,1)S(1)}, bf16[320,1024]{1,0:T(8,128)(2,1)S(1)}, u32[]{:S(2)}, u32[]{:S(2)}) collective-permute-start(bf16[320,1024]{1,0:T(8,128)(2,1)S(1)} %reshape.31), channel_id=1, source_target_pairs={{0,2},{2,0},{1,3},{3,1},{4,6},{6,4},{5,7},{7,5},{8,10},{10,8},{9,1... | collective-permute-start | bytes 1966088 | tf_op jit(solution)/shard_map/ppermute | solution.py:33
  61.0 25.6 %collective-permute-start.3 = (bf16[320,1024]{1,0:T(8,128)(2,1)}, bf16[320,1024]{1,0:T(8,128)(2,1)S(1)}, u32[]{:S(2)}, u32[]{:S(2)}) collective-permute-start(bf16[320,1024]{1,0:T(8,128)(2,1)} %reshape.32), channel_id=1, source_target_pairs={{0,1},{1,0},{2,3},{3,2},{4,5},{5,4},{6,7},{7,6},{8,9},{9,8},{10,11... | collective-permute-start | bytes 1966088 | tf_op jit(solution)/shard_map/ppermute | solution.py:29
  61.0 26.8 %collective-permute-start = (bf16[320,1024]{1,0:T(8,128)(2,1)S(1)}, bf16[320,1024]{1,0:T(8,128)(2,1)S(1)}, u32[]{:S(2)}, u32[]{:S(2)}) collective-permute-start(bf16[320,1024]{1,0:T(8,128)(2,1)S(1)} %reshape.31), channel_id=1, source_target_pairs={{0,1},{1,0},{2,3},{3,2},{4,5},{5,4},{6,7},{7,6},{8,9},{9,8},{10,11... | collective-permute-start | bytes 1966088 | tf_op jit(solution)/shard_map/ppermute | solution.py:29
  76.6 11.3 %collective-permute-start.5 = (bf16[320,1024]{1,0:T(8,128)(2,1)}, bf16[320,1024]{1,0:T(8,128)(2,1)S(1)}, u32[]{:S(2)}, u32[]{:S(2)}) collective-permute-start(bf16[320,1024]{1,0:T(8,128)(2,1)} %collective-permute-done.4), channel_id=1, source_target_pairs={{0,1},{1,0},{2,3},{3,2},{4,5},{5,4},{6,7},{7,6},{8,9},{9,8},{10,11... | collective-permute-start | bytes 1966088 | tf_op jit(solution)/shard_map/ppermute | solution.py:29
  86.6 4.3 %collective-permute-start.2 = (bf16[320,1024]{1,0:T(8,128)(2,1)S(1)}, bf16[320,1024]{1,0:T(8,128)(2,1)S(1)}, u32[]{:S(2)}, u32[]{:S(2)}) collective-permute-start(bf16[320,1024]{1,0:T(8,128)(2,1)S(1)} %collective-permute-done.1), channel_id=1, source_target_pairs={{0,1},{1,0},{2,3},{3,2},{4,5},{5,4},{6,7},{7,6},{8,9},{9,8},{10,11... | collective-permute-start | bytes 1966088 | tf_op jit(solution)/shard_map/ppermute | solution.py:29
  88.0 2.9 %copy-start.3 = (bf16[1280,1024]{1,0:T(8,128)(2,1)}, bf16[1280,1024]{1,0:T(8,128)(2,1)S(1)}, u32[]{:S(2)}) copy-start(bf16[1280,1024]{1,0:T(8,128)(2,1)S(1)} %constant_dynamic-update-slice_fusion.4) | copy-start | bytes 7864324
  88.0 4.6 %copy-start.4 = (bf16[1,1024,1024]{2,1,0:T(8,128)(2,1)S(1)}, bf16[1,1024,1024]{2,1,0:T(8,128)(2,1)}, u32[]{:S(2)}) copy-start(bf16[1,1024,1024]{2,1,0:T(8,128)(2,1)} %param.13) | copy-start | bytes 6291460
  90.9 7.7 %copy-start.6 = (f32[1280,1024]{1,0:T(8,128)}, f32[1280,1024]{1,0:T(8,128)S(1)}, u32[]{:S(2)}) copy-start(f32[1280,1024]{1,0:T(8,128)S(1)} %fusion.14) | copy-start | bytes 15728644
  91.0 1.6 %copy-start.1 = (bf16[1280,1024]{1,0:T(8,128)(2,1)}, bf16[1280,1024]{1,0:T(8,128)(2,1)S(1)}, u32[]{:S(2)}) copy-start(bf16[1280,1024]{1,0:T(8,128)(2,1)S(1)} %constant_dynamic-update-slice_fusion) | copy-start | bytes 7864324
  98.7 2.9 %copy-start.5 = (bf16[1280,1024]{1,0:T(8,128)(2,1)}, bf16[1280,1024]{1,0:T(8,128)(2,1)S(1)}, u32[]{:S(2)}) copy-start(bf16[1280,1024]{1,0:T(8,128)(2,1)S(1)} %fusion.6) | copy-start | bytes 7864324
  101.8 3.2 %collective-permute-start.6 = (bf16[640,1024]{1,0:T(8,128)(2,1)S(1)}, bf16[640,1024]{1,0:T(8,128)(2,1)S(1)}, u32[]{:S(2)}, u32[]{:S(2)}) collective-permute-start(bf16[640,1024]{1,0:T(8,128)(2,1)S(1)} %pad_maximum_fusion.1), channel_id=1, source_target_pairs={{0,1},{1,0},{2,3},{3,2},{4,5},{5,4},{6,7},{7,6},{8,9},{9,8},{10,11... | collective-permute-start | bytes 3932168 | tf_op jit(solution)/shard_map/ppermute | solution.py:29
  105.3 17.1 %collective-permute-start.7 = (bf16[320,1024]{1,0:T(8,128)(2,1)S(1)}, bf16[320,1024]{1,0:T(8,128)(2,1)S(1)}, u32[]{:S(2)}, u32[]{:S(2)}) collective-permute-start(bf16[320,1024]{1,0:T(8,128)(2,1)S(1)} %fusion.21), channel_id=1, source_target_pairs={{0,2},{2,0},{1,3},{3,1},{4,6},{6,4},{5,7},{7,5},{8,10},{10,8},{9,1... | collective-permute-start | bytes 1966088 | tf_op jit(solution)/shard_map/ppermute | solution.py:33
  123.9 29.7 %all-to-all-start.1 = ((bf16[64,40,128]{2,1,0:T(8,128)(2,1)}), bf16[64,40,128]{2,1,0:T(8,128)(2,1)S(1)}, u32[]{:S(2)}, u32[]{:S(2)}) async-start(bf16[64,40,128]{2,1,0:T(8,128)(2,1)} %reshape.33), calls=%async_computation.1 | async-start | bytes 1310720 | tf_op jit(solution)/shard_map/all_to_all | solution.py:24
  132.0 6.9 %copy-start.2 = (bf16[1280,1024]{1,0:T(8,128)(2,1)S(1)}, bf16[1280,1024]{1,0:T(8,128)(2,1)}, u32[]{:S(2)}) copy-start(bf16[1280,1024]{1,0:T(8,128)(2,1)} %copy-done.1) | copy-start | bytes 7864324

commit v2 on v1

v2 whole, which is shorter than its diff:
```python
import functools

import jax
import jax.numpy as jnp
from jax import lax
from jax.experimental import pallas as pl
from jax.experimental.pallas import tpu as pltpu
from jax.sharding import PartitionSpec as P

BF = jnp.bfloat16
F32 = jnp.float32
LANES = 128
SCALE = 0.7978845608
CUBE = 0.044715
TO_CORE = ((0, 1), (1, 0), (2, 3), (3, 2))
TO_CHIP = ((0, 2), (2, 0), (1, 3), (3, 1))
SPLIT = (32, 32)
SMALL = 16 * 2**20
LARGE = 56 * 2**20


def dot(a, b, dims):
    return lax.dot_general(a, b, ((dims[0], dims[1]), ((), ())), preferred_element_type=F32)


def kernel_call(body, out_shape, limit, flops, size, **kw):
    return pl.pallas_call(
        body,
        out_shape=out_shape,
        compiler_params=pltpu.CompilerParams(vmem_limit_bytes=limit),
        cost_estimate=pl.CostEstimate(flops=flops, bytes_accessed=size, transcendentals=0),
        **kw,
    )


def shape(rows, width, dtype=BF):
    return jax.ShapeDtypeStruct((rows, width), dtype)


def to_core(rows):
    return lax.ppermute(rows, "replica", TO_CORE)


def to_chip(rows):
    return lax.ppermute(rows, "replica", TO_CHIP)


def places(ids, slots, capacity, columns):
    target = jnp.where(slots >= 0, ids * capacity + slots, -1)
    column_ids = lax.broadcasted_iota(jnp.int32, (columns, target.shape[1]), 0)
    return column_ids == target[0:1, :], column_ids == target[1:2, :]


def pack(rows, experts):
    count, width = rows.shape
    return rows.reshape(count, width // LANES, LANES).reshape(experts, -1, LANES)


def dispatch_kernel(experts, capacity, tokens, upstream, ids, slots, gates, sent):
    columns = experts * capacity
    first, second = places(ids[...], slots[...], capacity, columns)
    place = jnp.where(first | second, 1.0, 0.0).astype(BF)
    gate = jnp.where(first, gates[0:1, :], 0.0) + jnp.where(second, gates[1:2, :], 0.0)
    slot_gate = jnp.sum(gate, axis=1, keepdims=True)
    rows = dot(place, tokens[...], ((1,), (0,)))
    grads = slot_gate * dot(place, upstream[...], ((1,), (0,)))
    both = jnp.concatenate([pack(rows, experts), pack(grads, experts)], axis=1)
    sent[...] = both.reshape(-1, LANES).astype(BF)


def unpack_kernel(senders, got, own):
    blocks = got[...].astype(F32).reshape(senders, -1, LANES)
    per = blocks.shape[1] // 2
    n = own.shape[0] // 2
    own[pl.ds(0, n), :] = blocks[:, :per].reshape(n, -1).astype(BF)
    own[pl.ds(n, n), :] = blocks[:, per:].reshape(n, -1).astype(BF)


def expert_kernel(sizes, *refs):
    blocks, refs = refs[: len(sizes)], refs[len(sizes) :]
    w_in, w_out, active, grad_hidden, away, near = refs
    split = away.shape[0]
    x = jnp.concatenate([block[pl.ds(0, n), :] for n, block in zip(sizes, blocks)], axis=0)
    g = jnp.concatenate([block[pl.ds(n, n), :] for n, block in zip(sizes, blocks)], axis=0)
    hidden = dot(x, w_in[...], ((1,), (0,)))
    carried = dot(g, w_out[...], ((1,), (1,)))
    square = hidden * hidden
    bend = jnp.tanh(hidden * (SCALE + SCALE * CUBE * square))
    lift = 0.5 * (1.0 + bend)
    active[...] = (hidden * lift).astype(BF)
    slope = lift + hidden * (1.0 - bend * bend) * (0.5 * SCALE + 1.5 * SCALE * CUBE * square)
    back = (slope * carried).astype(BF)
    grad_hidden[...] = back
    part = dot(back, w_in[...], ((1,), (1,)))
    away[...] = part[:split].astype(BF)
    near[...] = part[split:]


def expert_step(blocks, w_in, w_out):
    width, units = w_in.shape
    sizes = [block.shape[0] // 2 for block in blocks]
    rows = sum(sizes)
    return kernel_call(
        functools.partial(expert_kernel, sizes),
        [shape(rows, units), shape(rows, units), shape(rows // 2, width), shape(rows // 2, width, F32)],
        LARGE,
        6 * rows * width * units,
        4 * width * units + 14 * rows * width,
    )(*blocks, w_in, w_out)


def weight_grads_kernel(sizes, runs, *refs):
    blocks, refs = refs[: len(sizes)], refs[len(sizes) :]
    count = len(runs)
    actives, refs = refs[:count], refs[count:]
    grad_hiddens, (grad_in, grad_out) = refs[:count], refs[count:]
    out_sum = in_sum = None
    at = 0
    for active, grad_hidden, run in zip(actives, grad_hiddens, runs):
        sides = list(zip(sizes[at : at + run], blocks[at : at + run]))
        at += run
        x = jnp.concatenate([block[pl.ds(0, n), :] for n, block in sides], axis=0)
        g = jnp.concatenate([block[pl.ds(n, n), :] for n, block in sides], axis=0)
        out_part = dot(active[...], g, ((0,), (0,)))
        in_part = dot(grad_hidden[...], x, ((0,), (0,)))
        out_sum = out_part if out_sum is None else out_sum + out_part
        in_sum = in_part if in_sum is None else in_sum + in_part
    grad_out[...] = out_sum.astype(BF)
    grad_in[...] = in_sum.T.astype(BF)


def weight_grads(made, width, units):
    tile = 256
    blocks = [block for group, _, _ in made for block in group]
    sizes = [block.shape[0] // 2 for block in blocks]
    runs = [len(group) for group, _, _ in made]
    rows = [active.shape[0] for _, active, _ in made]
    columns = [pl.BlockSpec((n, tile), lambda j: (0, j)) for n in rows]
    return kernel_call(
        functools.partial(weight_grads_kernel, sizes, runs),
        [shape(width, units), shape(units, width)],
        LARGE,
        4 * sum(rows) * width * units,
        4 * width * units + 8 * sum(rows) * width,
        grid=(units // tile,),
        in_specs=[pl.BlockSpec((2 * n, width), lambda j: (0, 0)) for n in sizes] + columns + columns,
        out_specs=[pl.BlockSpec((width, tile), lambda j: (0, j)), pl.BlockSpec((tile, width), lambda j: (j, 0))],
    )(*blocks, *[m[1] for m in made], *[m[2] for m in made])


def return_kernel(capacity, near, back, *refs):
    chips, out = refs[:-1], refs[-1]
    start = 0
    packed = []
    for chip in chips:
        n = chip.shape[0]
        at = pl.ds(start, n)
        rows = near[at, :] + back[at, :].astype(F32) + chip[...].astype(F32)
        packed.append(pack(rows, n // capacity).reshape(-1, LANES))
        start += n
    out[...] = jnp.concatenate(packed, axis=0).astype(BF)


def exchange(blocks, experts):
    moved = lax.all_to_all(blocks.reshape(experts, -1, LANES), "expert", split_axis=0, concat_axis=0, tiled=True)
    return moved.reshape(-1, LANES)


def reduce_core(away, near):
    return to_chip((near + to_core(away).astype(F32)).astype(BF))


def shards(tokens, upstream, expert_ids, slot_index, gate_weights, in_weight, out_weight):
    token_count, width = tokens.shape
    experts = lax.axis_size("expert")
    capacity = 5 * token_count // (2 * experts)
    columns = experts * capacity
    per = width // LANES * capacity * 2
    ids, slots, gates = expert_ids.T, slot_index.T, gate_weights.T
    sent = kernel_call(
        functools.partial(dispatch_kernel, experts, capacity), shape(experts * per, LANES), LARGE, 1, 1
    )(tokens, upstream, ids, slots, gates)
    got = exchange(sent, experts)
    w_in = in_weight[0]
    w_out = out_weight[0]
    owns = []
    start = 0
    for senders in SPLIT:
        at = start // senders
        owns.append(
            kernel_call(
                functools.partial(unpack_kernel, senders),
                shape(2 * senders * capacity, width),
                SMALL,
                10**6,
                10**6,
                grid=(1,),
                in_specs=[pl.BlockSpec((senders * per, LANES), lambda j, at=at: (at, 0))],
                out_specs=pl.BlockSpec((2 * senders * capacity, width), lambda j: (0, 0)),
            )(got)
        )
        start += senders
    barrier = lax.optimization_barrier
    cores = [to_core(own) for own in owns]
    blocks = cores + owns
    active, grad_hidden, away_own, near_own = expert_step(blocks, w_in, w_out)
    back_own = to_core(away_own)
    made = [(blocks, active, grad_hidden)]
    chips = [to_chip(owns[0])]
    sums = []
    for i in range(len(owns)):
        chip = chips[i]
        if i + 1 < len(owns):
            own, chip = barrier((owns[i + 1], chip))
            chips.append(to_chip(own))
        if i:
            chip, away, back_own = barrier((chip, away, back_own))
            sums.append(reduce_core(away, near))
        far = to_core(chip)
        active, grad_hidden, away, near = expert_step([far, chip], w_in, w_out)
        made.append(([far, chip], active, grad_hidden))
    away, sums[-1] = barrier((away, sums[-1]))
    sums.append(reduce_core(away, near))
    returned = kernel_call(
        functools.partial(return_kernel, capacity), shape(columns * width // LANES, LANES), SMALL, 10**6, 10**6
    )(near_own, back_own, *sums)
    arrived = exchange(returned, experts).reshape(columns, width)
    grad_in, grad_out = weight_grads(made, *w_in.shape)
    first, second = places(ids, slots, capacity, columns)
    place = (first | second).astype(BF)
    token_grad = dot(place, arrived, ((0,), (0,))).astype(BF)
    return token_grad, grad_in[None], grad_out[None]


def solution(mesh):
    rows = P(("expert", "replica"), None)
    return jax.shard_map(
        shards,
        mesh=mesh,
        in_specs=(rows, rows, rows, rows, rows, P("expert", None, "replica"), P("expert", "replica", None)),
        out_specs=(rows, P("expert", None, "replica"), P("expert", "replica", None)),
        check_vma=False,
    )
```

time: 155 us -> 144 us (0.929)
  Pallas kernels: 0 us -> 37.4 us
  matrix products: 30.5 us -> 1.05 us
  waiting for transfers between devices: 50.3 us -> 35.3 us
  local copies, waits for them, and re-layouts: 9.61 us -> 3.09 us
  starting transfers between devices: 12.1 us -> 13.9 us
    pallas_call x0 -> x8, Pallas kernels: none -> 37.4 us  [the longest x3 20.1 us: expert_step(): kernel_call(functools.partial(expert_kernel, sizes), [shape(rows, units),...]
    dot_general x8 -> x1, matrix products: 30.5 us -> 1.05 us  [dot(): lax.dot_general(a, b, ((dims[0], dims[1]), ((), ())), preferred_element_t...]
    ppermute x3 -> x4, waiting for transfers between devices: 40.2 us -> 23.5 us  [to_chip(): return lax.ppermute(rows, 'replica', TO_CHIP)]
    reshape x6 -> x0, local copies, waits for them, and re-layouts: 4.45 us -> none  [the longest x1 1.37 us: shards(): sent_tokens.reshape(experts, per, LANES)]
    convert_element_type x2, other arithmetic: 0.54 us -> 2.32 us  [reduce_core(): return to_chip((near + to_core(away).astype(F32)).astype(BF))]
    ppermute x3 -> x4, starting transfers between devices: 2.9 us -> 4.31 us  [to_chip(): return lax.ppermute(rows, 'replica', TO_CHIP)]
    unnamed x20 -> x22, local copies, waits for them, and re-layouts: 4.1 us -> 2.81 us
    ppermute x5 -> x7, waiting for transfers between devices: 2.67 us -> 3.18 us  [to_core(): return lax.ppermute(rows, 'replica', TO_CORE)]
  transfers between devices with their start and end apart: 9 -> 12, of which waited for: 5 -> 6; matrix products, arithmetic and copies ran while one was open for 13% -> 1% of each run, Pallas kernels for 0% -> 23%
where the time goes in v2:
time: 144 us
  blocking collectives  50 us (35%)
  Pallas kernels  37.4 us (26%)
  waiting for transfers between devices  35.3 us (25%)
  starting transfers between devices  13.9 us (10%)
  local copies, waits for them, and re-layouts  3.09 us (2%)
  other arithmetic  2.32 us (2%)
    all_to_all x1, blocking collectives, exchange(): lax.all_to_all(blocks.reshape(experts, -1, LANES), 'expert', split_axis=0...  50 us
    ppermute x4, waiting for transfers between devices, to_chip(): return lax.ppermute(rows, 'replica', TO_CHIP)  23.5 us
    pallas_call x3, Pallas kernels, expert_step(): kernel_call(functools.partial(expert_kernel, sizes), [shape(rows, units),...  20.1 us
    pallas_call x1, Pallas kernels, weight_grads(): kernel_call(functools.partial(weight_grads_kernel, sizes, runs), [shape(w...  12.7 us
    all_to_all x1, waiting for transfers between devices, exchange(): lax.all_to_all(blocks.reshape(experts, -1, LANES), 'expert', split_axis=0...  8.65 us
    all_to_all x1, starting transfers between devices, exchange(): lax.all_to_all(blocks.reshape(experts, -1, LANES), 'expert', split_axis=0...  7.73 us
    ppermute x4, starting transfers between devices, to_chip(): return lax.ppermute(rows, 'replica', TO_CHIP)  4.31 us
    ppermute x7, waiting for transfers between devices, to_core(): return lax.ppermute(rows, 'replica', TO_CORE)  3.18 us
  transfers between devices with their start and end apart: 12, of which 6 were waited for; matrix products, arithmetic and copies ran while one was open for 1% of the time, Pallas kernels for 23%

profile of v2, /device:TPU:32, one launch (start us, length us, event | category | flops | bytes accessed | tf_op | source)
XLA Modules:
  0.0 143.9 jit_solution(1071968142506122198)
XLA Ops:
  0.6 2.9 %shard_map.94 = bf16[5120,128]{1,0:T(8,128)(2,1)} custom-call(bf16[128,1024]{1,0:T(8,128)(2,1)} %tokens.1, bf16[128,1024]{1,0:T(8,128)(2,1)} %upstream.1, s32[2,128]{1,0:T(2,128)} %bitcast.20, s32[2,128]{1,0:T(2,128)} %bitcast.21, f32[2,128]{1,0:T(2,128)} %bitcast.22), custom_call_target="tpu_custom_call" | custom-call | flops 1 | bytes 1 | tf_op jit(solution)/shard_map/pallas_call | solution.py:180
  3.5 50.0 %all_to_all.10 = bf16[64,80,128]{2,1,0:T(8,128)(2,1)S(1)} all-to-all(bf16[64,80,128]{2,1,0:T(8,128)(2,1)} %bitcast.19), channel_id=1, replica_groups=mesh['expert'=64,'replica'=4] {'expert'}, dimensions={0} | all-to-all | bytes 2621440 | tf_op jit(solution)/shard_map/all_to_all | solution.py:165
  53.5 0.3 shard_map.95.refs_2_
  53.8 0.0 copy-start.1
  53.8 0.8 collective-permute-start.2
  54.5 0.0 collective-permute-start
  54.5 0.3 shard_map.96.refs_3_
  54.8 0.0 copy-start.2
  54.8 0.6 collective-permute-start.1
  55.4 13.3 %collective-permute-done.2.refs_1_.refs_5_ = bf16[320,1024]{1,0:T(8,128)(2,1)S(1)} collective-permute-done((bf16[320,1024]{1,0:T(8,128)(2,1)S(1)}, bf16[320,1024]{1,0:T(8,128)(2,1)S(1)}, u32[]{:S(2)}, u32[]{:S(2)}) %collective-permute-start.2) | collective-permute-done | bytes 655392 | tf_op jit(solution)/shard_map/ppermute | solution.py:45
  68.8 0.0 copy-start.5
  68.8 0.7 collective-permute-start.3
  69.4 0.0 collective-permute-start.4
  69.4 0.0 collective-permute-done.refs_0_
  69.4 0.0 copy-start.6
  69.4 0.0 collective-permute-done.1.refs_1_
  69.5 0.0 copy-start.7
  69.5 0.0 copy-done.1
  69.5 0.0 copy-done.2
  69.5 0.8 copy-done.6
  70.3 0.2 copy-done.7
  70.5 8.5 %shard_map.97 = (bf16[640,1024]{1,0:T(8,128)(2,1)}, bf16[640,1024]{1,0:T(8,128)(2,1)}, bf16[320,1024]{1,0:T(8,128)(2,1)}, f32[320,1024]{1,0:T(8,128)}) custom-call(bf16[320,1024]{1,0:T(8,128)(2,1)} %copy-done.6, bf16[320,1024]{1,0:T(8,128)(2,1)} %copy-done.7, bf16[320,1024]{1,0:T(8,128)(2,1)} %copy-done.1, bf16[320,1024]{1,0:T(8,128)(2,1)} %copy-done.2, ...), custom_call_target="tpu_custom_call" | custom-call | flops 4026531840 | bytes 13369344 | tf_op jit(solution)/shard_map/pallas_call | solution.py:103
  79.0 0.0 copy-done.5
  79.0 0.5 collective-permute-start.5
  79.5 0.0 collective-permute-done.4.refs_0_.refs_4_
  79.5 0.0 copy-start.9
  79.5 0.9 copy-done.9
  80.4 5.8 %shard_map.98 = (bf16[320,1024]{1,0:T(8,128)(2,1)}, bf16[320,1024]{1,0:T(8,128)(2,1)}, bf16[160,1024]{1,0:T(8,128)(2,1)}, f32[160,1024]{1,0:T(8,128)}) custom-call(bf16[320,1024]{1,0:T(8,128)(2,1)} %copy-done.9, bf16[320,1024]{1,0:T(8,128)(2,1)} %copy-done.5, bf16[1024,1024]{1,0:T(8,128)(2,1)} %bitcast.24, bf16[1024,1024]{1,0:T(8,128)(2,1)} %bitcast.27), custom_call_target="tpu_custom_call" | custom-call | flops 2013265920 | bytes 8781824 | tf_op jit(solution)/shard_map/pallas_call | solution.py:103
  86.2 0.0 collective-permute-done.3.refs_1_.refs_7_
  86.2 0.0 copy-start.8
  86.2 0.0 collective-permute-done.5.back
  86.2 0.3 collective-permute-start.7
  86.5 0.5 collective-permute-start.6
  87.0 1.3 collective-permute-done.7
  88.3 1.2 add_convert_fusion.1
  89.5 1.4 collective-permute-start.8
  90.9 0.0 collective-permute-done.6.refs_0_.refs_6_
  90.9 0.0 copy-done.8
  90.9 0.0 copy-start.10
  90.9 0.9 copy-done.10
  91.8 5.8 %shard_map.99 = (bf16[320,1024]{1,0:T(8,128)(2,1)}, bf16[320,1024]{1,0:T(8,128)(2,1)}, bf16[160,1024]{1,0:T(8,128)(2,1)}, f32[160,1024]{1,0:T(8,128)}) custom-call(bf16[320,1024]{1,0:T(8,128)(2,1)} %copy-done.10, bf16[320,1024]{1,0:T(8,128)(2,1)} %copy-done.8, bf16[1024,1024]{1,0:T(8,128)(2,1)} %bitcast.25, bf16[1024,1024]{1,0:T(8,128)(2,1)} %bitcast.28), custom_call_target="tpu_custom_call" | custom-call | flops 2013265920 | bytes 8781824 | tf_op jit(solution)/shard_map/pallas_call | solution.py:103
  97.6 0.0 copy-start
  97.6 1.7 %collective-permute-done.8.refs_0_ = bf16[160,1024]{1,0:T(8,128)(2,1)S(1)} collective-permute-done((bf16[160,1024]{1,0:T(8,128)(2,1)S(1)}, bf16[160,1024]{1,0:T(8,128)(2,1)S(1)}, u32[]{:S(2)}, u32[]{:S(2)}) %collective-permute-start.8) | collective-permute-done | bytes 327712 | tf_op jit(solution)/shard_map/ppermute | solution.py:45
  99.3 0.0 collective-permute-start.9
  99.3 1.8 %collective-permute-done.9 = bf16[160,1024]{1,0:T(8,128)(2,1)S(1)} collective-permute-done((bf16[160,1024]{1,0:T(8,128)(2,1)}, bf16[160,1024]{1,0:T(8,128)(2,1)S(1)}, u32[]{:S(2)}, u32[]{:S(2)}) %collective-permute-start.9) | collective-permute-done | bytes 327712 | tf_op jit(solution)/shard_map/ppermute | solution.py:41
  101.2 1.2 add_convert_fusion
  102.3 1.4 collective-permute-start.10
  103.8 8.4 %collective-permute-done.10.refs_1_ = bf16[160,1024]{1,0:T(8,128)(2,1)S(1)} collective-permute-done((bf16[160,1024]{1,0:T(8,128)(2,1)S(1)}, bf16[160,1024]{1,0:T(8,128)(2,1)S(1)}, u32[]{:S(2)}, u32[]{:S(2)}) %collective-permute-start.10) | collective-permute-done | bytes 327712 | tf_op jit(solution)/shard_map/ppermute | solution.py:45
  112.2 0.0 copy-done
  112.2 1.2 shard_map.100
  113.4 0.0 copy-start.3
  113.4 0.0 copy-start.4
  113.4 7.7 %all-to-all-start.1 = ((bf16[64,40,128]{2,1,0:T(8,128)(2,1)}), bf16[64,40,128]{2,1,0:T(8,128)(2,1)S(1)}, u32[]{:S(2)}, u32[]{:S(2)}) async-start(bf16[64,40,128]{2,1,0:T(8,128)(2,1)} %bitcast.9), calls=%async_computation.1 | async-start | bytes 1310720 | tf_op jit(solution)/shard_map/all_to_all | solution.py:165
  121.2 0.0 copy-done.3
  121.2 0.0 copy-done.4
  121.2 12.7 %shard_map.101 = (bf16[1024,1024]{1,0:T(8,128)(2,1)}, bf16[1024,1024]{1,0:T(8,128)(2,1)}) custom-call(bf16[320,1024]{1,0:T(8,128)(2,1)} %copy-done.6, bf16[320,1024]{1,0:T(8,128)(2,1)} %copy-done.7, bf16[320,1024]{1,0:T(8,128)(2,1)} %copy-done.1, bf16[320,1024]{1,0:T(8,128)(2,1)} %copy-done.2, bf16[320,1024]{1,0:T(8,128)(2,1)} %copy-done.9, ...), custom_call_target="tpu_custom_call" | custom-call | flops 5368709120 | bytes 14680064 | tf_op jit(solution)/shard_map/pallas_call | solution.py:139
  133.9 8.6 %all-to-all-done.1 = bf16[64,40,128]{2,1,0:T(8,128)(2,1)S(1)} async-done(((bf16[64,40,128]{2,1,0:T(8,128)(2,1)}), bf16[64,40,128]{2,1,0:T(8,128)(2,1)S(1)}, u32[]{:S(2)}, u32[]{:S(2)}) %all-to-all-start.1) | async-done | bytes 655392 | tf_op jit(solution)/shard_map/all_to_all | solution.py:165
  142.6 0.3 reshape_reshape.3
  142.8 1.1 convolution_convert_fusion
  (2 shorter events, 0.0 us)
Async XLA Ops:
  53.8 15.7 %copy-start.1 = (bf16[320,1024]{1,0:T(8,128)(2,1)}, bf16[320,1024]{1,0:T(8,128)(2,1)S(1)}, u32[]{:S(2)}) copy-start(bf16[320,1024]{1,0:T(8,128)(2,1)S(1)} %shard_map.95.refs_2_) | copy-start | bytes 1966084
  53.8 15.0 %collective-permute-start.2 = (bf16[320,1024]{1,0:T(8,128)(2,1)S(1)}, bf16[320,1024]{1,0:T(8,128)(2,1)S(1)}, u32[]{:S(2)}, u32[]{:S(2)}) collective-permute-start(bf16[320,1024]{1,0:T(8,128)(2,1)S(1)} %shard_map.95.refs_2_), channel_id=1, source_target_pairs={{0,2},{2,0},{1,3},{3,1},{4,6},{6,4},{5,7},{7,5},{8,10},{10,8},{9,1... | collective-permute-start | bytes 1966088 | tf_op jit(solution)/shard_map/ppermute | solution.py:45
  54.5 14.9 %collective-permute-start = (bf16[320,1024]{1,0:T(8,128)(2,1)S(1)}, bf16[320,1024]{1,0:T(8,128)(2,1)S(1)}, u32[]{:S(2)}, u32[]{:S(2)}) collective-permute-start(bf16[320,1024]{1,0:T(8,128)(2,1)S(1)} %shard_map.95.refs_2_), channel_id=1, source_target_pairs={{0,1},{1,0},{2,3},{3,2},{4,5},{5,4},{6,7},{7,6},{8,9},{9,8},{10,11... | collective-permute-start | bytes 1966088 | tf_op jit(solution)/shard_map/ppermute | solution.py:41
  54.8 14.7 %copy-start.2 = (bf16[320,1024]{1,0:T(8,128)(2,1)}, bf16[320,1024]{1,0:T(8,128)(2,1)S(1)}, u32[]{:S(2)}) copy-start(bf16[320,1024]{1,0:T(8,128)(2,1)S(1)} %shard_map.96.refs_3_) | copy-start | bytes 1966084
  54.8 14.6 %collective-permute-start.1 = (bf16[320,1024]{1,0:T(8,128)(2,1)S(1)}, bf16[320,1024]{1,0:T(8,128)(2,1)S(1)}, u32[]{:S(2)}, u32[]{:S(2)}) collective-permute-start(bf16[320,1024]{1,0:T(8,128)(2,1)S(1)} %shard_map.96.refs_3_), channel_id=1, source_target_pairs={{0,1},{1,0},{2,3},{3,2},{4,5},{5,4},{6,7},{7,6},{8,9},{9,8},{10,11... | collective-permute-start | bytes 1966088 | tf_op jit(solution)/shard_map/ppermute | solution.py:41
  68.8 10.3 %copy-start.5 = (bf16[320,1024]{1,0:T(8,128)(2,1)}, bf16[320,1024]{1,0:T(8,128)(2,1)S(1)}, u32[]{:S(2)}) copy-start(bf16[320,1024]{1,0:T(8,128)(2,1)S(1)} %collective-permute-done.2.refs_1_.refs_5_) | copy-start | bytes 1966084
  68.8 17.4 %collective-permute-start.3 = (bf16[320,1024]{1,0:T(8,128)(2,1)S(1)}, bf16[320,1024]{1,0:T(8,128)(2,1)S(1)}, u32[]{:S(2)}, u32[]{:S(2)}) collective-permute-start(bf16[320,1024]{1,0:T(8,128)(2,1)S(1)} %shard_map.96.refs_3_), channel_id=1, source_target_pairs={{0,2},{2,0},{1,3},{3,1},{4,6},{6,4},{5,7},{7,5},{8,10},{10,8},{9,1... | collective-permute-start | bytes 1966088 | tf_op jit(solution)/shard_map/ppermute | solution.py:45
  69.4 10.1 %collective-permute-start.4 = (bf16[320,1024]{1,0:T(8,128)(2,1)S(1)}, bf16[320,1024]{1,0:T(8,128)(2,1)S(1)}, u32[]{:S(2)}, u32[]{:S(2)}) collective-permute-start(bf16[320,1024]{1,0:T(8,128)(2,1)S(1)} %collective-permute-done.2.refs_1_.refs_5_), channel_id=1, source_target_pairs={{0,1},{1,0},{2,3},{3,2},{4,5},{5,4},{6,7},{7,6},{8,9},{9,8},{10,11... | collective-permute-start | bytes 1966088 | tf_op jit(solution)/shard_map/ppermute | solution.py:41
  69.4 0.8 copy-start.6
  69.5 1.1 copy-start.7
  79.0 7.2 %collective-permute-start.5 = (bf16[320,1024]{1,0:T(8,128)(2,1)}, bf16[320,1024]{1,0:T(8,128)(2,1)S(1)}, u32[]{:S(2)}, u32[]{:S(2)}) collective-permute-start(bf16[320,1024]{1,0:T(8,128)(2,1)} %get-tuple-element.28), channel_id=1, source_target_pairs={{0,1},{1,0},{2,3},{3,2},{4,5},{5,4},{6,7},{7,6},{8,9},{9,8},{10,11... | collective-permute-start | bytes 1966088 | tf_op jit(solution)/shard_map/ppermute | solution.py:41
  79.5 0.9 copy-start.9
  86.2 4.7 %copy-start.8 = (bf16[320,1024]{1,0:T(8,128)(2,1)}, bf16[320,1024]{1,0:T(8,128)(2,1)S(1)}, u32[]{:S(2)}) copy-start(bf16[320,1024]{1,0:T(8,128)(2,1)S(1)} %collective-permute-done.3.refs_1_.refs_7_) | copy-start | bytes 1966084
  86.2 2.1 %collective-permute-start.7 = (bf16[160,1024]{1,0:T(8,128)(2,1)}, bf16[160,1024]{1,0:T(8,128)(2,1)S(1)}, u32[]{:S(2)}, u32[]{:S(2)}) collective-permute-start(bf16[160,1024]{1,0:T(8,128)(2,1)} %get-tuple-element.33), channel_id=1, source_target_pairs={{0,1},{1,0},{2,3},{3,2},{4,5},{5,4},{6,7},{7,6},{8,9},{9,8},{10,11... | collective-permute-start | bytes 983048 | tf_op jit(solution)/shard_map/ppermute | solution.py:41
  86.5 4.4 %collective-permute-start.6 = (bf16[320,1024]{1,0:T(8,128)(2,1)S(1)}, bf16[320,1024]{1,0:T(8,128)(2,1)S(1)}, u32[]{:S(2)}, u32[]{:S(2)}) collective-permute-start(bf16[320,1024]{1,0:T(8,128)(2,1)S(1)} %collective-permute-done.3.refs_1_.refs_7_), channel_id=1, source_target_pairs={{0,1},{1,0},{2,3},{3,2},{4,5},{5,4},{6,7},{7,6},{8,9},{9,8},{10,11... | collective-permute-start | bytes 1966088 | tf_op jit(solution)/shard_map/ppermute | solution.py:41
  89.5 9.8 %collective-permute-start.8 = (bf16[160,1024]{1,0:T(8,128)(2,1)S(1)}, bf16[160,1024]{1,0:T(8,128)(2,1)S(1)}, u32[]{:S(2)}, u32[]{:S(2)}) collective-permute-start(bf16[160,1024]{1,0:T(8,128)(2,1)S(1)} %add_convert_fusion.1), channel_id=1, source_target_pairs={{0,2},{2,0},{1,3},{3,1},{4,6},{6,4},{5,7},{7,5},{8,10},{10,8},{9,1... | collective-permute-start | bytes 983048 | tf_op jit(solution)/shard_map/ppermute | solution.py:45
  90.9 0.9 copy-start.10
  97.6 14.6 %copy-start = (f32[320,1024]{1,0:T(8,128)S(1)}, f32[320,1024]{1,0:T(8,128)}, u32[]{:S(2)}) copy-start(f32[320,1024]{1,0:T(8,128)} %get-tuple-element.24.near) | copy-start | bytes 3932164
  99.3 1.8 %collective-permute-start.9 = (bf16[160,1024]{1,0:T(8,128)(2,1)}, bf16[160,1024]{1,0:T(8,128)(2,1)S(1)}, u32[]{:S(2)}, u32[]{:S(2)}) collective-permute-start(bf16[160,1024]{1,0:T(8,128)(2,1)} %get-tuple-element.36), channel_id=1, source_target_pairs={{0,1},{1,0},{2,3},{3,2},{4,5},{5,4},{6,7},{7,6},{8,9},{9,8},{10,11... | collective-permute-start | bytes 983048 | tf_op jit(solution)/shard_map/ppermute | solution.py:41
  102.3 9.8 %collective-permute-start.10 = (bf16[160,1024]{1,0:T(8,128)(2,1)S(1)}, bf16[160,1024]{1,0:T(8,128)(2,1)S(1)}, u32[]{:S(2)}, u32[]{:S(2)}) collective-permute-start(bf16[160,1024]{1,0:T(8,128)(2,1)S(1)} %add_convert_fusion), channel_id=1, source_target_pairs={{0,2},{2,0},{1,3},{3,1},{4,6},{6,4},{5,7},{7,5},{8,10},{10,8},{9,1... | collective-permute-start | bytes 983048 | tf_op jit(solution)/shard_map/ppermute | solution.py:45
  113.4 7.7 %copy-start.3 = (s32[128,2]{0,1:T(2,128)S(1)}, s32[128,2]{0,1:T(2,128)}, u32[]{:S(2)}) copy-start(s32[128,2]{0,1:T(2,128)} %param.9) | copy-start | bytes 3076
  113.4 7.8 %copy-start.4 = (s32[128,2]{0,1:T(2,128)S(1)}, s32[128,2]{0,1:T(2,128)}, u32[]{:S(2)}) copy-start(s32[128,2]{0,1:T(2,128)} %param.10) | copy-start | bytes 3076
  113.4 29.1 %all-to-all-start.1 = ((bf16[64,40,128]{2,1,0:T(8,128)(2,1)}), bf16[64,40,128]{2,1,0:T(8,128)(2,1)S(1)}, u32[]{:S(2)}, u32[]{:S(2)}) async-start(bf16[64,40,128]{2,1,0:T(8,128)(2,1)} %bitcast.9), calls=%async_computation.1 | async-start | bytes 1310720 | tf_op jit(solution)/shard_map/all_to_all | solution.py:165

commit v3 on v2

--- a/solution.py
+++ b/solution.py
@@ -17,6 +17,8 @@
 SPLIT = (32, 32)
 SMALL = 16 * 2**20
 LARGE = 56 * 2**20
+EXPERT = 24 * 2**20
+GRADS = 56 * 2**20
 
 
 def dot(a, b, dims):
@@ -68,8 +70,10 @@
     sent[...] = both.reshape(-1, LANES).astype(BF)
 
 
-def unpack_kernel(senders, got, own):
-    blocks = got[...].astype(F32).reshape(senders, -1, LANES)
+def unpack_kernel(start, senders, got, own):
+    per = own.shape[0] * own.shape[1] // (senders * LANES)
+    rows = got[pl.ds(start * per, senders * per), :]
+    blocks = rows.astype(F32).reshape(senders, -1, LANES)
     per = blocks.shape[1] // 2
     n = own.shape[0] // 2
     own[pl.ds(0, n), :] = blocks[:, :per].reshape(n, -1).astype(BF)
@@ -103,7 +107,7 @@
     return kernel_call(
         functools.partial(expert_kernel, sizes),
         [shape(rows, units), shape(rows, units), shape(rows // 2, width), shape(rows // 2, width, F32)],
-        LARGE,
+        EXPERT,
         6 * rows * width * units,
         4 * width * units + 14 * rows * width,
     )(*blocks, w_in, w_out)
@@ -139,7 +143,7 @@
     return kernel_call(
         functools.partial(weight_grads_kernel, sizes, runs),
         [shape(width, units), shape(units, width)],
-        LARGE,
+        GRADS,
         4 * sum(rows) * width * units,
         4 * width * units + 8 * sum(rows) * width,
         grid=(units // tile,),
@@ -148,26 +152,24 @@
     )(*blocks, *[m[1] for m in made], *[m[2] for m in made])
 
 
-def return_kernel(capacity, near, back, *refs):
-    chips, out = refs[:-1], refs[-1]
-    start = 0
-    packed = []
-    for chip in chips:
-        n = chip.shape[0]
-        at = pl.ds(start, n)
-        rows = near[at, :] + back[at, :].astype(F32) + chip[...].astype(F32)
-        packed.append(pack(rows, n // capacity).reshape(-1, LANES))
-        start += n
-    out[...] = jnp.concatenate(packed, axis=0).astype(BF)
+def first_return_kernel(capacity, near, back, chip, packed, base):
+    n = chip.shape[0]
+    rows = near[pl.ds(0, n), :] + back[pl.ds(0, n), :].astype(F32) + chip[...].astype(F32)
+    packed[...] = pack(rows, n // capacity).reshape(-1, LANES).astype(BF)
+    rest = pl.ds(n, near.shape[0] - n)
+    base[...] = near[rest, :] + back[rest, :].astype(F32)
+
+
+def last_return_kernel(capacity, packed, base, chip, out):
+    done = packed.shape[0]
+    out[pl.ds(0, done), :] = packed[...]
+    rows = base[...] + chip[...].astype(F32)
+    out[pl.ds(done, out.shape[0] - done), :] = pack(rows, rows.shape[0] // capacity).reshape(-1, LANES).astype(BF)
 
 
 def exchange(blocks, experts):
     moved = lax.all_to_all(blocks.reshape(experts, -1, LANES), "expert", split_axis=0, concat_axis=0, tiled=True)
     return moved.reshape(-1, LANES)
-
-
-def reduce_core(away, near):
-    return to_chip((near + to_core(away).astype(F32)).astype(BF))
 
 
 def shards(tokens, upstream, expert_ids, slot_index, gate_weights, in_weight, out_weight):
@@ -186,44 +188,48 @@
     owns = []
     start = 0
     for senders in SPLIT:
-        at = start // senders
         owns.append(
             kernel_call(
-                functools.partial(unpack_kernel, senders),
+                functools.partial(unpack_kernel, start, senders),
                 shape(2 * senders * capacity, width),
                 SMALL,
                 10**6,
                 10**6,
-                grid=(1,),
-                in_specs=[pl.BlockSpec((senders * per, LANES), lambda j, at=at: (at, 0))],
-                out_specs=pl.BlockSpec((2 * senders * capacity, width), lambda j: (0, 0)),
             )(got)
         )
         start += senders
     barrier = lax.optimization_barrier
+    chips = [to_chip(own) for own in owns]
     cores = [to_core(own) for own in owns]
     blocks = cores + owns
+    chips[0], blocks[0], blocks[1] = barrier((chips[0], blocks[0], blocks[1]))
     active, grad_hidden, away_own, near_own = expert_step(blocks, w_in, w_out)
     back_own = to_core(away_own)
     made = [(blocks, active, grad_hidden)]
-    chips = [to_chip(owns[0])]
     sums = []
-    for i in range(len(owns)):
-        chip = chips[i]
-        if i + 1 < len(owns):
-            own, chip = barrier((owns[i + 1], chip))
-            chips.append(to_chip(own))
+    for i, chip in enumerate(chips):
         if i:
-            chip, away, back_own = barrier((chip, away, back_own))
-            sums.append(reduce_core(away, near))
+            chip, sent, back_own = barrier((chip, sent, back_own))
+            sums.append(to_chip(sent))
         far = to_core(chip)
         active, grad_hidden, away, near = expert_step([far, chip], w_in, w_out)
         made.append(([far, chip], active, grad_hidden))
-    away, sums[-1] = barrier((away, sums[-1]))
-    sums.append(reduce_core(away, near))
+        if sums:
+            near, sums[-1] = barrier((near, sums[-1]))
+        sent = (near + to_core(away).astype(F32)).astype(BF)
+    sums.append(to_chip(sent))
+    per = width // LANES
+    n = sums[0].shape[0]
+    packed, base = kernel_call(
+        functools.partial(first_return_kernel, capacity),
+        [shape(n * per, LANES), shape(columns - n, width, F32)],
+        SMALL,
+        10**6,
+        10**6,
+    )(near_own, back_own, sums[0])
     returned = kernel_call(
-        functools.partial(return_kernel, capacity), shape(columns * width // LANES, LANES), SMALL, 10**6, 10**6
-    )(near_own, back_own, *sums)
+        functools.partial(last_return_kernel, capacity), shape(columns * per, LANES), SMALL, 10**6, 10**6
+    )(packed, base, sums[1])
     arrived = exchange(returned, experts).reshape(columns, width)
     grad_in, grad_out = weight_grads(made, *w_in.shape)
     first, second = places(ids, slots, capacity, columns)

time: 144 us -> 136 us (0.944)
  Pallas kernels: 37.4 us -> 26.1 us
  waiting for transfers between devices: 35.3 us -> 42.3 us
  other arithmetic: 2.32 us -> 0.15 us
    pallas_call x3, Pallas kernels: 20.1 us -> 8.71 us  [expert_step(): kernel_call(functools.partial(expert_kernel, sizes), [shape(rows, units),...]
    ppermute x4, waiting for transfers between devices: 23.5 us -> 31.6 us  [to_chip(): return lax.ppermute(rows, 'replica', TO_CHIP)]
    convert_element_type x2, other arithmetic: 2.32 us -> 0.15 us  [shards(): sent = (near + to_core(away).astype(F32)).astype(BF)]
  transfers between devices with their start and end apart: 12 -> 12, of which waited for: 6 -> 7; matrix products, arithmetic and copies ran while one was open for 1% -> 0% of each run, Pallas kernels for 23% -> 16%
where the time goes in v3:
time: 136 us
  blocking collectives  50.1 us (37%)
  waiting for transfers between devices  42.3 us (31%)
  Pallas kernels  26.1 us (19%)
  starting transfers between devices  12.9 us (9%)
  local copies, waits for them, and re-layouts  2.49 us (2%)
    all_to_all x1, blocking collectives, exchange(): lax.all_to_all(blocks.reshape(experts, -1, LANES), 'expert', split_axis=0...  50.1 us
    ppermute x4, waiting for transfers between devices, to_chip(): return lax.ppermute(rows, 'replica', TO_CHIP)  31.6 us
    pallas_call x1, Pallas kernels, weight_grads(): kernel_call(functools.partial(weight_grads_kernel, sizes, runs), [shape(w...  12.7 us
    pallas_call x3, Pallas kernels, expert_step(): kernel_call(functools.partial(expert_kernel, sizes), [shape(rows, units),...  8.71 us
    all_to_all x1, waiting for transfers between devices, exchange(): lax.all_to_all(blocks.reshape(experts, -1, LANES), 'expert', split_axis=0...  8.13 us
    all_to_all x1, starting transfers between devices, exchange(): lax.all_to_all(blocks.reshape(experts, -1, LANES), 'expert', split_axis=0...  8.12 us
    ppermute x4, starting transfers between devices, to_chip(): return lax.ppermute(rows, 'replica', TO_CHIP)  3.06 us
    pallas_call x1, Pallas kernels, shards(): kernel_call(functools.partial(dispatch_kernel, experts, capacity), shape(...  2.86 us
  transfers between devices with their start and end apart: 12, of which 7 were waited for; matrix products, arithmetic and copies ran while one was open for 0% of the time, Pallas kernels for 16%

profile of v3, /device:TPU:32, one launch (start us, length us, event | category | flops | bytes accessed | tf_op | source)
XLA Modules:
  0.0 136.0 jit_solution(308543383382291090)
XLA Ops:
  0.6 2.9 %shard_map.94 = bf16[5120,128]{1,0:T(8,128)(2,1)} custom-call(bf16[128,1024]{1,0:T(8,128)(2,1)} %tokens.1, bf16[128,1024]{1,0:T(8,128)(2,1)} %upstream.1, s32[2,128]{1,0:T(2,128)} %bitcast.26, s32[2,128]{1,0:T(2,128)} %bitcast.27, f32[2,128]{1,0:T(2,128)} %bitcast.28), custom_call_target="tpu_custom_call" | custom-call | flops 1 | bytes 1 | tf_op jit(solution)/shard_map/pallas_call | solution.py:182
  3.5 50.1 %all_to_all.10 = bf16[64,80,128]{2,1,0:T(8,128)(2,1)S(1)} all-to-all(bf16[64,80,128]{2,1,0:T(8,128)(2,1)} %bitcast.25), channel_id=1, replica_groups=mesh['expert'=64,'replica'=4] {'expert'}, dimensions={0} | all-to-all | bytes 2621440 | tf_op jit(solution)/shard_map/all_to_all | solution.py:171
  53.6 0.3 shard_map.95.refs_2_
  53.9 0.0 copy-start
  53.9 0.8 collective-permute-start
  54.7 0.0 collective-permute-start.1
  54.7 0.3 shard_map.96.refs_3_
  55.0 0.0 copy-start.1
  55.0 0.6 collective-permute-start.2
  55.6 12.2 %collective-permute-done.refs_1_.refs_5_ = bf16[320,1024]{1,0:T(8,128)(2,1)S(1)} collective-permute-done((bf16[320,1024]{1,0:T(8,128)(2,1)S(1)}, bf16[320,1024]{1,0:T(8,128)(2,1)S(1)}, u32[]{:S(2)}, u32[]{:S(2)}) %collective-permute-start) | collective-permute-done | bytes 655392 | tf_op jit(solution)/shard_map/ppermute | solution.py:47
  67.8 0.0 collective-permute-done.1.refs_0_
  67.8 0.0 collective-permute-done.2.refs_1_
  67.8 0.0 copy-start.6
  67.8 0.1 collective-permute-start.4
  67.9 0.8 collective-permute-start.3
  68.7 0.0 copy-done.3
  68.7 0.0 copy-done.2
  68.7 4.3 %shard_map.97 = (bf16[640,1024]{1,0:T(8,128)(2,1)S(1)}, bf16[640,1024]{1,0:T(8,128)(2,1)S(1)}, bf16[320,1024]{1,0:T(8,128)(2,1)S(1)}, f32[320,1024]{1,0:T(8,128)S(1)}) custom-call(bf16[320,1024]{1,0:T(8,128)(2,1)S(1)} %collective-permute-done.1.refs_0_, bf16[320,1024]{1,0:T(8,128)(2,1)S(1)} %collective-permute-done.2.refs_1_, ...), custom_call_target="tpu_custom_call" | custom-call | flops 4026531840 | bytes 13369344 | tf_op jit(solution)/shard_map/pallas_call | solution.py:107
  72.9 0.0 copy-done
  72.9 0.0 copy-done.1
  72.9 0.0 copy-done.5
  73.0 0.0 copy-done.6
  73.0 0.0 copy-start.14
  73.0 1.1 copy-done.14
  74.1 1.1 copy-done.15
  75.1 0.1 collective-permute-start.6
  75.3 0.0 collective-permute-done.4.refs_0_.refs_4_
  75.3 0.0 copy-done.4
  75.3 2.2 %shard_map.98 = (bf16[320,1024]{1,0:T(8,128)(2,1)S(1)}, bf16[320,1024]{1,0:T(8,128)(2,1)S(1)}, bf16[160,1024]{1,0:T(8,128)(2,1)S(1)}, f32[160,1024]{1,0:T(8,128)S(1)}) custom-call(bf16[320,1024]{1,0:T(8,128)(2,1)S(1)} %collective-permute-done.4.refs_0_.refs_4_, bf16[320,1024]{1,0:T(8,128)(2,1)S(1)} %collective-permute-done.refs_1_.refs_5_, ...), custom_call_target="tpu_custom_call" | custom-call | flops 2013265920 | bytes 8781824 | tf_op jit(solution)/shard_map/pallas_call | solution.py:107
  77.5 0.0 copy-done.7
  77.5 0.0 copy-start.10
  77.5 0.0 copy-start.11
  77.5 0.6 collective-permute-start.5
  78.2 1.3 collective-permute-done.5
  79.4 0.1 add_convert_fusion.1
  79.5 5.5 %collective-permute-done.3.refs_1_.refs_7_ = bf16[320,1024]{1,0:T(8,128)(2,1)S(1)} collective-permute-done((bf16[320,1024]{1,0:T(8,128)(2,1)S(1)}, bf16[320,1024]{1,0:T(8,128)(2,1)S(1)}, u32[]{:S(2)}, u32[]{:S(2)}) %collective-permute-start.3) | collective-permute-done | bytes 655392 | tf_op jit(solution)/shard_map/ppermute | solution.py:47
  85.0 0.0 collective-permute-done.6.back
  85.0 0.0 collective-permute-start.7
  85.1 0.8 collective-permute-start.8
  85.8 0.0 copy-done.10
  85.8 0.0 copy-done.11
  85.8 1.3 collective-permute-done.7.refs_0_.refs_6_
  87.1 2.2 %shard_map.99 = (bf16[320,1024]{1,0:T(8,128)(2,1)S(1)}, bf16[320,1024]{1,0:T(8,128)(2,1)S(1)}, bf16[160,1024]{1,0:T(8,128)(2,1)S(1)}, f32[160,1024]{1,0:T(8,128)S(1)}) custom-call(bf16[320,1024]{1,0:T(8,128)(2,1)S(1)} %collective-permute-done.7.refs_0_.refs_6_, bf16[320,1024]{1,0:T(8,128)(2,1)S(1)} %collective-permute-done.3.refs_1_.refs_7_, ...), custom_call_target="tpu_custom_call" | custom-call | flops 2013265920 | bytes 8781824 | tf_op jit(solution)/shard_map/pallas_call | solution.py:107
  89.4 0.0 copy-done.8
  89.4 0.0 copy-done.9
  89.4 0.0 copy-start.12
  89.4 0.0 copy-start.13
  89.4 0.2 collective-permute-start.9
  89.6 5.5 %collective-permute-done.8.chip = bf16[160,1024]{1,0:T(8,128)(2,1)S(1)} collective-permute-done((bf16[160,1024]{1,0:T(8,128)(2,1)S(1)}, bf16[160,1024]{1,0:T(8,128)(2,1)S(1)}, u32[]{:S(2)}, u32[]{:S(2)}) %collective-permute-start.8) | collective-permute-done | bytes 327712 | tf_op jit(solution)/shard_map/ppermute | solution.py:47
  95.2 0.0 collective-permute-done.9
  95.2 0.1 add_convert_fusion
  95.3 0.8 collective-permute-start.10
  96.0 0.3 shard_map.100
  96.3 0.0 copy-done.12
  96.3 0.0 copy-done.13
  96.3 8.3 %collective-permute-done.10.chip = bf16[160,1024]{1,0:T(8,128)(2,1)S(1)} collective-permute-done((bf16[160,1024]{1,0:T(8,128)(2,1)S(1)}, bf16[160,1024]{1,0:T(8,128)(2,1)S(1)}, u32[]{:S(2)}, u32[]{:S(2)}) %collective-permute-start.10) | collective-permute-done | bytes 327712 | tf_op jit(solution)/shard_map/ppermute | solution.py:47
  104.6 1.0 shard_map.101
  105.7 8.1 %all-to-all-start.1 = ((bf16[64,40,128]{2,1,0:T(8,128)(2,1)}), bf16[64,40,128]{2,1,0:T(8,128)(2,1)S(1)}, u32[]{:S(2)}, u32[]{:S(2)}) async-start(bf16[64,40,128]{2,1,0:T(8,128)(2,1)} %bitcast.9), calls=%async_computation.1 | async-start | bytes 1310720 | tf_op jit(solution)/shard_map/all_to_all | solution.py:171
  113.8 0.0 copy-done.16
  113.8 0.0 copy-done.17
  113.8 12.7 %shard_map.102 = (bf16[1024,1024]{1,0:T(8,128)(2,1)}, bf16[1024,1024]{1,0:T(8,128)(2,1)}) custom-call(bf16[320,1024]{1,0:T(8,128)(2,1)} %copy-done.5, bf16[320,1024]{1,0:T(8,128)(2,1)} %copy-done.6, bf16[320,1024]{1,0:T(8,128)(2,1)} %copy-done, bf16[320,1024]{1,0:T(8,128)(2,1)} %copy-done.1, bf16[320,1024]{1,0:T(8,128)(2,1)} %copy-done.7, ...), custom_call_target="tpu_custom_call" | custom-call | flops 5368709120 | bytes 14680064 | tf_op jit(solution)/shard_map/pallas_call | solution.py:143
  126.5 8.1 %all-to-all-done.1 = bf16[64,40,128]{2,1,0:T(8,128)(2,1)S(1)} async-done(((bf16[64,40,128]{2,1,0:T(8,128)(2,1)}), bf16[64,40,128]{2,1,0:T(8,128)(2,1)S(1)}, u32[]{:S(2)}, u32[]{:S(2)}) %all-to-all-start.1) | async-done | bytes 655392 | tf_op jit(solution)/shard_map/all_to_all | solution.py:171
  134.7 0.3 reshape_reshape.3
  134.9 1.1 convolution_convert_fusion
  (12 shorter events, 0.0 us)
Async XLA Ops:
  3.5 65.2 %copy-start.3 = (bf16[1,1024,1024]{2,1,0:T(8,128)(2,1)S(1)}, bf16[1,1024,1024]{2,1,0:T(8,128)(2,1)}, u32[]{:S(2)}) copy-start(bf16[1,1024,1024]{2,1,0:T(8,128)(2,1)} %param.13) | copy-start | bytes 6291460
  53.6 15.0 %copy-start.2 = (bf16[1,1024,1024]{2,1,0:T(8,128)(2,1)S(1)}, bf16[1,1024,1024]{2,1,0:T(8,128)(2,1)}, u32[]{:S(2)}) copy-start(bf16[1,1024,1024]{2,1,0:T(8,128)(2,1)} %param.12) | copy-start | bytes 6291460
  53.9 19.0 %copy-start = (bf16[320,1024]{1,0:T(8,128)(2,1)}, bf16[320,1024]{1,0:T(8,128)(2,1)S(1)}, u32[]{:S(2)}) copy-start(bf16[320,1024]{1,0:T(8,128)(2,1)S(1)} %shard_map.95.refs_2_) | copy-start | bytes 1966084
  53.9 13.9 %collective-permute-start = (bf16[320,1024]{1,0:T(8,128)(2,1)S(1)}, bf16[320,1024]{1,0:T(8,128)(2,1)S(1)}, u32[]{:S(2)}, u32[]{:S(2)}) collective-permute-start(bf16[320,1024]{1,0:T(8,128)(2,1)S(1)} %shard_map.95.refs_2_), channel_id=1, source_target_pairs={{0,2},{2,0},{1,3},{3,1},{4,6},{6,4},{5,7},{7,5},{8,10},{10,8},{9,1... | collective-permute-start | bytes 1966088 | tf_op jit(solution)/shard_map/ppermute | solution.py:47
  54.7 13.1 %collective-permute-start.1 = (bf16[320,1024]{1,0:T(8,128)(2,1)S(1)}, bf16[320,1024]{1,0:T(8,128)(2,1)S(1)}, u32[]{:S(2)}, u32[]{:S(2)}) collective-permute-start(bf16[320,1024]{1,0:T(8,128)(2,1)S(1)} %shard_map.95.refs_2_), channel_id=1, source_target_pairs={{0,1},{1,0},{2,3},{3,2},{4,5},{5,4},{6,7},{7,6},{8,9},{9,8},{10,11... | collective-permute-start | bytes 1966088 | tf_op jit(solution)/shard_map/ppermute | solution.py:43
  55.0 18.0 %copy-start.1 = (bf16[320,1024]{1,0:T(8,128)(2,1)}, bf16[320,1024]{1,0:T(8,128)(2,1)S(1)}, u32[]{:S(2)}) copy-start(bf16[320,1024]{1,0:T(8,128)(2,1)S(1)} %shard_map.96.refs_3_) | copy-start | bytes 1966084
  55.0 12.8 %collective-permute-start.2 = (bf16[320,1024]{1,0:T(8,128)(2,1)S(1)}, bf16[320,1024]{1,0:T(8,128)(2,1)S(1)}, u32[]{:S(2)}, u32[]{:S(2)}) collective-permute-start(bf16[320,1024]{1,0:T(8,128)(2,1)S(1)} %shard_map.96.refs_3_), channel_id=1, source_target_pairs={{0,1},{1,0},{2,3},{3,2},{4,5},{5,4},{6,7},{7,6},{8,9},{9,8},{10,11... | collective-permute-start | bytes 1966088 | tf_op jit(solution)/shard_map/ppermute | solution.py:43
  67.8 7.5 %copy-start.4 = (bf16[320,1024]{1,0:T(8,128)(2,1)}, bf16[320,1024]{1,0:T(8,128)(2,1)S(1)}, u32[]{:S(2)}) copy-start(bf16[320,1024]{1,0:T(8,128)(2,1)S(1)} %collective-permute-done.refs_1_.refs_5_) | copy-start | bytes 1966084
  67.8 5.2 %copy-start.5 = (bf16[320,1024]{1,0:T(8,128)(2,1)}, bf16[320,1024]{1,0:T(8,128)(2,1)S(1)}, u32[]{:S(2)}) copy-start(bf16[320,1024]{1,0:T(8,128)(2,1)S(1)} %collective-permute-done.1.refs_0_) | copy-start | bytes 1966084
  67.8 5.2 %copy-start.6 = (bf16[320,1024]{1,0:T(8,128)(2,1)}, bf16[320,1024]{1,0:T(8,128)(2,1)S(1)}, u32[]{:S(2)}) copy-start(bf16[320,1024]{1,0:T(8,128)(2,1)S(1)} %collective-permute-done.2.refs_1_) | copy-start | bytes 1966084
  67.8 7.5 %collective-permute-start.4 = (bf16[320,1024]{1,0:T(8,128)(2,1)S(1)}, bf16[320,1024]{1,0:T(8,128)(2,1)S(1)}, u32[]{:S(2)}, u32[]{:S(2)}) collective-permute-start(bf16[320,1024]{1,0:T(8,128)(2,1)S(1)} %collective-permute-done.refs_1_.refs_5_), channel_id=1, source_target_pairs={{0,1},{1,0},{2,3},{3,2},{4,5},{5,4},{6,7},{7,6},{8,9},{9,8},{10,11... | collective-permute-start | bytes 1966088 | tf_op jit(solution)/shard_map/ppermute | solution.py:43
  67.9 17.2 %collective-permute-start.3 = (bf16[320,1024]{1,0:T(8,128)(2,1)S(1)}, bf16[320,1024]{1,0:T(8,128)(2,1)S(1)}, u32[]{:S(2)}, u32[]{:S(2)}) collective-permute-start(bf16[320,1024]{1,0:T(8,128)(2,1)S(1)} %shard_map.96.refs_3_), channel_id=1, source_target_pairs={{0,2},{2,0},{1,3},{3,1},{4,6},{6,4},{5,7},{7,5},{8,10},{10,8},{9,1... | collective-permute-start | bytes 1966088 | tf_op jit(solution)/shard_map/ppermute | solution.py:47
  73.0 1.1 copy-start.14
  74.0 1.1 copy-start.15
  75.1 9.9 %collective-permute-start.6 = (bf16[320,1024]{1,0:T(8,128)(2,1)S(1)}, bf16[320,1024]{1,0:T(8,128)(2,1)S(1)}, u32[]{:S(2)}, u32[]{:S(2)}) collective-permute-start(bf16[320,1024]{1,0:T(8,128)(2,1)S(1)} %get-tuple-element.33), channel_id=1, source_target_pairs={{0,1},{1,0},{2,3},{3,2},{4,5},{5,4},{6,7},{7,6},{8,9},{9,8},{10,11... | collective-permute-start | bytes 1966088 | tf_op jit(solution)/shard_map/ppermute | solution.py:43
  75.3 2.2 %copy-start.7 = (bf16[320,1024]{1,0:T(8,128)(2,1)}, bf16[320,1024]{1,0:T(8,128)(2,1)S(1)}, u32[]{:S(2)}) copy-start(bf16[320,1024]{1,0:T(8,128)(2,1)S(1)} %collective-permute-done.4.refs_0_.refs_4_) | copy-start | bytes 1966084
  77.5 8.3 %copy-start.10 = (bf16[320,1024]{1,0:T(8,128)(2,1)}, bf16[320,1024]{1,0:T(8,128)(2,1)S(1)}, u32[]{:S(2)}) copy-start(bf16[320,1024]{1,0:T(8,128)(2,1)S(1)} %get-tuple-element.44.refs_9_) | copy-start | bytes 1966084
  77.5 8.3 %copy-start.11 = (bf16[320,1024]{1,0:T(8,128)(2,1)}, bf16[320,1024]{1,0:T(8,128)(2,1)S(1)}, u32[]{:S(2)}) copy-start(bf16[320,1024]{1,0:T(8,128)(2,1)S(1)} %get-tuple-element.47.refs_12_) | copy-start | bytes 1966084
  77.5 1.9 %collective-permute-start.5 = (bf16[160,1024]{1,0:T(8,128)(2,1)S(1)}, bf16[160,1024]{1,0:T(8,128)(2,1)S(1)}, u32[]{:S(2)}, u32[]{:S(2)}) collective-permute-start(bf16[160,1024]{1,0:T(8,128)(2,1)S(1)} %get-tuple-element.32), channel_id=1, source_target_pairs={{0,1},{1,0},{2,3},{3,2},{4,5},{5,4},{6,7},{7,6},{8,9},{9,8},{10,11... | collective-permute-start | bytes 983048 | tf_op jit(solution)/shard_map/ppermute | solution.py:43
  85.0 4.3 %copy-start.8 = (bf16[320,1024]{1,0:T(8,128)(2,1)}, bf16[320,1024]{1,0:T(8,128)(2,1)S(1)}, u32[]{:S(2)}) copy-start(bf16[320,1024]{1,0:T(8,128)(2,1)S(1)} %collective-permute-done.3.refs_1_.refs_7_) | copy-start | bytes 1966084
  85.0 2.1 %collective-permute-start.7 = (bf16[320,1024]{1,0:T(8,128)(2,1)S(1)}, bf16[320,1024]{1,0:T(8,128)(2,1)S(1)}, u32[]{:S(2)}, u32[]{:S(2)}) collective-permute-start(bf16[320,1024]{1,0:T(8,128)(2,1)S(1)} %collective-permute-done.3.refs_1_.refs_7_), channel_id=1, source_target_pairs={{0,1},{1,0},{2,3},{3,2},{4,5},{5,4},{6,7},{7,6},{8,9},{9,8},{10,11... | collective-permute-start | bytes 1966088 | tf_op jit(solution)/shard_map/ppermute | solution.py:43
  85.1 10.1 %collective-permute-start.8 = (bf16[160,1024]{1,0:T(8,128)(2,1)S(1)}, bf16[160,1024]{1,0:T(8,128)(2,1)S(1)}, u32[]{:S(2)}, u32[]{:S(2)}) collective-permute-start(bf16[160,1024]{1,0:T(8,128)(2,1)S(1)} %add_convert_fusion.1), channel_id=1, source_target_pairs={{0,2},{2,0},{1,3},{3,1},{4,6},{6,4},{5,7},{7,5},{8,10},{10,8},{9,1... | collective-permute-start | bytes 983048 | tf_op jit(solution)/shard_map/ppermute | solution.py:47
  87.1 2.2 %copy-start.9 = (bf16[320,1024]{1,0:T(8,128)(2,1)}, bf16[320,1024]{1,0:T(8,128)(2,1)S(1)}, u32[]{:S(2)}) copy-start(bf16[320,1024]{1,0:T(8,128)(2,1)S(1)} %collective-permute-done.7.refs_0_.refs_6_) | copy-start | bytes 1966084
  89.4 6.9 %copy-start.12 = (bf16[320,1024]{1,0:T(8,128)(2,1)}, bf16[320,1024]{1,0:T(8,128)(2,1)S(1)}, u32[]{:S(2)}) copy-start(bf16[320,1024]{1,0:T(8,128)(2,1)S(1)} %get-tuple-element.45.refs_10_) | copy-start | bytes 1966084
  89.4 6.9 %copy-start.13 = (bf16[320,1024]{1,0:T(8,128)(2,1)}, bf16[320,1024]{1,0:T(8,128)(2,1)S(1)}, u32[]{:S(2)}) copy-start(bf16[320,1024]{1,0:T(8,128)(2,1)S(1)} %get-tuple-element.48.refs_13_) | copy-start | bytes 1966084
  89.4 5.8 %collective-permute-start.9 = (bf16[160,1024]{1,0:T(8,128)(2,1)S(1)}, bf16[160,1024]{1,0:T(8,128)(2,1)S(1)}, u32[]{:S(2)}, u32[]{:S(2)}) collective-permute-start(bf16[160,1024]{1,0:T(8,128)(2,1)S(1)} %get-tuple-element.42), channel_id=1, source_target_pairs={{0,1},{1,0},{2,3},{3,2},{4,5},{5,4},{6,7},{7,6},{8,9},{9,8},{10,11... | collective-permute-start | bytes 983048 | tf_op jit(solution)/shard_map/ppermute | solution.py:43
  95.3 9.3 %collective-permute-start.10 = (bf16[160,1024]{1,0:T(8,128)(2,1)S(1)}, bf16[160,1024]{1,0:T(8,128)(2,1)S(1)}, u32[]{:S(2)}, u32[]{:S(2)}) collective-permute-start(bf16[160,1024]{1,0:T(8,128)(2,1)S(1)} %add_convert_fusion), channel_id=1, source_target_pairs={{0,2},{2,0},{1,3},{3,1},{4,6},{6,4},{5,7},{7,5},{8,10},{10,8},{9,1... | collective-permute-start | bytes 983048 | tf_op jit(solution)/shard_map/ppermute | solution.py:47
  104.6 9.2 %copy-start.16 = (s32[128,2]{0,1:T(2,128)S(1)}, s32[128,2]{0,1:T(2,128)}, u32[]{:S(2)}) copy-start(s32[128,2]{0,1:T(2,128)} %param.9) | copy-start | bytes 3076
  104.6 9.2 %copy-start.17 = (s32[128,2]{0,1:T(2,128)S(1)}, s32[128,2]{0,1:T(2,128)}, u32[]{:S(2)}) copy-start(s32[128,2]{0,1:T(2,128)} %param.10) | copy-start | bytes 3076
  105.7 29.0 %all-to-all-start.1 = ((bf16[64,40,128]{2,1,0:T(8,128)(2,1)}), bf16[64,40,128]{2,1,0:T(8,128)(2,1)S(1)}, u32[]{:S(2)}, u32[]{:S(2)}) async-start(bf16[64,40,128]{2,1,0:T(8,128)(2,1)} %bitcast.9), calls=%async_computation.1 | async-start | bytes 1310720 | tf_op jit(solution)/shard_map/all_to_all | solution.py:171

commit v4 on v3

--- a/solution.py
+++ b/solution.py
@@ -15,6 +15,8 @@
 TO_CORE = ((0, 1), (1, 0), (2, 3), (3, 2))
 TO_CHIP = ((0, 2), (2, 0), (1, 3), (3, 1))
 SPLIT = (32, 32)
+FAR = 4
+BACK = 2
 SMALL = 16 * 2**20
 LARGE = 56 * 2**20
 EXPERT = 24 * 2**20
@@ -80,12 +82,27 @@
     own[pl.ds(n, n), :] = blocks[:, per:].reshape(n, -1).astype(BF)
 
 
-def expert_kernel(sizes, *refs):
-    blocks, refs = refs[: len(sizes)], refs[len(sizes) :]
+def rows_of(counts, refs):
+    x, g = [], []
+    at = 0
+    for count in counts:
+        pieces = refs[at : at + count]
+        at += count
+        if count == 1:
+            n = pieces[0].shape[0] // 2
+            x.append(pieces[0][pl.ds(0, n), :])
+            g.append(pieces[0][pl.ds(n, n), :])
+        else:
+            x += [piece[...] for piece in pieces[: count // 2]]
+            g += [piece[...] for piece in pieces[count // 2 :]]
+    return jnp.concatenate(x, axis=0), jnp.concatenate(g, axis=0)
+
+
+def expert_kernel(counts, *refs):
+    blocks, refs = refs[: sum(counts)], refs[sum(counts) :]
     w_in, w_out, active, grad_hidden, away, near = refs
     split = away.shape[0]
-    x = jnp.concatenate([block[pl.ds(0, n), :] for n, block in zip(sizes, blocks)], axis=0)
-    g = jnp.concatenate([block[pl.ds(n, n), :] for n, block in zip(sizes, blocks)], axis=0)
+    x, g = rows_of(counts, blocks)
     hidden = dot(x, w_in[...], ((1,), (0,)))
     carried = dot(g, w_out[...], ((1,), (1,)))
     square = hidden * hidden
@@ -102,10 +119,11 @@
 
 def expert_step(blocks, w_in, w_out):
     width, units = w_in.shape
-    sizes = [block.shape[0] // 2 for block in blocks]
-    rows = sum(sizes)
+    counts = [len(block) for block in blocks]
+    blocks = [piece for block in blocks for piece in block]
+    rows = sum(piece.shape[0] for piece in blocks) // 2
     return kernel_call(
-        functools.partial(expert_kernel, sizes),
+        functools.partial(expert_kernel, counts),
         [shape(rows, units), shape(rows, units), shape(rows // 2, width), shape(rows // 2, width, F32)],
         EXPERT,
         6 * rows * width * units,
@@ -113,18 +131,16 @@
     )(*blocks, w_in, w_out)
 
 
-def weight_grads_kernel(sizes, runs, *refs):
-    blocks, refs = refs[: len(sizes)], refs[len(sizes) :]
-    count = len(runs)
-    actives, refs = refs[:count], refs[count:]
-    grad_hiddens, (grad_in, grad_out) = refs[:count], refs[count:]
+def weight_grads_kernel(groups, *refs):
+    total = sum(sum(counts) for counts in groups)
+    blocks, refs = refs[:total], refs[total:]
+    actives, refs = refs[: len(groups)], refs[len(groups) :]
+    grad_hiddens, (grad_in, grad_out) = refs[: len(groups)], refs[len(groups) :]
     out_sum = in_sum = None
     at = 0
-    for active, grad_hidden, run in zip(actives, grad_hiddens, runs):
-        sides = list(zip(sizes[at : at + run], blocks[at : at + run]))
-        at += run
-        x = jnp.concatenate([block[pl.ds(0, n), :] for n, block in sides], axis=0)
-        g = jnp.concatenate([block[pl.ds(n, n), :] for n, block in sides], axis=0)
+    for active, grad_hidden, counts in zip(actives, grad_hiddens, groups):
+        x, g = rows_of(counts, blocks[at : at + sum(counts)])
+        at += sum(counts)
         out_part = dot(active[...], g, ((0,), (0,)))
         in_part = dot(grad_hidden[...], x, ((0,), (0,)))
         out_sum = out_part if out_sum is None else out_sum + out_part
@@ -135,21 +151,25 @@
 
 def weight_grads(made, width, units):
     tile = 256
-    blocks = [block for group, _, _ in made for block in group]
-    sizes = [block.shape[0] // 2 for block in blocks]
-    runs = [len(group) for group, _, _ in made]
+    groups = [[len(block) for block in blocks] for blocks, _, _ in made]
+    pieces = [piece for blocks, _, _ in made for block in blocks for piece in block]
     rows = [active.shape[0] for _, active, _ in made]
     columns = [pl.BlockSpec((n, tile), lambda j: (0, j)) for n in rows]
     return kernel_call(
-        functools.partial(weight_grads_kernel, sizes, runs),
+        functools.partial(weight_grads_kernel, groups),
         [shape(width, units), shape(units, width)],
         GRADS,
         4 * sum(rows) * width * units,
         4 * width * units + 8 * sum(rows) * width,
         grid=(units // tile,),
-        in_specs=[pl.BlockSpec((2 * n, width), lambda j: (0, 0)) for n in sizes] + columns + columns,
+        in_specs=[pl.BlockSpec(piece.shape, lambda j: (0, 0)) for piece in pieces] + columns + columns,
         out_specs=[pl.BlockSpec((width, tile), lambda j: (0, j)), pl.BlockSpec((tile, width), lambda j: (j, 0))],
-    )(*blocks, *[m[1] for m in made], *[m[2] for m in made])
+    )(*pieces, *[m[1] for m in made], *[m[2] for m in made])
+
+
+def core_pieces(rows, count):
+    step = rows.shape[0] // count
+    return [to_core(rows[i * step : (i + 1) * step]) for i in range(count)]
 
 
 def first_return_kernel(capacity, near, back, chip, packed, base):
@@ -201,8 +221,7 @@
     barrier = lax.optimization_barrier
     chips = [to_chip(own) for own in owns]
     cores = [to_core(own) for own in owns]
-    blocks = cores + owns
-    chips[0], blocks[0], blocks[1] = barrier((chips[0], blocks[0], blocks[1]))
+    blocks = [[block] for block in cores + owns]
     active, grad_hidden, away_own, near_own = expert_step(blocks, w_in, w_out)
     back_own = to_core(away_own)
     made = [(blocks, active, grad_hidden)]
@@ -211,12 +230,12 @@
         if i:
             chip, sent, back_own = barrier((chip, sent, back_own))
             sums.append(to_chip(sent))
-        far = to_core(chip)
-        active, grad_hidden, away, near = expert_step([far, chip], w_in, w_out)
-        made.append(([far, chip], active, grad_hidden))
+        blocks = [core_pieces(chip, FAR), [chip]]
+        active, grad_hidden, away, near = expert_step(blocks, w_in, w_out)
+        made.append((blocks, active, grad_hidden))
         if sums:
             near, sums[-1] = barrier((near, sums[-1]))
-        sent = (near + to_core(away).astype(F32)).astype(BF)
+        sent = (near + jnp.concatenate(core_pieces(away, BACK), axis=0).astype(F32)).astype(BF)
     sums.append(to_chip(sent))
     per = width // LANES
     n = sums[0].shape[0]

time: 136 us -> 133 us (0.978)
  waiting for transfers between devices: 42.3 us -> 38.1 us
  starting transfers between devices: 12.9 us -> 15.6 us
  local copies, waits for them, and re-layouts: 2.49 us -> 0.52 us
    ppermute x4, waiting for transfers between devices: 31.6 us -> 28.6 us  [to_chip(): return lax.ppermute(rows, 'replica', TO_CHIP)]
    ppermute x7 -> x15, starting transfers between devices: 1.69 us -> 4.37 us  [to_core(): return lax.ppermute(rows, 'replica', TO_CORE)]
    unnamed x36 -> x48, local copies, waits for them, and re-layouts: 2.21 us -> 0.1 us
  transfers between devices with their start and end apart: 12 -> 20, of which waited for: 7 -> 8; matrix products, arithmetic and copies ran while one was open for 0% -> 0% of each run, Pallas kernels for 16% -> 17%
where the time goes in v4:
time: 133 us
  blocking collectives  50 us (38%)
  waiting for transfers between devices  38.1 us (29%)
  Pallas kernels  26.1 us (20%)
  starting transfers between devices  15.6 us (12%)
    all_to_all x1, blocking collectives, exchange(): lax.all_to_all(blocks.reshape(experts, -1, LANES), 'expert', split_axis=0...  50 us
    ppermute x4, waiting for transfers between devices, to_chip(): return lax.ppermute(rows, 'replica', TO_CHIP)  28.6 us
    pallas_call x1, Pallas kernels, weight_grads(): kernel_call(functools.partial(weight_grads_kernel, groups), [shape(width,...  12.7 us
    pallas_call x3, Pallas kernels, expert_step(): kernel_call(functools.partial(expert_kernel, counts), [shape(rows, units)...  8.71 us
    all_to_all x1, waiting for transfers between devices, exchange(): lax.all_to_all(blocks.reshape(experts, -1, LANES), 'expert', split_axis=0...  7.72 us
    all_to_all x1, starting transfers between devices, exchange(): lax.all_to_all(blocks.reshape(experts, -1, LANES), 'expert', split_axis=0...  7.69 us
    ppermute x15, starting transfers between devices, to_core(): return lax.ppermute(rows, 'replica', TO_CORE)  4.37 us
    ppermute x4, starting transfers between devices, to_chip(): return lax.ppermute(rows, 'replica', TO_CHIP)  3.55 us
  transfers between devices with their start and end apart: 20, of which 8 were waited for; matrix products, arithmetic and copies ran while one was open for 0% of the time, Pallas kernels for 17%

profile of v4, /device:TPU:32, one launch (start us, length us, event | category | flops | bytes accessed | tf_op | source)
XLA Modules:
  0.0 132.6 jit_solution(11209819642647421187)
XLA Ops:
  0.6 2.9 %shard_map.94 = bf16[5120,128]{1,0:T(8,128)(2,1)} custom-call(bf16[128,1024]{1,0:T(8,128)(2,1)} %tokens.1, bf16[128,1024]{1,0:T(8,128)(2,1)} %upstream.1, s32[2,128]{1,0:T(2,128)} %bitcast.26, s32[2,128]{1,0:T(2,128)} %bitcast.27, f32[2,128]{1,0:T(2,128)} %bitcast.28), custom_call_target="tpu_custom_call" | custom-call | flops 1 | bytes 1 | tf_op jit(solution)/shard_map/pallas_call | solution.py:202
  3.5 50.0 %all_to_all.10 = bf16[64,80,128]{2,1,0:T(8,128)(2,1)S(1)} all-to-all(bf16[64,80,128]{2,1,0:T(8,128)(2,1)} %bitcast.25), channel_id=1, replica_groups=mesh['expert'=64,'replica'=4] {'expert'}, dimensions={0} | all-to-all | bytes 2621440 | tf_op jit(solution)/shard_map/all_to_all | solution.py:191
  53.5 0.3 shard_map.95.refs_2_
  53.8 0.0 copy-start.4
  53.8 0.8 collective-permute-start.3
  54.6 0.0 collective-permute-start
  54.6 0.3 shard_map.96.refs_3_
  54.8 0.6 collective-permute-start.1
  55.4 1.3 %collective-permute-start.2 = (bf16[320,1024]{1,0:T(8,128)(2,1)S(1)}, bf16[320,1024]{1,0:T(8,128)(2,1)S(1)}, u32[]{:S(2)}, u32[]{:S(2)}) collective-permute-start(bf16[320,1024]{1,0:T(8,128)(2,1)S(1)} %shard_map.96.refs_3_), channel_id=1, source_target_pairs={{0,2},{2,0},{1,3},{3,1},{4,6},{6,4},{5,7},{7,5},{8,10},{10,8},{9,1... | collective-permute-start | bytes 1966088 | tf_op jit(solution)/shard_map/ppermute | solution.py:49
  56.8 14.8 %collective-permute-done.3.refs_4_.refs_8_ = bf16[320,1024]{1,0:T(8,128)(2,1)S(1)} collective-permute-done((bf16[320,1024]{1,0:T(8,128)(2,1)S(1)}, bf16[320,1024]{1,0:T(8,128)(2,1)S(1)}, u32[]{:S(2)}, u32[]{:S(2)}) %collective-permute-start.3) | collective-permute-done | bytes 655392 | tf_op jit(solution)/shard_map/ppermute | solution.py:49
  71.6 0.1 collective-permute-start.4
  71.7 0.5 collective-permute-start.5
  72.2 0.0 collective-permute-done.refs_0_
  72.2 0.1 collective-permute-start.6
  72.3 0.0 collective-permute-done.1.refs_1_
  72.3 0.4 collective-permute-start.7
  72.7 0.0 copy-done.2
  72.7 0.0 copy-done.4
  72.7 4.3 %shard_map.97 = (bf16[640,1024]{1,0:T(8,128)(2,1)S(1)}, bf16[640,1024]{1,0:T(8,128)(2,1)S(1)}, bf16[320,1024]{1,0:T(8,128)(2,1)S(1)}, f32[320,1024]{1,0:T(8,128)S(1)}) custom-call(bf16[320,1024]{1,0:T(8,128)(2,1)S(1)} %collective-permute-done.refs_0_, bf16[320,1024]{1,0:T(8,128)(2,1)S(1)} %collective-permute-done.1.refs_1_, ...), custom_call_target="tpu_custom_call" | custom-call | flops 4026531840 | bytes 13369344 | tf_op jit(solution)/shard_map/pallas_call | solution.py:125
  77.0 0.0 copy-done.3
  77.0 0.0 copy-done.6
  77.0 0.0 copy-done.7
  77.0 0.0 copy-start.20
  77.0 0.0 copy-start.21
  77.0 0.0 collective-permute-done.4.refs_0_.refs_4_
  77.1 0.0 copy-start.8
  77.1 0.4 collective-permute-start.10
  77.4 0.0 collective-permute-done.5.refs_1_.refs_5_
  77.4 0.0 collective-permute-done.6.refs_2_.refs_6_
  77.5 0.0 collective-permute-done.7.refs_3_.refs_7_
  77.5 0.0 copy-done
  77.5 2.2 %shard_map.98 = (bf16[320,1024]{1,0:T(8,128)(2,1)S(1)}, bf16[320,1024]{1,0:T(8,128)(2,1)S(1)}, bf16[160,1024]{1,0:T(8,128)(2,1)S(1)}, f32[160,1024]{1,0:T(8,128)S(1)}) custom-call(bf16[80,1024]{1,0:T(8,128)(2,1)S(1)} %collective-permute-done.4.refs_0_.refs_4_, bf16[80,1024]{1,0:T(8,128)(2,1)S(1)} %collective-permute-done.5.refs_1_.refs_5_, ...), custom_call_target="tpu_custom_call" | custom-call | flops 2013265920 | bytes 8781824 | tf_op jit(solution)/shard_map/pallas_call | solution.py:125
  79.8 0.5 collective-permute-start.9
  80.3 0.1 collective-permute-start.8
  80.4 0.9 collective-permute-done.9
  81.3 0.4 collective-permute-done.8
  81.7 0.1 add_convert_fusion.1
  81.8 0.0 collective-permute-done.2.refs_4_.refs_13_
  81.8 0.0 collective-permute-done.10.back
  81.9 0.3 collective-permute-start.11
  82.2 0.3 collective-permute-start.12
  82.5 0.2 collective-permute-start.13
  82.7 0.3 collective-permute-start.14
  83.0 0.7 collective-permute-start.15
  83.7 0.0 collective-permute-done.11.refs_0_.refs_9_
  83.7 0.0 collective-permute-done.12.refs_1_.refs_10_
  83.7 0.2 collective-permute-done.13.refs_2_.refs_11_
  83.9 0.2 collective-permute-done.14.refs_3_.refs_12_
  84.1 2.2 %shard_map.99 = (bf16[320,1024]{1,0:T(8,128)(2,1)S(1)}, bf16[320,1024]{1,0:T(8,128)(2,1)S(1)}, bf16[160,1024]{1,0:T(8,128)(2,1)S(1)}, f32[160,1024]{1,0:T(8,128)S(1)}) custom-call(bf16[80,1024]{1,0:T(8,128)(2,1)S(1)} %collective-permute-done.11.refs_0_.refs_9_, bf16[80,1024]{1,0:T(8,128)(2,1)S(1)} %collective-permute-done.12.refs_1_.refs_10_, ...), custom_call_target="tpu_custom_call" | custom-call | flops 2013265920 | bytes 8781824 | tf_op jit(solution)/shard_map/pallas_call | solution.py:125
  86.5 0.4 collective-permute-start.17
  86.8 0.2 collective-permute-start.16
  87.1 5.8 %collective-permute-done.15.chip = bf16[160,1024]{1,0:T(8,128)(2,1)S(1)} collective-permute-done((bf16[160,1024]{1,0:T(8,128)(2,1)S(1)}, bf16[160,1024]{1,0:T(8,128)(2,1)S(1)}, u32[]{:S(2)}, u32[]{:S(2)}) %collective-permute-start.15) | collective-permute-done | bytes 327712 | tf_op jit(solution)/shard_map/ppermute | solution.py:49
  92.9 0.0 collective-permute-done.17
  92.9 0.0 collective-permute-done.16
  92.9 0.1 add_convert_fusion
  93.0 0.8 collective-permute-start.18
  93.7 0.3 shard_map.100
  94.0 8.1 %collective-permute-done.18.chip = bf16[160,1024]{1,0:T(8,128)(2,1)S(1)} collective-permute-done((bf16[160,1024]{1,0:T(8,128)(2,1)S(1)}, bf16[160,1024]{1,0:T(8,128)(2,1)S(1)}, u32[]{:S(2)}, u32[]{:S(2)}) %collective-permute-start.18) | collective-permute-done | bytes 327712 | tf_op jit(solution)/shard_map/ppermute | solution.py:49
  102.1 1.0 shard_map.101
  103.1 7.7 %all-to-all-start.1 = ((bf16[64,40,128]{2,1,0:T(8,128)(2,1)}), bf16[64,40,128]{2,1,0:T(8,128)(2,1)S(1)}, u32[]{:S(2)}, u32[]{:S(2)}) async-start(bf16[64,40,128]{2,1,0:T(8,128)(2,1)} %bitcast.9), calls=%async_computation.1 | async-start | bytes 1310720 | tf_op jit(solution)/shard_map/all_to_all | solution.py:191
  110.9 12.7 %shard_map.102 = (bf16[1024,1024]{1,0:T(8,128)(2,1)}, bf16[1024,1024]{1,0:T(8,128)(2,1)}) custom-call(bf16[320,1024]{1,0:T(8,128)(2,1)} %copy-done.6, bf16[320,1024]{1,0:T(8,128)(2,1)} %copy-done.7, bf16[320,1024]{1,0:T(8,128)(2,1)} %copy-done.2, bf16[320,1024]{1,0:T(8,128)(2,1)} %copy-done.3, bf16[80,1024]{1,0:T(8,128)(2,1)} %copy-done.8, ...), custom_call_target="tpu_custom_call" | custom-call | flops 5368709120 | bytes 14680064 | tf_op jit(solution)/shard_map/pallas_call | solution.py:158
  123.6 7.7 %all-to-all-done.1 = bf16[64,40,128]{2,1,0:T(8,128)(2,1)S(1)} async-done(((bf16[64,40,128]{2,1,0:T(8,128)(2,1)}), bf16[64,40,128]{2,1,0:T(8,128)(2,1)S(1)}, u32[]{:S(2)}, u32[]{:S(2)}) %all-to-all-start.1) | async-done | bytes 655392 | tf_op jit(solution)/shard_map/all_to_all | solution.py:191
  131.3 0.3 reshape_reshape.3
  131.6 1.1 convolution_convert_fusion
  (44 shorter events, 0.2 us)
Async XLA Ops:
  53.5 19.2 %copy-start.5 = (bf16[1,1024,1024]{2,1,0:T(8,128)(2,1)S(1)}, bf16[1,1024,1024]{2,1,0:T(8,128)(2,1)}, u32[]{:S(2)}) copy-start(bf16[1,1024,1024]{2,1,0:T(8,128)(2,1)} %param.13) | copy-start | bytes 6291460
  53.8 18.9 %copy-start.2 = (bf16[320,1024]{1,0:T(8,128)(2,1)}, bf16[320,1024]{1,0:T(8,128)(2,1)S(1)}, u32[]{:S(2)}) copy-start(bf16[320,1024]{1,0:T(8,128)(2,1)S(1)} %shard_map.95.refs_2_) | copy-start | bytes 1966084
  53.8 18.9 %copy-start.4 = (bf16[1,1024,1024]{2,1,0:T(8,128)(2,1)S(1)}, bf16[1,1024,1024]{2,1,0:T(8,128)(2,1)}, u32[]{:S(2)}) copy-start(bf16[1,1024,1024]{2,1,0:T(8,128)(2,1)} %param.12) | copy-start | bytes 6291460
  53.8 17.8 %collective-permute-start.3 = (bf16[320,1024]{1,0:T(8,128)(2,1)S(1)}, bf16[320,1024]{1,0:T(8,128)(2,1)S(1)}, u32[]{:S(2)}, u32[]{:S(2)}) collective-permute-start(bf16[320,1024]{1,0:T(8,128)(2,1)S(1)} %shard_map.95.refs_2_), channel_id=1, source_target_pairs={{0,2},{2,0},{1,3},{3,1},{4,6},{6,4},{5,7},{7,5},{8,10},{10,8},{9,1... | collective-permute-start | bytes 1966088 | tf_op jit(solution)/shard_map/ppermute | solution.py:49
  54.6 17.6 %collective-permute-start = (bf16[320,1024]{1,0:T(8,128)(2,1)S(1)}, bf16[320,1024]{1,0:T(8,128)(2,1)S(1)}, u32[]{:S(2)}, u32[]{:S(2)}) collective-permute-start(bf16[320,1024]{1,0:T(8,128)(2,1)S(1)} %shard_map.95.refs_2_), channel_id=1, source_target_pairs={{0,1},{1,0},{2,3},{3,2},{4,5},{5,4},{6,7},{7,6},{8,9},{9,8},{10,11... | collective-permute-start | bytes 1966088 | tf_op jit(solution)/shard_map/ppermute | solution.py:45
  54.8 22.2 %copy-start.3 = (bf16[320,1024]{1,0:T(8,128)(2,1)}, bf16[320,1024]{1,0:T(8,128)(2,1)S(1)}, u32[]{:S(2)}) copy-start(bf16[320,1024]{1,0:T(8,128)(2,1)S(1)} %shard_map.96.refs_3_) | copy-start | bytes 1966084
  54.8 17.5 %collective-permute-start.1 = (bf16[320,1024]{1,0:T(8,128)(2,1)S(1)}, bf16[320,1024]{1,0:T(8,128)(2,1)S(1)}, u32[]{:S(2)}, u32[]{:S(2)}) collective-permute-start(bf16[320,1024]{1,0:T(8,128)(2,1)S(1)} %shard_map.96.refs_3_), channel_id=1, source_target_pairs={{0,1},{1,0},{2,3},{3,2},{4,5},{5,4},{6,7},{7,6},{8,9},{9,8},{10,11... | collective-permute-start | bytes 1966088 | tf_op jit(solution)/shard_map/ppermute | solution.py:45
  55.4 26.4 %collective-permute-start.2 = (bf16[320,1024]{1,0:T(8,128)(2,1)S(1)}, bf16[320,1024]{1,0:T(8,128)(2,1)S(1)}, u32[]{:S(2)}, u32[]{:S(2)}) collective-permute-start(bf16[320,1024]{1,0:T(8,128)(2,1)S(1)} %shard_map.96.refs_3_), channel_id=1, source_target_pairs={{0,2},{2,0},{1,3},{3,1},{4,6},{6,4},{5,7},{7,5},{8,10},{10,8},{9,1... | collective-permute-start | bytes 1966088 | tf_op jit(solution)/shard_map/ppermute | solution.py:49
  71.5 5.9 %copy-start = (bf16[320,1024]{1,0:T(8,128)(2,1)}, bf16[320,1024]{1,0:T(8,128)(2,1)S(1)}, u32[]{:S(2)}) copy-start(bf16[320,1024]{1,0:T(8,128)(2,1)S(1)} %collective-permute-done.3.refs_4_.refs_8_) | copy-start | bytes 1966084
  71.6 5.5 %collective-permute-start.4 = (bf16[80,1024]{1,0:T(8,128)(2,1)S(1)}, bf16[80,1024]{1,0:T(8,128)(2,1)S(1)}, u32[]{:S(2)}, u32[]{:S(2)}) collective-permute-start(bf16[80,1024]{1,0:T(8,128)(2,1)S(1)} %get-tuple-element.52), channel_id=1, source_target_pairs={{0,1},{1,0},{2,3},{3,2},{4,5},{5,4},{6,7},{7,6},{8,9},{9,8},{10,11... | collective-permute-start | bytes 491528 | tf_op jit(solution)/shard_map/ppermute | solution.py:45
  71.7 5.7 %collective-permute-start.5 = (bf16[80,1024]{1,0:T(8,128)(2,1)S(1)}, bf16[80,1024]{1,0:T(8,128)(2,1)S(1)}, u32[]{:S(2)}, u32[]{:S(2)}) collective-permute-start(bf16[80,1024]{1,0:T(8,128)(2,1)S(1)} %get-tuple-element.51), channel_id=1, source_target_pairs={{0,1},{1,0},{2,3},{3,2},{4,5},{5,4},{6,7},{7,6},{8,9},{9,8},{10,11... | collective-permute-start | bytes 491528 | tf_op jit(solution)/shard_map/ppermute | solution.py:45
  72.2 4.8 %copy-start.6 = (bf16[320,1024]{1,0:T(8,128)(2,1)}, bf16[320,1024]{1,0:T(8,128)(2,1)S(1)}, u32[]{:S(2)}) copy-start(bf16[320,1024]{1,0:T(8,128)(2,1)S(1)} %collective-permute-done.refs_0_) | copy-start | bytes 1966084
  72.2 5.3 %collective-permute-start.6 = (bf16[80,1024]{1,0:T(8,128)(2,1)S(1)}, bf16[80,1024]{1,0:T(8,128)(2,1)S(1)}, u32[]{:S(2)}, u32[]{:S(2)}) collective-permute-start(bf16[80,1024]{1,0:T(8,128)(2,1)S(1)} %get-tuple-element.50), channel_id=1, source_target_pairs={{0,1},{1,0},{2,3},{3,2},{4,5},{5,4},{6,7},{7,6},{8,9},{9,8},{10,11... | collective-permute-start | bytes 491528 | tf_op jit(solution)/shard_map/ppermute | solution.py:45
  72.3 4.7 %copy-start.7 = (bf16[320,1024]{1,0:T(8,128)(2,1)}, bf16[320,1024]{1,0:T(8,128)(2,1)S(1)}, u32[]{:S(2)}) copy-start(bf16[320,1024]{1,0:T(8,128)(2,1)S(1)} %collective-permute-done.1.refs_1_) | copy-start | bytes 1966084
  72.3 5.2 %collective-permute-start.7 = (bf16[80,1024]{1,0:T(8,128)(2,1)S(1)}, bf16[80,1024]{1,0:T(8,128)(2,1)S(1)}, u32[]{:S(2)}, u32[]{:S(2)}) collective-permute-start(bf16[80,1024]{1,0:T(8,128)(2,1)S(1)} %get-tuple-element.49), channel_id=1, source_target_pairs={{0,1},{1,0},{2,3},{3,2},{4,5},{5,4},{6,7},{7,6},{8,9},{9,8},{10,11... | collective-permute-start | bytes 491528 | tf_op jit(solution)/shard_map/ppermute | solution.py:45
  77.0 2.7 %copy-start.20 = (bf16[640,1024]{1,0:T(8,128)(2,1)}, bf16[640,1024]{1,0:T(8,128)(2,1)S(1)}, u32[]{:S(2)}) copy-start(bf16[640,1024]{1,0:T(8,128)(2,1)S(1)} %get-tuple-element.37.refs_14_) | copy-start | bytes 3932164
  77.0 2.7 %copy-start.21 = (bf16[640,1024]{1,0:T(8,128)(2,1)}, bf16[640,1024]{1,0:T(8,128)(2,1)S(1)}, u32[]{:S(2)}) copy-start(bf16[640,1024]{1,0:T(8,128)(2,1)S(1)} %get-tuple-element.40.refs_17_) | copy-start | bytes 3932164
  77.1 2.7 %copy-start.8 = (bf16[80,1024]{1,0:T(8,128)(2,1)}, bf16[80,1024]{1,0:T(8,128)(2,1)S(1)}, u32[]{:S(2)}) copy-start(bf16[80,1024]{1,0:T(8,128)(2,1)S(1)} %collective-permute-done.4.refs_0_.refs_4_) | copy-start | bytes 491524
  77.1 4.8 %collective-permute-start.10 = (bf16[320,1024]{1,0:T(8,128)(2,1)S(1)}, bf16[320,1024]{1,0:T(8,128)(2,1)S(1)}, u32[]{:S(2)}, u32[]{:S(2)}) collective-permute-start(bf16[320,1024]{1,0:T(8,128)(2,1)S(1)} %get-tuple-element.27), channel_id=1, source_target_pairs={{0,1},{1,0},{2,3},{3,2},{4,5},{5,4},{6,7},{7,6},{8,9},{9,8},{10,11... | collective-permute-start | bytes 1966088 | tf_op jit(solution)/shard_map/ppermute | solution.py:45
  77.4 2.3 %copy-start.9 = (bf16[80,1024]{1,0:T(8,128)(2,1)}, bf16[80,1024]{1,0:T(8,128)(2,1)S(1)}, u32[]{:S(2)}) copy-start(bf16[80,1024]{1,0:T(8,128)(2,1)S(1)} %collective-permute-done.5.refs_1_.refs_5_) | copy-start | bytes 491524
  77.4 2.3 %copy-start.10 = (bf16[80,1024]{1,0:T(8,128)(2,1)}, bf16[80,1024]{1,0:T(8,128)(2,1)S(1)}, u32[]{:S(2)}) copy-start(bf16[80,1024]{1,0:T(8,128)(2,1)S(1)} %collective-permute-done.6.refs_2_.refs_6_) | copy-start | bytes 491524
  77.5 2.3 %copy-start.11 = (bf16[80,1024]{1,0:T(8,128)(2,1)}, bf16[80,1024]{1,0:T(8,128)(2,1)S(1)}, u32[]{:S(2)}) copy-start(bf16[80,1024]{1,0:T(8,128)(2,1)S(1)} %collective-permute-done.7.refs_3_.refs_7_) | copy-start | bytes 491524
  79.8 2.1 %copy-start.16 = (bf16[320,1024]{1,0:T(8,128)(2,1)}, bf16[320,1024]{1,0:T(8,128)(2,1)S(1)}, u32[]{:S(2)}) copy-start(bf16[320,1024]{1,0:T(8,128)(2,1)S(1)} %get-tuple-element.38.refs_15_) | copy-start | bytes 1966084
  79.8 2.1 %copy-start.17 = (bf16[320,1024]{1,0:T(8,128)(2,1)}, bf16[320,1024]{1,0:T(8,128)(2,1)S(1)}, u32[]{:S(2)}) copy-start(bf16[320,1024]{1,0:T(8,128)(2,1)S(1)} %get-tuple-element.41.refs_18_) | copy-start | bytes 1966084
  79.8 1.5 %collective-permute-start.9 = (bf16[80,1024]{1,0:T(8,128)(2,1)S(1)}, bf16[80,1024]{1,0:T(8,128)(2,1)S(1)}, u32[]{:S(2)}, u32[]{:S(2)}) collective-permute-start(bf16[80,1024]{1,0:T(8,128)(2,1)S(1)} %get-tuple-element.56), channel_id=1, source_target_pairs={{0,1},{1,0},{2,3},{3,2},{4,5},{5,4},{6,7},{7,6},{8,9},{9,8},{10,11... | collective-permute-start | bytes 491528 | tf_op jit(solution)/shard_map/ppermute | solution.py:45
  80.3 1.4 %collective-permute-start.8 = (bf16[80,1024]{1,0:T(8,128)(2,1)S(1)}, bf16[80,1024]{1,0:T(8,128)(2,1)S(1)}, u32[]{:S(2)}, u32[]{:S(2)}) collective-permute-start(bf16[80,1024]{1,0:T(8,128)(2,1)S(1)} %get-tuple-element.55), channel_id=1, source_target_pairs={{0,1},{1,0},{2,3},{3,2},{4,5},{5,4},{6,7},{7,6},{8,9},{9,8},{10,11... | collective-permute-start | bytes 491528 | tf_op jit(solution)/shard_map/ppermute | solution.py:45
  81.8 4.5 %copy-start.1 = (bf16[320,1024]{1,0:T(8,128)(2,1)}, bf16[320,1024]{1,0:T(8,128)(2,1)S(1)}, u32[]{:S(2)}) copy-start(bf16[320,1024]{1,0:T(8,128)(2,1)S(1)} %collective-permute-done.2.refs_4_.refs_13_) | copy-start | bytes 1966084
  81.9 1.8 %collective-permute-start.11 = (bf16[80,1024]{1,0:T(8,128)(2,1)S(1)}, bf16[80,1024]{1,0:T(8,128)(2,1)S(1)}, u32[]{:S(2)}, u32[]{:S(2)}) collective-permute-start(bf16[80,1024]{1,0:T(8,128)(2,1)S(1)} %get-tuple-element.48), channel_id=1, source_target_pairs={{0,1},{1,0},{2,3},{3,2},{4,5},{5,4},{6,7},{7,6},{8,9},{9,8},{10,11... | collective-permute-start | bytes 491528 | tf_op jit(solution)/shard_map/ppermute | solution.py:45
  82.2 1.5 %collective-permute-start.12 = (bf16[80,1024]{1,0:T(8,128)(2,1)S(1)}, bf16[80,1024]{1,0:T(8,128)(2,1)S(1)}, u32[]{:S(2)}, u32[]{:S(2)}) collective-permute-start(bf16[80,1024]{1,0:T(8,128)(2,1)S(1)} %get-tuple-element.47), channel_id=1, source_target_pairs={{0,1},{1,0},{2,3},{3,2},{4,5},{5,4},{6,7},{7,6},{8,9},{9,8},{10,11... | collective-permute-start | bytes 491528 | tf_op jit(solution)/shard_map/ppermute | solution.py:45
  82.5 1.4 %collective-permute-start.13 = (bf16[80,1024]{1,0:T(8,128)(2,1)S(1)}, bf16[80,1024]{1,0:T(8,128)(2,1)S(1)}, u32[]{:S(2)}, u32[]{:S(2)}) collective-permute-start(bf16[80,1024]{1,0:T(8,128)(2,1)S(1)} %get-tuple-element.46), channel_id=1, source_target_pairs={{0,1},{1,0},{2,3},{3,2},{4,5},{5,4},{6,7},{7,6},{8,9},{9,8},{10,11... | collective-permute-start | bytes 491528 | tf_op jit(solution)/shard_map/ppermute | solution.py:45
  82.7 1.4 %collective-permute-start.14 = (bf16[80,1024]{1,0:T(8,128)(2,1)S(1)}, bf16[80,1024]{1,0:T(8,128)(2,1)S(1)}, u32[]{:S(2)}, u32[]{:S(2)}) collective-permute-start(bf16[80,1024]{1,0:T(8,128)(2,1)S(1)} %get-tuple-element.45), channel_id=1, source_target_pairs={{0,1},{1,0},{2,3},{3,2},{4,5},{5,4},{6,7},{7,6},{8,9},{9,8},{10,11... | collective-permute-start | bytes 491528 | tf_op jit(solution)/shard_map/ppermute | solution.py:45
  83.0 9.8 %collective-permute-start.15 = (bf16[160,1024]{1,0:T(8,128)(2,1)S(1)}, bf16[160,1024]{1,0:T(8,128)(2,1)S(1)}, u32[]{:S(2)}, u32[]{:S(2)}) collective-permute-start(bf16[160,1024]{1,0:T(8,128)(2,1)S(1)} %add_convert_fusion.1), channel_id=1, source_target_pairs={{0,2},{2,0},{1,3},{3,1},{4,6},{6,4},{5,7},{7,5},{8,10},{10,8},{9,1... | collective-permute-start | bytes 983048 | tf_op jit(solution)/shard_map/ppermute | solution.py:49
  83.7 2.7 %copy-start.12 = (bf16[80,1024]{1,0:T(8,128)(2,1)}, bf16[80,1024]{1,0:T(8,128)(2,1)S(1)}, u32[]{:S(2)}) copy-start(bf16[80,1024]{1,0:T(8,128)(2,1)S(1)} %collective-permute-done.11.refs_0_.refs_9_) | copy-start | bytes 491524
  83.7 2.7 %copy-start.13 = (bf16[80,1024]{1,0:T(8,128)(2,1)}, bf16[80,1024]{1,0:T(8,128)(2,1)S(1)}, u32[]{:S(2)}) copy-start(bf16[80,1024]{1,0:T(8,128)(2,1)S(1)} %collective-permute-done.12.refs_1_.refs_10_) | copy-start | bytes 491524
  83.9 2.5 %copy-start.14 = (bf16[80,1024]{1,0:T(8,128)(2,1)}, bf16[80,1024]{1,0:T(8,128)(2,1)S(1)}, u32[]{:S(2)}) copy-start(bf16[80,1024]{1,0:T(8,128)(2,1)S(1)} %collective-permute-done.13.refs_2_.refs_11_) | copy-start | bytes 491524
  84.1 2.3 %copy-start.15 = (bf16[80,1024]{1,0:T(8,128)(2,1)}, bf16[80,1024]{1,0:T(8,128)(2,1)S(1)}, u32[]{:S(2)}) copy-start(bf16[80,1024]{1,0:T(8,128)(2,1)S(1)} %collective-permute-done.14.refs_3_.refs_12_) | copy-start | bytes 491524
  86.4 7.6 %copy-start.18 = (bf16[320,1024]{1,0:T(8,128)(2,1)}, bf16[320,1024]{1,0:T(8,128)(2,1)S(1)}, u32[]{:S(2)}) copy-start(bf16[320,1024]{1,0:T(8,128)(2,1)S(1)} %get-tuple-element.39.refs_16_) | copy-start | bytes 1966084
  86.4 7.6 %copy-start.19 = (bf16[320,1024]{1,0:T(8,128)(2,1)}, bf16[320,1024]{1,0:T(8,128)(2,1)S(1)}, u32[]{:S(2)}) copy-start(bf16[320,1024]{1,0:T(8,128)(2,1)S(1)} %get-tuple-element.42.refs_19_) | copy-start | bytes 1966084
  86.5 6.4 %collective-permute-start.17 = (bf16[80,1024]{1,0:T(8,128)(2,1)S(1)}, bf16[80,1024]{1,0:T(8,128)(2,1)S(1)}, u32[]{:S(2)}, u32[]{:S(2)}) collective-permute-start(bf16[80,1024]{1,0:T(8,128)(2,1)S(1)} %get-tuple-element.54), channel_id=1, source_target_pairs={{0,1},{1,0},{2,3},{3,2},{4,5},{5,4},{6,7},{7,6},{8,9},{9,8},{10,11... | collective-permute-start | bytes 491528 | tf_op jit(solution)/shard_map/ppermute | solution.py:45
  86.8 6.0 %collective-permute-start.16 = (bf16[80,1024]{1,0:T(8,128)(2,1)S(1)}, bf16[80,1024]{1,0:T(8,128)(2,1)S(1)}, u32[]{:S(2)}, u32[]{:S(2)}) collective-permute-start(bf16[80,1024]{1,0:T(8,128)(2,1)S(1)} %get-tuple-element.53), channel_id=1, source_target_pairs={{0,1},{1,0},{2,3},{3,2},{4,5},{5,4},{6,7},{7,6},{8,9},{9,8},{10,11... | collective-permute-start | bytes 491528 | tf_op jit(solution)/shard_map/ppermute | solution.py:45
  93.0 9.1 %collective-permute-start.18 = (bf16[160,1024]{1,0:T(8,128)(2,1)S(1)}, bf16[160,1024]{1,0:T(8,128)(2,1)S(1)}, u32[]{:S(2)}, u32[]{:S(2)}) collective-permute-start(bf16[160,1024]{1,0:T(8,128)(2,1)S(1)} %add_convert_fusion), channel_id=1, source_target_pairs={{0,2},{2,0},{1,3},{3,1},{4,6},{6,4},{5,7},{7,5},{8,10},{10,8},{9,1... | collective-permute-start | bytes 983048 | tf_op jit(solution)/shard_map/ppermute | solution.py:49
  102.1 8.7 %copy-start.22 = (s32[128,2]{0,1:T(2,128)S(1)}, s32[128,2]{0,1:T(2,128)}, u32[]{:S(2)}) copy-start(s32[128,2]{0,1:T(2,128)} %param.9) | copy-start | bytes 3076
  102.1 8.8 %copy-start.23 = (s32[128,2]{0,1:T(2,128)S(1)}, s32[128,2]{0,1:T(2,128)}, u32[]{:S(2)}) copy-start(s32[128,2]{0,1:T(2,128)} %param.10) | copy-start | bytes 3076
  103.1 28.2 %all-to-all-start.1 = ((bf16[64,40,128]{2,1,0:T(8,128)(2,1)}), bf16[64,40,128]{2,1,0:T(8,128)(2,1)S(1)}, u32[]{:S(2)}, u32[]{:S(2)}) async-start(bf16[64,40,128]{2,1,0:T(8,128)(2,1)} %bitcast.9), calls=%async_computation.1 | async-start | bytes 1310720 | tf_op jit(solution)/shard_map/all_to_all | solution.py:191

commit v5 on v4

--- a/solution.py
+++ b/solution.py
@@ -15,8 +15,8 @@
 TO_CORE = ((0, 1), (1, 0), (2, 3), (3, 2))
 TO_CHIP = ((0, 2), (2, 0), (1, 3), (3, 1))
 SPLIT = (32, 32)
-FAR = 4
-BACK = 2
+FAR = (4, 1)
+BACK = (2, 2)
 SMALL = 16 * 2**20
 LARGE = 56 * 2**20
 EXPERT = 24 * 2**20
@@ -177,14 +177,29 @@
     rows = near[pl.ds(0, n), :] + back[pl.ds(0, n), :].astype(F32) + chip[...].astype(F32)
     packed[...] = pack(rows, n // capacity).reshape(-1, LANES).astype(BF)
     rest = pl.ds(n, near.shape[0] - n)
-    base[...] = near[rest, :] + back[rest, :].astype(F32)
-
-
-def last_return_kernel(capacity, packed, base, chip, out):
+    rows = near[rest, :] + back[rest, :].astype(F32)
+    base[...] = pack(rows, rows.shape[0] // capacity).reshape(-1, LANES)
+
+
+def last_return_kernel(packed, base, chip, out):
     done = packed.shape[0]
     out[pl.ds(0, done), :] = packed[...]
-    rows = base[...] + chip[...].astype(F32)
-    out[pl.ds(done, out.shape[0] - done), :] = pack(rows, rows.shape[0] // capacity).reshape(-1, LANES).astype(BF)
+    out[pl.ds(done, out.shape[0] - done), :] = (base[...] + chip[...].astype(F32)).astype(BF)
+
+
+def sum_kernel(capacity, near, *refs):
+    backs, sent = refs[:-1], refs[-1]
+    n = near.shape[0]
+    rows = near[...] + jnp.concatenate([v[...] for v in backs], axis=0).astype(F32)
+    sent[...] = pack(rows, n // capacity).reshape(-1, LANES).astype(BF)
+
+
+def combine_kernel(experts, capacity, arrived, ids, slots, out):
+    columns = experts * capacity
+    rows = arrived[...].astype(F32).reshape(columns, -1).astype(BF)
+    first, second = places(ids[...], slots[...], capacity, columns)
+    place = jnp.where(first | second, 1.0, 0.0).astype(BF)
+    out[...] = dot(place, rows, ((0,), (0,))).astype(BF)
 
 
 def exchange(blocks, experts):
@@ -230,30 +245,35 @@
         if i:
             chip, sent, back_own = barrier((chip, sent, back_own))
             sums.append(to_chip(sent))
-        blocks = [core_pieces(chip, FAR), [chip]]
+        blocks = [core_pieces(chip, FAR[i]), [chip]]
         active, grad_hidden, away, near = expert_step(blocks, w_in, w_out)
         made.append((blocks, active, grad_hidden))
-        if sums:
-            near, sums[-1] = barrier((near, sums[-1]))
-        sent = (near + jnp.concatenate(core_pieces(away, BACK), axis=0).astype(F32)).astype(BF)
-    sums.append(to_chip(sent))
+        backs = core_pieces(away, BACK[i])
+        if not sums:
+            sent = (near + jnp.concatenate(backs, axis=0).astype(F32)).astype(BF)
     per = width // LANES
     n = sums[0].shape[0]
+    rest = columns - n
+    sent = kernel_call(
+        functools.partial(sum_kernel, capacity), shape(rest * per, LANES), SMALL, 10**6, 10**6
+    )(near, *backs)
+    sent, sums[0] = barrier((sent, sums[0]))
+    sums.append(to_chip(sent))
     packed, base = kernel_call(
         functools.partial(first_return_kernel, capacity),
-        [shape(n * per, LANES), shape(columns - n, width, F32)],
+        [shape(n * per, LANES), shape(rest * per, LANES, F32)],
         SMALL,
         10**6,
         10**6,
     )(near_own, back_own, sums[0])
     returned = kernel_call(
-        functools.partial(last_return_kernel, capacity), shape(columns * per, LANES), SMALL, 10**6, 10**6
+        last_return_kernel, shape(columns * per, LANES), SMALL, 10**6, 10**6
     )(packed, base, sums[1])
-    arrived = exchange(returned, experts).reshape(columns, width)
+    arrived = exchange(returned, experts)
     grad_in, grad_out = weight_grads(made, *w_in.shape)
-    first, second = places(ids, slots, capacity, columns)
-    place = (first | second).astype(BF)
-    token_grad = dot(place, arrived, ((0,), (0,))).astype(BF)
+    token_grad = kernel_call(
+        functools.partial(combine_kernel, experts, capacity), shape(token_count, width), SMALL, 10**6, 10**6
+    )(arrived, ids, slots)
     return token_grad, grad_in[None], grad_out[None]
 
 

time: 133 us -> 133 us (level)
  Pallas kernels: 26.1 us -> 27.6 us
    ppermute x4, waiting for transfers between devices: 28.6 us -> 26.6 us  [to_chip(): return lax.ppermute(rows, 'replica', TO_CHIP)]
    ppermute x15 -> x12, waiting for transfers between devices: 1.73 us -> 3.61 us  [to_core(): return lax.ppermute(rows, 'replica', TO_CORE)]
    ppermute x15 -> x12, starting transfers between devices: 4.37 us -> 3.58 us  [to_core(): return lax.ppermute(rows, 'replica', TO_CORE)]
  transfers between devices with their start and end apart: 20 -> 17, of which waited for: 8 -> 9; matrix products, arithmetic and copies ran while one was open for 0% -> 0% of each run, Pallas kernels for 17% -> 17%
where the time goes in v5:
time: 133 us; the launch traced here: 132 us
  blocking collectives  50 us (38%)
  waiting for transfers between devices  38.3 us (29%)
  Pallas kernels  27.6 us (21%)
  starting transfers between devices  15.1 us (11%)
    all_to_all x1, blocking collectives, exchange(): lax.all_to_all(blocks.reshape(experts, -1, LANES), 'expert', split_axis=0...  50 us
    ppermute x4, waiting for transfers between devices, to_chip(): return lax.ppermute(rows, 'replica', TO_CHIP)  26.6 us
    pallas_call x1, Pallas kernels, weight_grads(): kernel_call(functools.partial(weight_grads_kernel, groups), [shape(width,...  12.7 us
    pallas_call x3, Pallas kernels, expert_step(): kernel_call(functools.partial(expert_kernel, counts), [shape(rows, units)...  8.71 us
    all_to_all x1, waiting for transfers between devices, exchange(): lax.all_to_all(blocks.reshape(experts, -1, LANES), 'expert', split_axis=0...  8.13 us
    all_to_all x1, starting transfers between devices, exchange(): lax.all_to_all(blocks.reshape(experts, -1, LANES), 'expert', split_axis=0...  8.09 us
    ppermute x12, waiting for transfers between devices, to_core(): return lax.ppermute(rows, 'replica', TO_CORE)  3.61 us
    ppermute x12, starting transfers between devices, to_core(): return lax.ppermute(rows, 'replica', TO_CORE)  3.58 us
  transfers between devices with their start and end apart: 17, of which 9 were waited for; matrix products, arithmetic and copies ran while one was open for 0% of the time, Pallas kernels for 17%

profile of v5, /device:TPU:32, one launch (start us, length us, event | category | flops | bytes accessed | tf_op | source)
XLA Modules:
  0.0 132.3 jit_solution(2732841720454899901)
XLA Ops:
  0.6 2.9 %shard_map.94 = bf16[5120,128]{1,0:T(8,128)(2,1)} custom-call(bf16[128,1024]{1,0:T(8,128)(2,1)} %tokens.1, bf16[128,1024]{1,0:T(8,128)(2,1)} %upstream.1, s32[2,128]{1,0:T(2,128)} %bitcast.14, s32[2,128]{1,0:T(2,128)} %bitcast.16, f32[2,128]{1,0:T(2,128)} %bitcast.25), custom_call_target="tpu_custom_call" | custom-call | flops 1 | bytes 1 | tf_op jit(solution)/shard_map/pallas_call | solution.py:217
  3.5 50.0 %all_to_all.10 = bf16[64,80,128]{2,1,0:T(8,128)(2,1)S(1)} all-to-all(bf16[64,80,128]{2,1,0:T(8,128)(2,1)} %bitcast.24), channel_id=1, replica_groups=mesh['expert'=64,'replica'=4] {'expert'}, dimensions={0} | all-to-all | bytes 2621440 | tf_op jit(solution)/shard_map/all_to_all | solution.py:206
  53.5 0.3 shard_map.95.refs_2_
  53.8 0.0 copy-start.1
  53.8 0.0 copy-start.5
  53.8 0.8 collective-permute-start.3
  54.6 0.0 collective-permute-start
  54.6 0.3 shard_map.96.refs_3_
  54.8 0.0 copy-start.2
  54.8 0.6 collective-permute-start.1
  55.4 1.3 %collective-permute-start.2 = (bf16[320,1024]{1,0:T(8,128)(2,1)S(1)}, bf16[320,1024]{1,0:T(8,128)(2,1)S(1)}, u32[]{:S(2)}, u32[]{:S(2)}) collective-permute-start(bf16[320,1024]{1,0:T(8,128)(2,1)S(1)} %shard_map.96.refs_3_), channel_id=1, source_target_pairs={{0,2},{2,0},{1,3},{3,1},{4,6},{6,4},{5,7},{7,5},{8,10},{10,8},{9,1... | collective-permute-start | bytes 1966088 | tf_op jit(solution)/shard_map/ppermute | solution.py:49
  56.8 14.8 %collective-permute-done.3.refs_4_.refs_8_ = bf16[320,1024]{1,0:T(8,128)(2,1)S(1)} collective-permute-done((bf16[320,1024]{1,0:T(8,128)(2,1)S(1)}, bf16[320,1024]{1,0:T(8,128)(2,1)S(1)}, u32[]{:S(2)}, u32[]{:S(2)}) %collective-permute-start.3) | collective-permute-done | bytes 655392 | tf_op jit(solution)/shard_map/ppermute | solution.py:49
  71.6 0.1 collective-permute-start.4
  71.7 0.5 collective-permute-start.5
  72.2 0.0 collective-permute-done.refs_0_
  72.2 0.1 collective-permute-start.6
  72.3 0.0 collective-permute-done.1.refs_1_
  72.3 0.4 collective-permute-start.7
  72.7 0.0 copy-done.1
  72.7 0.0 copy-done.6
  72.7 0.0 copy-done.5
  72.7 4.3 %shard_map.97 = (bf16[640,1024]{1,0:T(8,128)(2,1)S(1)}, bf16[640,1024]{1,0:T(8,128)(2,1)S(1)}, bf16[320,1024]{1,0:T(8,128)(2,1)S(1)}, f32[320,1024]{1,0:T(8,128)S(1)}) custom-call(bf16[320,1024]{1,0:T(8,128)(2,1)S(1)} %collective-permute-done.refs_0_, bf16[320,1024]{1,0:T(8,128)(2,1)S(1)} %collective-permute-done.1.refs_1_, ...), custom_call_target="tpu_custom_call" | custom-call | flops 4026531840 | bytes 13369344 | tf_op jit(solution)/shard_map/pallas_call | solution.py:125
  77.0 0.0 copy-done.2
  77.0 0.0 copy-done.7
  77.0 0.0 copy-done.8
  77.0 0.0 copy-start.19
  77.0 0.0 copy-start.20
  77.0 0.0 collective-permute-done.4.refs_0_.refs_4_
  77.1 0.0 copy-start.11
  77.1 0.4 collective-permute-start.10
  77.4 0.0 collective-permute-done.5.refs_1_.refs_5_
  77.4 0.0 collective-permute-done.6.refs_2_.refs_6_
  77.4 0.0 copy-start.13
  77.5 0.0 collective-permute-done.7.refs_3_.refs_7_
  77.5 2.2 %shard_map.98 = (bf16[320,1024]{1,0:T(8,128)(2,1)S(1)}, bf16[320,1024]{1,0:T(8,128)(2,1)S(1)}, bf16[160,1024]{1,0:T(8,128)(2,1)S(1)}, f32[160,1024]{1,0:T(8,128)S(1)}) custom-call(bf16[80,1024]{1,0:T(8,128)(2,1)S(1)} %collective-permute-done.4.refs_0_.refs_4_, bf16[80,1024]{1,0:T(8,128)(2,1)S(1)} %collective-permute-done.5.refs_1_.refs_5_, ...), custom_call_target="tpu_custom_call" | custom-call | flops 2013265920 | bytes 8781824 | tf_op jit(solution)/shard_map/pallas_call | solution.py:125
  79.8 0.5 collective-permute-start.9
  80.3 0.1 collective-permute-start.8
  80.4 0.9 collective-permute-done.9
  81.3 0.4 collective-permute-done.8
  81.7 0.1 add_convert_fusion
  81.8 0.0 collective-permute-done.2.refs_1_.refs_10_
  81.8 0.0 copy-start.9
  81.8 0.0 collective-permute-done.10.back
  81.8 0.3 collective-permute-start.11
  82.2 0.7 collective-permute-start.14
  82.8 1.2 collective-permute-done.11.refs_0_.refs_9_
  84.0 2.2 %shard_map.99 = (bf16[320,1024]{1,0:T(8,128)(2,1)S(1)}, bf16[320,1024]{1,0:T(8,128)(2,1)S(1)}, bf16[160,1024]{1,0:T(8,128)(2,1)S(1)}, f32[160,1024]{1,0:T(8,128)S(1)}) custom-call(bf16[320,1024]{1,0:T(8,128)(2,1)S(1)} %collective-permute-done.11.refs_0_.refs_9_, bf16[320,1024]{1,0:T(8,128)(2,1)S(1)} %collective-permute-done.2.refs_1_.refs_10_, ...), custom_call_target="tpu_custom_call" | custom-call | flops 2013265920 | bytes 8781824 | tf_op jit(solution)/shard_map/pallas_call | solution.py:125
  86.3 0.3 collective-permute-start.12
  86.7 0.3 collective-permute-start.13
  86.9 0.9 collective-permute-done.12.refs_0_
  87.8 0.2 collective-permute-done.13.refs_1_
  88.1 0.2 shard_map.100
  88.2 3.8 %collective-permute-done.14.chip = bf16[160,1024]{1,0:T(8,128)(2,1)S(1)} collective-permute-done((bf16[160,1024]{1,0:T(8,128)(2,1)S(1)}, bf16[160,1024]{1,0:T(8,128)(2,1)S(1)}, u32[]{:S(2)}, u32[]{:S(2)}) %collective-permute-start.14) | collective-permute-done | bytes 327712 | tf_op jit(solution)/shard_map/ppermute | solution.py:49
  92.0 0.7 collective-permute-start.15
  92.7 0.4 shard_map.101
  93.1 8.0 %collective-permute-done.15.chip = bf16[1280,128]{1,0:T(8,128)(2,1)S(1)} collective-permute-done((bf16[1280,128]{1,0:T(8,128)(2,1)S(1)}, bf16[1280,128]{1,0:T(8,128)(2,1)S(1)}, u32[]{:S(2)}, u32[]{:S(2)}) %collective-permute-start.15) | collective-permute-done | bytes 327712 | tf_op jit(solution)/shard_map/ppermute | solution.py:49
  101.1 0.9 shard_map.102
  102.0 8.1 %all-to-all-start.1 = ((bf16[64,40,128]{2,1,0:T(8,128)(2,1)}), bf16[64,40,128]{2,1,0:T(8,128)(2,1)S(1)}, u32[]{:S(2)}, u32[]{:S(2)}) async-start(bf16[64,40,128]{2,1,0:T(8,128)(2,1)} %bitcast.7), calls=%async_computation.1 | async-start | bytes 1310720 | tf_op jit(solution)/shard_map/all_to_all | solution.py:206
  110.1 0.0 copy-start.3
  110.2 0.0 copy-start.4
  110.2 12.7 %shard_map.104 = (bf16[1024,1024]{1,0:T(8,128)(2,1)}, bf16[1024,1024]{1,0:T(8,128)(2,1)}) custom-call(bf16[320,1024]{1,0:T(8,128)(2,1)} %copy-done.7, bf16[320,1024]{1,0:T(8,128)(2,1)} %copy-done.8, bf16[320,1024]{1,0:T(8,128)(2,1)} %copy-done.1, bf16[320,1024]{1,0:T(8,128)(2,1)} %copy-done.2, bf16[80,1024]{1,0:T(8,128)(2,1)} %copy-done.11, ...), custom_call_target="tpu_custom_call" | custom-call | flops 5368709120 | bytes 14680064 | tf_op jit(solution)/shard_map/pallas_call | solution.py:158
  122.9 8.1 %all-to-all-done.1 = bf16[64,40,128]{2,1,0:T(8,128)(2,1)S(1)} async-done(((bf16[64,40,128]{2,1,0:T(8,128)(2,1)}), bf16[64,40,128]{2,1,0:T(8,128)(2,1)S(1)}, u32[]{:S(2)}, u32[]{:S(2)}) %all-to-all-start.1) | async-done | bytes 655392 | tf_op jit(solution)/shard_map/all_to_all | solution.py:206
  131.0 0.0 copy-done.4
  131.0 1.3 shard_map.103
  (28 shorter events, 0.1 us)
Async XLA Ops:
  53.5 19.2 %copy-start.6 = (bf16[1,1024,1024]{2,1,0:T(8,128)(2,1)S(1)}, bf16[1,1024,1024]{2,1,0:T(8,128)(2,1)}, u32[]{:S(2)}) copy-start(bf16[1,1024,1024]{2,1,0:T(8,128)(2,1)} %param.13) | copy-start | bytes 6291460
  53.8 18.9 %copy-start.1 = (bf16[320,1024]{1,0:T(8,128)(2,1)}, bf16[320,1024]{1,0:T(8,128)(2,1)S(1)}, u32[]{:S(2)}) copy-start(bf16[320,1024]{1,0:T(8,128)(2,1)S(1)} %shard_map.95.refs_2_) | copy-start | bytes 1966084
  53.8 18.9 %copy-start.5 = (bf16[1,1024,1024]{2,1,0:T(8,128)(2,1)S(1)}, bf16[1,1024,1024]{2,1,0:T(8,128)(2,1)}, u32[]{:S(2)}) copy-start(bf16[1,1024,1024]{2,1,0:T(8,128)(2,1)} %param.12) | copy-start | bytes 6291460
  53.8 17.8 %collective-permute-start.3 = (bf16[320,1024]{1,0:T(8,128)(2,1)S(1)}, bf16[320,1024]{1,0:T(8,128)(2,1)S(1)}, u32[]{:S(2)}, u32[]{:S(2)}) collective-permute-start(bf16[320,1024]{1,0:T(8,128)(2,1)S(1)} %shard_map.95.refs_2_), channel_id=1, source_target_pairs={{0,2},{2,0},{1,3},{3,1},{4,6},{6,4},{5,7},{7,5},{8,10},{10,8},{9,1... | collective-permute-start | bytes 1966088 | tf_op jit(solution)/shard_map/ppermute | solution.py:49
  54.6 17.6 %collective-permute-start = (bf16[320,1024]{1,0:T(8,128)(2,1)S(1)}, bf16[320,1024]{1,0:T(8,128)(2,1)S(1)}, u32[]{:S(2)}, u32[]{:S(2)}) collective-permute-start(bf16[320,1024]{1,0:T(8,128)(2,1)S(1)} %shard_map.95.refs_2_), channel_id=1, source_target_pairs={{0,1},{1,0},{2,3},{3,2},{4,5},{5,4},{6,7},{7,6},{8,9},{9,8},{10,11... | collective-permute-start | bytes 1966088 | tf_op jit(solution)/shard_map/ppermute | solution.py:45
  54.8 22.2 %copy-start.2 = (bf16[320,1024]{1,0:T(8,128)(2,1)}, bf16[320,1024]{1,0:T(8,128)(2,1)S(1)}, u32[]{:S(2)}) copy-start(bf16[320,1024]{1,0:T(8,128)(2,1)S(1)} %shard_map.96.refs_3_) | copy-start | bytes 1966084
  54.8 17.5 %collective-permute-start.1 = (bf16[320,1024]{1,0:T(8,128)(2,1)S(1)}, bf16[320,1024]{1,0:T(8,128)(2,1)S(1)}, u32[]{:S(2)}, u32[]{:S(2)}) collective-permute-start(bf16[320,1024]{1,0:T(8,128)(2,1)S(1)} %shard_map.96.refs_3_), channel_id=1, source_target_pairs={{0,1},{1,0},{2,3},{3,2},{4,5},{5,4},{6,7},{7,6},{8,9},{9,8},{10,11... | collective-permute-start | bytes 1966088 | tf_op jit(solution)/shard_map/ppermute | solution.py:45
  55.4 26.4 %collective-permute-start.2 = (bf16[320,1024]{1,0:T(8,128)(2,1)S(1)}, bf16[320,1024]{1,0:T(8,128)(2,1)S(1)}, u32[]{:S(2)}, u32[]{:S(2)}) collective-permute-start(bf16[320,1024]{1,0:T(8,128)(2,1)S(1)} %shard_map.96.refs_3_), channel_id=1, source_target_pairs={{0,2},{2,0},{1,3},{3,1},{4,6},{6,4},{5,7},{7,5},{8,10},{10,8},{9,1... | collective-permute-start | bytes 1966088 | tf_op jit(solution)/shard_map/ppermute | solution.py:49
  71.5 5.9 %copy-start = (bf16[320,1024]{1,0:T(8,128)(2,1)}, bf16[320,1024]{1,0:T(8,128)(2,1)S(1)}, u32[]{:S(2)}) copy-start(bf16[320,1024]{1,0:T(8,128)(2,1)S(1)} %collective-permute-done.3.refs_4_.refs_8_) | copy-start | bytes 1966084
  71.6 5.5 %collective-permute-start.4 = (bf16[80,1024]{1,0:T(8,128)(2,1)S(1)}, bf16[80,1024]{1,0:T(8,128)(2,1)S(1)}, u32[]{:S(2)}, u32[]{:S(2)}) collective-permute-start(bf16[80,1024]{1,0:T(8,128)(2,1)S(1)} %get-tuple-element.48), channel_id=1, source_target_pairs={{0,1},{1,0},{2,3},{3,2},{4,5},{5,4},{6,7},{7,6},{8,9},{9,8},{10,11... | collective-permute-start | bytes 491528 | tf_op jit(solution)/shard_map/ppermute | solution.py:45
  71.7 5.7 %collective-permute-start.5 = (bf16[80,1024]{1,0:T(8,128)(2,1)S(1)}, bf16[80,1024]{1,0:T(8,128)(2,1)S(1)}, u32[]{:S(2)}, u32[]{:S(2)}) collective-permute-start(bf16[80,1024]{1,0:T(8,128)(2,1)S(1)} %get-tuple-element.47), channel_id=1, source_target_pairs={{0,1},{1,0},{2,3},{3,2},{4,5},{5,4},{6,7},{7,6},{8,9},{9,8},{10,11... | collective-permute-start | bytes 491528 | tf_op jit(solution)/shard_map/ppermute | solution.py:45
  72.2 4.8 %copy-start.7 = (bf16[320,1024]{1,0:T(8,128)(2,1)}, bf16[320,1024]{1,0:T(8,128)(2,1)S(1)}, u32[]{:S(2)}) copy-start(bf16[320,1024]{1,0:T(8,128)(2,1)S(1)} %collective-permute-done.refs_0_) | copy-start | bytes 1966084
  72.2 5.3 %collective-permute-start.6 = (bf16[80,1024]{1,0:T(8,128)(2,1)S(1)}, bf16[80,1024]{1,0:T(8,128)(2,1)S(1)}, u32[]{:S(2)}, u32[]{:S(2)}) collective-permute-start(bf16[80,1024]{1,0:T(8,128)(2,1)S(1)} %get-tuple-element.46), channel_id=1, source_target_pairs={{0,1},{1,0},{2,3},{3,2},{4,5},{5,4},{6,7},{7,6},{8,9},{9,8},{10,11... | collective-permute-start | bytes 491528 | tf_op jit(solution)/shard_map/ppermute | solution.py:45
  72.3 4.7 %copy-start.8 = (bf16[320,1024]{1,0:T(8,128)(2,1)}, bf16[320,1024]{1,0:T(8,128)(2,1)S(1)}, u32[]{:S(2)}) copy-start(bf16[320,1024]{1,0:T(8,128)(2,1)S(1)} %collective-permute-done.1.refs_1_) | copy-start | bytes 1966084
  72.3 5.2 %collective-permute-start.7 = (bf16[80,1024]{1,0:T(8,128)(2,1)S(1)}, bf16[80,1024]{1,0:T(8,128)(2,1)S(1)}, u32[]{:S(2)}, u32[]{:S(2)}) collective-permute-start(bf16[80,1024]{1,0:T(8,128)(2,1)S(1)} %get-tuple-element.45), channel_id=1, source_target_pairs={{0,1},{1,0},{2,3},{3,2},{4,5},{5,4},{6,7},{7,6},{8,9},{9,8},{10,11... | collective-permute-start | bytes 491528 | tf_op jit(solution)/shard_map/ppermute | solution.py:45
  77.0 2.7 %copy-start.19 = (bf16[640,1024]{1,0:T(8,128)(2,1)}, bf16[640,1024]{1,0:T(8,128)(2,1)S(1)}, u32[]{:S(2)}) copy-start(bf16[640,1024]{1,0:T(8,128)(2,1)S(1)} %get-tuple-element.37.refs_11_) | copy-start | bytes 3932164
  77.0 2.7 %copy-start.20 = (bf16[640,1024]{1,0:T(8,128)(2,1)}, bf16[640,1024]{1,0:T(8,128)(2,1)S(1)}, u32[]{:S(2)}) copy-start(bf16[640,1024]{1,0:T(8,128)(2,1)S(1)} %get-tuple-element.40.refs_14_) | copy-start | bytes 3932164
  77.1 2.7 %copy-start.11 = (bf16[80,1024]{1,0:T(8,128)(2,1)}, bf16[80,1024]{1,0:T(8,128)(2,1)S(1)}, u32[]{:S(2)}) copy-start(bf16[80,1024]{1,0:T(8,128)(2,1)S(1)} %collective-permute-done.4.refs_0_.refs_4_) | copy-start | bytes 491524
  77.1 4.8 %collective-permute-start.10 = (bf16[320,1024]{1,0:T(8,128)(2,1)S(1)}, bf16[320,1024]{1,0:T(8,128)(2,1)S(1)}, u32[]{:S(2)}, u32[]{:S(2)}) collective-permute-start(bf16[320,1024]{1,0:T(8,128)(2,1)S(1)} %get-tuple-element.27), channel_id=1, source_target_pairs={{0,1},{1,0},{2,3},{3,2},{4,5},{5,4},{6,7},{7,6},{8,9},{9,8},{10,11... | collective-permute-start | bytes 1966088 | tf_op jit(solution)/shard_map/ppermute | solution.py:45
  77.4 2.3 %copy-start.12 = (bf16[80,1024]{1,0:T(8,128)(2,1)}, bf16[80,1024]{1,0:T(8,128)(2,1)S(1)}, u32[]{:S(2)}) copy-start(bf16[80,1024]{1,0:T(8,128)(2,1)S(1)} %collective-permute-done.5.refs_1_.refs_5_) | copy-start | bytes 491524
  77.4 2.3 %copy-start.13 = (bf16[80,1024]{1,0:T(8,128)(2,1)}, bf16[80,1024]{1,0:T(8,128)(2,1)S(1)}, u32[]{:S(2)}) copy-start(bf16[80,1024]{1,0:T(8,128)(2,1)S(1)} %collective-permute-done.6.refs_2_.refs_6_) | copy-start | bytes 491524
  77.5 2.3 %copy-start.14 = (bf16[80,1024]{1,0:T(8,128)(2,1)}, bf16[80,1024]{1,0:T(8,128)(2,1)S(1)}, u32[]{:S(2)}) copy-start(bf16[80,1024]{1,0:T(8,128)(2,1)S(1)} %collective-permute-done.7.refs_3_.refs_7_) | copy-start | bytes 491524
  79.8 6.5 %copy-start.15 = (bf16[320,1024]{1,0:T(8,128)(2,1)}, bf16[320,1024]{1,0:T(8,128)(2,1)S(1)}, u32[]{:S(2)}) copy-start(bf16[320,1024]{1,0:T(8,128)(2,1)S(1)} %get-tuple-element.38.refs_12_) | copy-start | bytes 1966084
  79.8 6.5 %copy-start.16 = (bf16[320,1024]{1,0:T(8,128)(2,1)}, bf16[320,1024]{1,0:T(8,128)(2,1)S(1)}, u32[]{:S(2)}) copy-start(bf16[320,1024]{1,0:T(8,128)(2,1)S(1)} %get-tuple-element.41.refs_15_) | copy-start | bytes 1966084
  79.8 1.5 %collective-permute-start.9 = (bf16[80,1024]{1,0:T(8,128)(2,1)S(1)}, bf16[80,1024]{1,0:T(8,128)(2,1)S(1)}, u32[]{:S(2)}, u32[]{:S(2)}) collective-permute-start(bf16[80,1024]{1,0:T(8,128)(2,1)S(1)} %get-tuple-element.52), channel_id=1, source_target_pairs={{0,1},{1,0},{2,3},{3,2},{4,5},{5,4},{6,7},{7,6},{8,9},{9,8},{10,11... | collective-permute-start | bytes 491528 | tf_op jit(solution)/shard_map/ppermute | solution.py:45
  80.3 1.4 %collective-permute-start.8 = (bf16[80,1024]{1,0:T(8,128)(2,1)S(1)}, bf16[80,1024]{1,0:T(8,128)(2,1)S(1)}, u32[]{:S(2)}, u32[]{:S(2)}) collective-permute-start(bf16[80,1024]{1,0:T(8,128)(2,1)S(1)} %get-tuple-element.51), channel_id=1, source_target_pairs={{0,1},{1,0},{2,3},{3,2},{4,5},{5,4},{6,7},{7,6},{8,9},{9,8},{10,11... | collective-permute-start | bytes 491528 | tf_op jit(solution)/shard_map/ppermute | solution.py:45
  81.8 4.5 %copy-start.9 = (bf16[320,1024]{1,0:T(8,128)(2,1)}, bf16[320,1024]{1,0:T(8,128)(2,1)S(1)}, u32[]{:S(2)}) copy-start(bf16[320,1024]{1,0:T(8,128)(2,1)S(1)} %collective-permute-done.2.refs_1_.refs_10_) | copy-start | bytes 1966084
  81.8 2.2 %collective-permute-start.11 = (bf16[320,1024]{1,0:T(8,128)(2,1)S(1)}, bf16[320,1024]{1,0:T(8,128)(2,1)S(1)}, u32[]{:S(2)}, u32[]{:S(2)}) collective-permute-start(bf16[320,1024]{1,0:T(8,128)(2,1)S(1)} %collective-permute-done.2.refs_1_.refs_10_), channel_id=1, source_target_pairs={{0,1},{1,0},{2,3},{3,2},{4,5},{5,4},{6,7},{7,6},{8,9},{9,8},{10,11... | collective-permute-start | bytes 1966088 | tf_op jit(solution)/shard_map/ppermute | solution.py:45
  82.2 9.9 %collective-permute-start.14 = (bf16[160,1024]{1,0:T(8,128)(2,1)S(1)}, bf16[160,1024]{1,0:T(8,128)(2,1)S(1)}, u32[]{:S(2)}, u32[]{:S(2)}) collective-permute-start(bf16[160,1024]{1,0:T(8,128)(2,1)S(1)} %add_convert_fusion), channel_id=1, source_target_pairs={{0,2},{2,0},{1,3},{3,1},{4,6},{6,4},{5,7},{7,5},{8,10},{10,8},{9,1... | collective-permute-start | bytes 983048 | tf_op jit(solution)/shard_map/ppermute | solution.py:49
  84.0 2.3 %copy-start.10 = (bf16[320,1024]{1,0:T(8,128)(2,1)}, bf16[320,1024]{1,0:T(8,128)(2,1)S(1)}, u32[]{:S(2)}) copy-start(bf16[320,1024]{1,0:T(8,128)(2,1)S(1)} %collective-permute-done.11.refs_0_.refs_9_) | copy-start | bytes 1966084
  86.3 6.8 %copy-start.17 = (bf16[320,1024]{1,0:T(8,128)(2,1)}, bf16[320,1024]{1,0:T(8,128)(2,1)S(1)}, u32[]{:S(2)}) copy-start(bf16[320,1024]{1,0:T(8,128)(2,1)S(1)} %get-tuple-element.39.refs_13_) | copy-start | bytes 1966084
  86.3 6.8 %copy-start.18 = (bf16[320,1024]{1,0:T(8,128)(2,1)}, bf16[320,1024]{1,0:T(8,128)(2,1)S(1)}, u32[]{:S(2)}) copy-start(bf16[320,1024]{1,0:T(8,128)(2,1)S(1)} %get-tuple-element.42.refs_16_) | copy-start | bytes 1966084
  86.3 1.5 %collective-permute-start.12 = (bf16[80,1024]{1,0:T(8,128)(2,1)S(1)}, bf16[80,1024]{1,0:T(8,128)(2,1)S(1)}, u32[]{:S(2)}, u32[]{:S(2)}) collective-permute-start(bf16[80,1024]{1,0:T(8,128)(2,1)S(1)} %get-tuple-element.50), channel_id=1, source_target_pairs={{0,1},{1,0},{2,3},{3,2},{4,5},{5,4},{6,7},{7,6},{8,9},{9,8},{10,11... | collective-permute-start | bytes 491528 | tf_op jit(solution)/shard_map/ppermute | solution.py:45
  86.7 1.4 %collective-permute-start.13 = (bf16[80,1024]{1,0:T(8,128)(2,1)S(1)}, bf16[80,1024]{1,0:T(8,128)(2,1)S(1)}, u32[]{:S(2)}, u32[]{:S(2)}) collective-permute-start(bf16[80,1024]{1,0:T(8,128)(2,1)S(1)} %get-tuple-element.49), channel_id=1, source_target_pairs={{0,1},{1,0},{2,3},{3,2},{4,5},{5,4},{6,7},{7,6},{8,9},{9,8},{10,11... | collective-permute-start | bytes 491528 | tf_op jit(solution)/shard_map/ppermute | solution.py:45
  92.0 9.1 %collective-permute-start.15 = (bf16[1280,128]{1,0:T(8,128)(2,1)S(1)}, bf16[1280,128]{1,0:T(8,128)(2,1)S(1)}, u32[]{:S(2)}, u32[]{:S(2)}) collective-permute-start(bf16[1280,128]{1,0:T(8,128)(2,1)S(1)} %shard_map.100), channel_id=1, source_target_pairs={{0,2},{2,0},{1,3},{3,1},{4,6},{6,4},{5,7},{7,5},{8,10},{10,8},{9,1... | collective-permute-start | bytes 983048 | tf_op jit(solution)/shard_map/ppermute | solution.py:49
  102.0 29.0 %all-to-all-start.1 = ((bf16[64,40,128]{2,1,0:T(8,128)(2,1)}), bf16[64,40,128]{2,1,0:T(8,128)(2,1)S(1)}, u32[]{:S(2)}, u32[]{:S(2)}) async-start(bf16[64,40,128]{2,1,0:T(8,128)(2,1)} %bitcast.7), calls=%async_computation.1 | async-start | bytes 1310720 | tf_op jit(solution)/shard_map/all_to_all | solution.py:206
  110.1 20.9 %copy-start.3 = (s32[128,2]{0,1:T(2,128)S(1)}, s32[128,2]{0,1:T(2,128)}, u32[]{:S(2)}) copy-start(s32[128,2]{0,1:T(2,128)} %param.9) | copy-start | bytes 3076
  110.2 20.9 %copy-start.4 = (s32[128,2]{0,1:T(2,128)S(1)}, s32[128,2]{0,1:T(2,128)}, u32[]{:S(2)}) copy-start(s32[128,2]{0,1:T(2,128)} %param.10) | copy-start | bytes 3076

commit v6 on v4

--- a/solution.py
+++ b/solution.py
@@ -15,8 +15,8 @@
 TO_CORE = ((0, 1), (1, 0), (2, 3), (3, 2))
 TO_CHIP = ((0, 2), (2, 0), (1, 3), (3, 1))
 SPLIT = (32, 32)
-FAR = 4
-BACK = 2
+FAR = (4, 1)
+BACK = (2, 2)
 SMALL = 16 * 2**20
 LARGE = 56 * 2**20
 EXPERT = 24 * 2**20
@@ -230,12 +230,12 @@
         if i:
             chip, sent, back_own = barrier((chip, sent, back_own))
             sums.append(to_chip(sent))
-        blocks = [core_pieces(chip, FAR), [chip]]
+        blocks = [core_pieces(chip, FAR[i]), [chip]]
         active, grad_hidden, away, near = expert_step(blocks, w_in, w_out)
         made.append((blocks, active, grad_hidden))
         if sums:
             near, sums[-1] = barrier((near, sums[-1]))
-        sent = (near + jnp.concatenate(core_pieces(away, BACK), axis=0).astype(F32)).astype(BF)
+        sent = (near + jnp.concatenate(core_pieces(away, BACK[i]), axis=0).astype(F32)).astype(BF)
     sums.append(to_chip(sent))
     per = width // LANES
     n = sums[0].shape[0]

time: 133 us -> 133 us (level)
    ppermute x15 -> x12, starting transfers between devices: 4.37 us -> 3.58 us  [to_core(): return lax.ppermute(rows, 'replica', TO_CORE)]
  transfers between devices with their start and end apart: 20 -> 17, of which waited for: 8 -> 7; matrix products, arithmetic and copies ran while one was open for 0% -> 0% of each run, Pallas kernels for 17% -> 17%
where the time goes in v6:
time: 133 us
  blocking collectives  50 us (38%)
  waiting for transfers between devices  38.6 us (29%)
  Pallas kernels  26.1 us (20%)
  starting transfers between devices  15.2 us (11%)
    all_to_all x1, blocking collectives, exchange(): lax.all_to_all(blocks.reshape(experts, -1, LANES), 'expert', split_axis=0...  50 us
    ppermute x4, waiting for transfers between devices, to_chip(): return lax.ppermute(rows, 'replica', TO_CHIP)  28 us
    pallas_call x1, Pallas kernels, weight_grads(): kernel_call(functools.partial(weight_grads_kernel, groups), [shape(width,...  12.7 us
    pallas_call x3, Pallas kernels, expert_step(): kernel_call(functools.partial(expert_kernel, counts), [shape(rows, units)...  8.71 us
    all_to_all x1, waiting for transfers between devices, exchange(): lax.all_to_all(blocks.reshape(experts, -1, LANES), 'expert', split_axis=0...  8.1 us
    all_to_all x1, starting transfers between devices, exchange(): lax.all_to_all(blocks.reshape(experts, -1, LANES), 'expert', split_axis=0...  8.09 us
    ppermute x12, starting transfers between devices, to_core(): return lax.ppermute(rows, 'replica', TO_CORE)  3.58 us
    ppermute x4, starting transfers between devices, to_chip(): return lax.ppermute(rows, 'replica', TO_CHIP)  3.55 us
  transfers between devices with their start and end apart: 17, of which 7 were waited for; matrix products, arithmetic and copies ran while one was open for 0% of the time, Pallas kernels for 17%

profile of v6, /device:TPU:32, one launch (start us, length us, event | category | flops | bytes accessed | tf_op | source)
XLA Modules:
  0.0 132.6 jit_solution(1281883750038215062)
XLA Ops:
  0.6 2.9 %shard_map.94 = bf16[5120,128]{1,0:T(8,128)(2,1)} custom-call(bf16[128,1024]{1,0:T(8,128)(2,1)} %tokens.1, bf16[128,1024]{1,0:T(8,128)(2,1)} %upstream.1, s32[2,128]{1,0:T(2,128)} %bitcast.26, s32[2,128]{1,0:T(2,128)} %bitcast.27, f32[2,128]{1,0:T(2,128)} %bitcast.28), custom_call_target="tpu_custom_call" | custom-call | flops 1 | bytes 1 | tf_op jit(solution)/shard_map/pallas_call | solution.py:202
  3.5 50.0 %all_to_all.10 = bf16[64,80,128]{2,1,0:T(8,128)(2,1)S(1)} all-to-all(bf16[64,80,128]{2,1,0:T(8,128)(2,1)} %bitcast.25), channel_id=1, replica_groups=mesh['expert'=64,'replica'=4] {'expert'}, dimensions={0} | all-to-all | bytes 2621440 | tf_op jit(solution)/shard_map/all_to_all | solution.py:191
  53.5 0.3 shard_map.95.refs_2_
  53.8 0.0 copy-start.1
  53.8 0.0 copy-start.3
  53.8 0.8 collective-permute-start.3
  54.6 0.0 collective-permute-start
  54.6 0.3 shard_map.96.refs_3_
  54.8 0.0 copy-start.2
  54.8 0.6 collective-permute-start.1
  55.4 1.3 %collective-permute-start.2 = (bf16[320,1024]{1,0:T(8,128)(2,1)S(1)}, bf16[320,1024]{1,0:T(8,128)(2,1)S(1)}, u32[]{:S(2)}, u32[]{:S(2)}) collective-permute-start(bf16[320,1024]{1,0:T(8,128)(2,1)S(1)} %shard_map.96.refs_3_), channel_id=1, source_target_pairs={{0,2},{2,0},{1,3},{3,1},{4,6},{6,4},{5,7},{7,5},{8,10},{10,8},{9,1... | collective-permute-start | bytes 1966088 | tf_op jit(solution)/shard_map/ppermute | solution.py:49
  56.8 14.8 %collective-permute-done.3.refs_4_.refs_8_ = bf16[320,1024]{1,0:T(8,128)(2,1)S(1)} collective-permute-done((bf16[320,1024]{1,0:T(8,128)(2,1)S(1)}, bf16[320,1024]{1,0:T(8,128)(2,1)S(1)}, u32[]{:S(2)}, u32[]{:S(2)}) %collective-permute-start.3) | collective-permute-done | bytes 655392 | tf_op jit(solution)/shard_map/ppermute | solution.py:49
  71.6 0.1 collective-permute-start.4
  71.7 0.5 collective-permute-start.5
  72.2 0.0 collective-permute-done.refs_0_
  72.2 0.1 collective-permute-start.6
  72.3 0.0 collective-permute-done.1.refs_1_
  72.3 0.4 collective-permute-start.7
  72.7 0.0 copy-done.1
  72.7 0.0 copy-done.4
  72.7 0.0 copy-done.3
  72.7 4.3 %shard_map.97 = (bf16[640,1024]{1,0:T(8,128)(2,1)S(1)}, bf16[640,1024]{1,0:T(8,128)(2,1)S(1)}, bf16[320,1024]{1,0:T(8,128)(2,1)S(1)}, f32[320,1024]{1,0:T(8,128)S(1)}) custom-call(bf16[320,1024]{1,0:T(8,128)(2,1)S(1)} %collective-permute-done.refs_0_, bf16[320,1024]{1,0:T(8,128)(2,1)S(1)} %collective-permute-done.1.refs_1_, ...), custom_call_target="tpu_custom_call" | custom-call | flops 4026531840 | bytes 13369344 | tf_op jit(solution)/shard_map/pallas_call | solution.py:125
  77.0 0.0 collective-permute-done.4.refs_0_.refs_4_
  77.1 0.0 copy-start.9
  77.1 0.4 collective-permute-start.10
  77.4 0.0 collective-permute-done.5.refs_1_.refs_5_
  77.4 0.0 collective-permute-done.6.refs_2_.refs_6_
  77.5 0.0 collective-permute-done.7.refs_3_.refs_7_
  77.5 2.2 %shard_map.98 = (bf16[320,1024]{1,0:T(8,128)(2,1)S(1)}, bf16[320,1024]{1,0:T(8,128)(2,1)S(1)}, bf16[160,1024]{1,0:T(8,128)(2,1)S(1)}, f32[160,1024]{1,0:T(8,128)S(1)}) custom-call(bf16[80,1024]{1,0:T(8,128)(2,1)S(1)} %collective-permute-done.4.refs_0_.refs_4_, bf16[80,1024]{1,0:T(8,128)(2,1)S(1)} %collective-permute-done.5.refs_1_.refs_5_, ...), custom_call_target="tpu_custom_call" | custom-call | flops 2013265920 | bytes 8781824 | tf_op jit(solution)/shard_map/pallas_call | solution.py:125
  79.7 0.0 copy-done.17
  79.7 0.0 copy-done.18
  79.7 0.0 copy-done.9
  79.7 0.0 copy-done.10
  79.8 0.0 copy-done.11
  79.8 0.0 copy-done.12
  79.8 0.0 copy-start.13
  79.8 0.0 copy-start.14
  79.8 0.5 collective-permute-start.9
  80.3 0.1 collective-permute-start.8
  80.4 0.9 collective-permute-done.9
  81.3 0.4 collective-permute-done.8
  81.7 0.1 add_convert_fusion.1
  81.8 0.0 collective-permute-done.2.refs_1_.refs_10_
  81.8 0.0 collective-permute-done.10.back
  81.8 0.3 collective-permute-start.11
  82.2 0.7 collective-permute-start.12
  82.8 0.0 copy-done.13
  82.8 1.2 collective-permute-done.11.refs_0_.refs_9_
  84.0 2.2 %shard_map.99 = (bf16[320,1024]{1,0:T(8,128)(2,1)S(1)}, bf16[320,1024]{1,0:T(8,128)(2,1)S(1)}, bf16[160,1024]{1,0:T(8,128)(2,1)S(1)}, f32[160,1024]{1,0:T(8,128)S(1)}) custom-call(bf16[320,1024]{1,0:T(8,128)(2,1)S(1)} %collective-permute-done.11.refs_0_.refs_9_, bf16[320,1024]{1,0:T(8,128)(2,1)S(1)} %collective-permute-done.2.refs_1_.refs_10_, ...), custom_call_target="tpu_custom_call" | custom-call | flops 2013265920 | bytes 8781824 | tf_op jit(solution)/shard_map/pallas_call | solution.py:125
  86.3 0.3 collective-permute-start.14
  86.6 0.3 collective-permute-start.13
  86.9 5.1 %collective-permute-done.12.chip = bf16[160,1024]{1,0:T(8,128)(2,1)S(1)} collective-permute-done((bf16[160,1024]{1,0:T(8,128)(2,1)S(1)}, bf16[160,1024]{1,0:T(8,128)(2,1)S(1)}, u32[]{:S(2)}, u32[]{:S(2)}) %collective-permute-start.12) | collective-permute-done | bytes 327712 | tf_op jit(solution)/shard_map/ppermute | solution.py:49
  92.0 0.0 collective-permute-done.14
  92.0 0.0 collective-permute-done.13
  92.0 0.1 add_convert_fusion
  92.1 0.8 collective-permute-start.15
  92.9 0.3 shard_map.100
  93.2 8.1 %collective-permute-done.15.chip = bf16[160,1024]{1,0:T(8,128)(2,1)S(1)} collective-permute-done((bf16[160,1024]{1,0:T(8,128)(2,1)S(1)}, bf16[160,1024]{1,0:T(8,128)(2,1)S(1)}, u32[]{:S(2)}, u32[]{:S(2)}) %collective-permute-start.15) | collective-permute-done | bytes 327712 | tf_op jit(solution)/shard_map/ppermute | solution.py:49
  101.3 1.0 shard_map.101
  102.3 8.1 %all-to-all-start.1 = ((bf16[64,40,128]{2,1,0:T(8,128)(2,1)}), bf16[64,40,128]{2,1,0:T(8,128)(2,1)S(1)}, u32[]{:S(2)}, u32[]{:S(2)}) async-start(bf16[64,40,128]{2,1,0:T(8,128)(2,1)} %bitcast.9), calls=%async_computation.1 | async-start | bytes 1310720 | tf_op jit(solution)/shard_map/all_to_all | solution.py:191
  110.5 12.7 %shard_map.102 = (bf16[1024,1024]{1,0:T(8,128)(2,1)}, bf16[1024,1024]{1,0:T(8,128)(2,1)}) custom-call(bf16[320,1024]{1,0:T(8,128)(2,1)} %copy-done.5, bf16[320,1024]{1,0:T(8,128)(2,1)} %copy-done.6, bf16[320,1024]{1,0:T(8,128)(2,1)} %copy-done.1, bf16[320,1024]{1,0:T(8,128)(2,1)} %copy-done.2, bf16[80,1024]{1,0:T(8,128)(2,1)} %copy-done.9, ...), custom_call_target="tpu_custom_call" | custom-call | flops 5368709120 | bytes 14680064 | tf_op jit(solution)/shard_map/pallas_call | solution.py:158
  123.2 8.1 %all-to-all-done.1 = bf16[64,40,128]{2,1,0:T(8,128)(2,1)S(1)} async-done(((bf16[64,40,128]{2,1,0:T(8,128)(2,1)}), bf16[64,40,128]{2,1,0:T(8,128)(2,1)S(1)}, u32[]{:S(2)}, u32[]{:S(2)}) %all-to-all-start.1) | async-done | bytes 655392 | tf_op jit(solution)/shard_map/all_to_all | solution.py:191
  131.3 0.3 reshape_reshape.3
  131.6 1.1 convolution_convert_fusion
  (31 shorter events, 0.2 us)
Async XLA Ops:
  53.5 19.2 %copy-start.4 = (bf16[1,1024,1024]{2,1,0:T(8,128)(2,1)S(1)}, bf16[1,1024,1024]{2,1,0:T(8,128)(2,1)}, u32[]{:S(2)}) copy-start(bf16[1,1024,1024]{2,1,0:T(8,128)(2,1)} %param.13) | copy-start | bytes 6291460
  53.8 18.9 %copy-start.1 = (bf16[320,1024]{1,0:T(8,128)(2,1)}, bf16[320,1024]{1,0:T(8,128)(2,1)S(1)}, u32[]{:S(2)}) copy-start(bf16[320,1024]{1,0:T(8,128)(2,1)S(1)} %shard_map.95.refs_2_) | copy-start | bytes 1966084
  53.8 18.9 %copy-start.3 = (bf16[1,1024,1024]{2,1,0:T(8,128)(2,1)S(1)}, bf16[1,1024,1024]{2,1,0:T(8,128)(2,1)}, u32[]{:S(2)}) copy-start(bf16[1,1024,1024]{2,1,0:T(8,128)(2,1)} %param.12) | copy-start | bytes 6291460
  53.8 17.8 %collective-permute-start.3 = (bf16[320,1024]{1,0:T(8,128)(2,1)S(1)}, bf16[320,1024]{1,0:T(8,128)(2,1)S(1)}, u32[]{:S(2)}, u32[]{:S(2)}) collective-permute-start(bf16[320,1024]{1,0:T(8,128)(2,1)S(1)} %shard_map.95.refs_2_), channel_id=1, source_target_pairs={{0,2},{2,0},{1,3},{3,1},{4,6},{6,4},{5,7},{7,5},{8,10},{10,8},{9,1... | collective-permute-start | bytes 1966088 | tf_op jit(solution)/shard_map/ppermute | solution.py:49
  54.6 17.6 %collective-permute-start = (bf16[320,1024]{1,0:T(8,128)(2,1)S(1)}, bf16[320,1024]{1,0:T(8,128)(2,1)S(1)}, u32[]{:S(2)}, u32[]{:S(2)}) collective-permute-start(bf16[320,1024]{1,0:T(8,128)(2,1)S(1)} %shard_map.95.refs_2_), channel_id=1, source_target_pairs={{0,1},{1,0},{2,3},{3,2},{4,5},{5,4},{6,7},{7,6},{8,9},{9,8},{10,11... | collective-permute-start | bytes 1966088 | tf_op jit(solution)/shard_map/ppermute | solution.py:45
  54.8 22.2 %copy-start.2 = (bf16[320,1024]{1,0:T(8,128)(2,1)}, bf16[320,1024]{1,0:T(8,128)(2,1)S(1)}, u32[]{:S(2)}) copy-start(bf16[320,1024]{1,0:T(8,128)(2,1)S(1)} %shard_map.96.refs_3_) | copy-start | bytes 1966084
  54.8 17.5 %collective-permute-start.1 = (bf16[320,1024]{1,0:T(8,128)(2,1)S(1)}, bf16[320,1024]{1,0:T(8,128)(2,1)S(1)}, u32[]{:S(2)}, u32[]{:S(2)}) collective-permute-start(bf16[320,1024]{1,0:T(8,128)(2,1)S(1)} %shard_map.96.refs_3_), channel_id=1, source_target_pairs={{0,1},{1,0},{2,3},{3,2},{4,5},{5,4},{6,7},{7,6},{8,9},{9,8},{10,11... | collective-permute-start | bytes 1966088 | tf_op jit(solution)/shard_map/ppermute | solution.py:45
  55.4 26.4 %collective-permute-start.2 = (bf16[320,1024]{1,0:T(8,128)(2,1)S(1)}, bf16[320,1024]{1,0:T(8,128)(2,1)S(1)}, u32[]{:S(2)}, u32[]{:S(2)}) collective-permute-start(bf16[320,1024]{1,0:T(8,128)(2,1)S(1)} %shard_map.96.refs_3_), channel_id=1, source_target_pairs={{0,2},{2,0},{1,3},{3,1},{4,6},{6,4},{5,7},{7,5},{8,10},{10,8},{9,1... | collective-permute-start | bytes 1966088 | tf_op jit(solution)/shard_map/ppermute | solution.py:49
  71.5 5.9 %copy-start = (bf16[320,1024]{1,0:T(8,128)(2,1)}, bf16[320,1024]{1,0:T(8,128)(2,1)S(1)}, u32[]{:S(2)}) copy-start(bf16[320,1024]{1,0:T(8,128)(2,1)S(1)} %collective-permute-done.3.refs_4_.refs_8_) | copy-start | bytes 1966084
  71.6 5.5 %collective-permute-start.4 = (bf16[80,1024]{1,0:T(8,128)(2,1)S(1)}, bf16[80,1024]{1,0:T(8,128)(2,1)S(1)}, u32[]{:S(2)}, u32[]{:S(2)}) collective-permute-start(bf16[80,1024]{1,0:T(8,128)(2,1)S(1)} %get-tuple-element.48), channel_id=1, source_target_pairs={{0,1},{1,0},{2,3},{3,2},{4,5},{5,4},{6,7},{7,6},{8,9},{9,8},{10,11... | collective-permute-start | bytes 491528 | tf_op jit(solution)/shard_map/ppermute | solution.py:45
  71.7 5.7 %collective-permute-start.5 = (bf16[80,1024]{1,0:T(8,128)(2,1)S(1)}, bf16[80,1024]{1,0:T(8,128)(2,1)S(1)}, u32[]{:S(2)}, u32[]{:S(2)}) collective-permute-start(bf16[80,1024]{1,0:T(8,128)(2,1)S(1)} %get-tuple-element.47), channel_id=1, source_target_pairs={{0,1},{1,0},{2,3},{3,2},{4,5},{5,4},{6,7},{7,6},{8,9},{9,8},{10,11... | collective-permute-start | bytes 491528 | tf_op jit(solution)/shard_map/ppermute | solution.py:45
  72.2 4.8 %copy-start.5 = (bf16[320,1024]{1,0:T(8,128)(2,1)}, bf16[320,1024]{1,0:T(8,128)(2,1)S(1)}, u32[]{:S(2)}) copy-start(bf16[320,1024]{1,0:T(8,128)(2,1)S(1)} %collective-permute-done.refs_0_) | copy-start | bytes 1966084
  72.2 5.3 %collective-permute-start.6 = (bf16[80,1024]{1,0:T(8,128)(2,1)S(1)}, bf16[80,1024]{1,0:T(8,128)(2,1)S(1)}, u32[]{:S(2)}, u32[]{:S(2)}) collective-permute-start(bf16[80,1024]{1,0:T(8,128)(2,1)S(1)} %get-tuple-element.46), channel_id=1, source_target_pairs={{0,1},{1,0},{2,3},{3,2},{4,5},{5,4},{6,7},{7,6},{8,9},{9,8},{10,11... | collective-permute-start | bytes 491528 | tf_op jit(solution)/shard_map/ppermute | solution.py:45
  72.3 4.7 %copy-start.6 = (bf16[320,1024]{1,0:T(8,128)(2,1)}, bf16[320,1024]{1,0:T(8,128)(2,1)S(1)}, u32[]{:S(2)}) copy-start(bf16[320,1024]{1,0:T(8,128)(2,1)S(1)} %collective-permute-done.1.refs_1_) | copy-start | bytes 1966084
  72.3 5.2 %collective-permute-start.7 = (bf16[80,1024]{1,0:T(8,128)(2,1)S(1)}, bf16[80,1024]{1,0:T(8,128)(2,1)S(1)}, u32[]{:S(2)}, u32[]{:S(2)}) collective-permute-start(bf16[80,1024]{1,0:T(8,128)(2,1)S(1)} %get-tuple-element.45), channel_id=1, source_target_pairs={{0,1},{1,0},{2,3},{3,2},{4,5},{5,4},{6,7},{7,6},{8,9},{9,8},{10,11... | collective-permute-start | bytes 491528 | tf_op jit(solution)/shard_map/ppermute | solution.py:45
  77.0 2.7 %copy-start.17 = (bf16[640,1024]{1,0:T(8,128)(2,1)}, bf16[640,1024]{1,0:T(8,128)(2,1)S(1)}, u32[]{:S(2)}) copy-start(bf16[640,1024]{1,0:T(8,128)(2,1)S(1)} %get-tuple-element.37.refs_11_) | copy-start | bytes 3932164
  77.0 2.7 %copy-start.18 = (bf16[640,1024]{1,0:T(8,128)(2,1)}, bf16[640,1024]{1,0:T(8,128)(2,1)S(1)}, u32[]{:S(2)}) copy-start(bf16[640,1024]{1,0:T(8,128)(2,1)S(1)} %get-tuple-element.40.refs_14_) | copy-start | bytes 3932164
  77.1 2.7 %copy-start.9 = (bf16[80,1024]{1,0:T(8,128)(2,1)}, bf16[80,1024]{1,0:T(8,128)(2,1)S(1)}, u32[]{:S(2)}) copy-start(bf16[80,1024]{1,0:T(8,128)(2,1)S(1)} %collective-permute-done.4.refs_0_.refs_4_) | copy-start | bytes 491524
  77.1 4.8 %collective-permute-start.10 = (bf16[320,1024]{1,0:T(8,128)(2,1)S(1)}, bf16[320,1024]{1,0:T(8,128)(2,1)S(1)}, u32[]{:S(2)}, u32[]{:S(2)}) collective-permute-start(bf16[320,1024]{1,0:T(8,128)(2,1)S(1)} %get-tuple-element.27), channel_id=1, source_target_pairs={{0,1},{1,0},{2,3},{3,2},{4,5},{5,4},{6,7},{7,6},{8,9},{9,8},{10,11... | collective-permute-start | bytes 1966088 | tf_op jit(solution)/shard_map/ppermute | solution.py:45
  77.4 2.3 %copy-start.10 = (bf16[80,1024]{1,0:T(8,128)(2,1)}, bf16[80,1024]{1,0:T(8,128)(2,1)S(1)}, u32[]{:S(2)}) copy-start(bf16[80,1024]{1,0:T(8,128)(2,1)S(1)} %collective-permute-done.5.refs_1_.refs_5_) | copy-start | bytes 491524
  77.4 2.3 %copy-start.11 = (bf16[80,1024]{1,0:T(8,128)(2,1)}, bf16[80,1024]{1,0:T(8,128)(2,1)S(1)}, u32[]{:S(2)}) copy-start(bf16[80,1024]{1,0:T(8,128)(2,1)S(1)} %collective-permute-done.6.refs_2_.refs_6_) | copy-start | bytes 491524
  77.5 2.3 %copy-start.12 = (bf16[80,1024]{1,0:T(8,128)(2,1)}, bf16[80,1024]{1,0:T(8,128)(2,1)S(1)}, u32[]{:S(2)}) copy-start(bf16[80,1024]{1,0:T(8,128)(2,1)S(1)} %collective-permute-done.7.refs_3_.refs_7_) | copy-start | bytes 491524
  79.8 3.1 %copy-start.13 = (bf16[320,1024]{1,0:T(8,128)(2,1)}, bf16[320,1024]{1,0:T(8,128)(2,1)S(1)}, u32[]{:S(2)}) copy-start(bf16[320,1024]{1,0:T(8,128)(2,1)S(1)} %get-tuple-element.38.refs_12_) | copy-start | bytes 1966084
  79.8 3.0 %copy-start.14 = (bf16[320,1024]{1,0:T(8,128)(2,1)}, bf16[320,1024]{1,0:T(8,128)(2,1)S(1)}, u32[]{:S(2)}) copy-start(bf16[320,1024]{1,0:T(8,128)(2,1)S(1)} %get-tuple-element.41.refs_15_) | copy-start | bytes 1966084
  79.8 1.5 %collective-permute-start.9 = (bf16[80,1024]{1,0:T(8,128)(2,1)S(1)}, bf16[80,1024]{1,0:T(8,128)(2,1)S(1)}, u32[]{:S(2)}, u32[]{:S(2)}) collective-permute-start(bf16[80,1024]{1,0:T(8,128)(2,1)S(1)} %get-tuple-element.52), channel_id=1, source_target_pairs={{0,1},{1,0},{2,3},{3,2},{4,5},{5,4},{6,7},{7,6},{8,9},{9,8},{10,11... | collective-permute-start | bytes 491528 | tf_op jit(solution)/shard_map/ppermute | solution.py:45
  80.3 1.4 %collective-permute-start.8 = (bf16[80,1024]{1,0:T(8,128)(2,1)S(1)}, bf16[80,1024]{1,0:T(8,128)(2,1)S(1)}, u32[]{:S(2)}, u32[]{:S(2)}) collective-permute-start(bf16[80,1024]{1,0:T(8,128)(2,1)S(1)} %get-tuple-element.51), channel_id=1, source_target_pairs={{0,1},{1,0},{2,3},{3,2},{4,5},{5,4},{6,7},{7,6},{8,9},{9,8},{10,11... | collective-permute-start | bytes 491528 | tf_op jit(solution)/shard_map/ppermute | solution.py:45
  81.8 4.4 %copy-start.7 = (bf16[320,1024]{1,0:T(8,128)(2,1)}, bf16[320,1024]{1,0:T(8,128)(2,1)S(1)}, u32[]{:S(2)}) copy-start(bf16[320,1024]{1,0:T(8,128)(2,1)S(1)} %collective-permute-done.2.refs_1_.refs_10_) | copy-start | bytes 1966084
  81.8 2.2 %collective-permute-start.11 = (bf16[320,1024]{1,0:T(8,128)(2,1)S(1)}, bf16[320,1024]{1,0:T(8,128)(2,1)S(1)}, u32[]{:S(2)}, u32[]{:S(2)}) collective-permute-start(bf16[320,1024]{1,0:T(8,128)(2,1)S(1)} %collective-permute-done.2.refs_1_.refs_10_), channel_id=1, source_target_pairs={{0,1},{1,0},{2,3},{3,2},{4,5},{5,4},{6,7},{7,6},{8,9},{9,8},{10,11... | collective-permute-start | bytes 1966088 | tf_op jit(solution)/shard_map/ppermute | solution.py:45
  82.2 9.9 %collective-permute-start.12 = (bf16[160,1024]{1,0:T(8,128)(2,1)S(1)}, bf16[160,1024]{1,0:T(8,128)(2,1)S(1)}, u32[]{:S(2)}, u32[]{:S(2)}) collective-permute-start(bf16[160,1024]{1,0:T(8,128)(2,1)S(1)} %add_convert_fusion.1), channel_id=1, source_target_pairs={{0,2},{2,0},{1,3},{3,1},{4,6},{6,4},{5,7},{7,5},{8,10},{10,8},{9,1... | collective-permute-start | bytes 983048 | tf_op jit(solution)/shard_map/ppermute | solution.py:49
  84.0 2.2 %copy-start.8 = (bf16[320,1024]{1,0:T(8,128)(2,1)}, bf16[320,1024]{1,0:T(8,128)(2,1)S(1)}, u32[]{:S(2)}) copy-start(bf16[320,1024]{1,0:T(8,128)(2,1)S(1)} %collective-permute-done.11.refs_0_.refs_9_) | copy-start | bytes 1966084
  86.3 6.9 %copy-start.15 = (bf16[320,1024]{1,0:T(8,128)(2,1)}, bf16[320,1024]{1,0:T(8,128)(2,1)S(1)}, u32[]{:S(2)}) copy-start(bf16[320,1024]{1,0:T(8,128)(2,1)S(1)} %get-tuple-element.39.refs_13_) | copy-start | bytes 1966084
  86.3 6.9 %copy-start.16 = (bf16[320,1024]{1,0:T(8,128)(2,1)}, bf16[320,1024]{1,0:T(8,128)(2,1)S(1)}, u32[]{:S(2)}) copy-start(bf16[320,1024]{1,0:T(8,128)(2,1)S(1)} %get-tuple-element.42.refs_16_) | copy-start | bytes 1966084
  86.3 5.7 %collective-permute-start.14 = (bf16[80,1024]{1,0:T(8,128)(2,1)S(1)}, bf16[80,1024]{1,0:T(8,128)(2,1)S(1)}, u32[]{:S(2)}, u32[]{:S(2)}) collective-permute-start(bf16[80,1024]{1,0:T(8,128)(2,1)S(1)} %get-tuple-element.50), channel_id=1, source_target_pairs={{0,1},{1,0},{2,3},{3,2},{4,5},{5,4},{6,7},{7,6},{8,9},{9,8},{10,11... | collective-permute-start | bytes 491528 | tf_op jit(solution)/shard_map/ppermute | solution.py:45
  86.6 5.4 %collective-permute-start.13 = (bf16[80,1024]{1,0:T(8,128)(2,1)S(1)}, bf16[80,1024]{1,0:T(8,128)(2,1)S(1)}, u32[]{:S(2)}, u32[]{:S(2)}) collective-permute-start(bf16[80,1024]{1,0:T(8,128)(2,1)S(1)} %get-tuple-element.49), channel_id=1, source_target_pairs={{0,1},{1,0},{2,3},{3,2},{4,5},{5,4},{6,7},{7,6},{8,9},{9,8},{10,11... | collective-permute-start | bytes 491528 | tf_op jit(solution)/shard_map/ppermute | solution.py:45
  92.1 9.2 %collective-permute-start.15 = (bf16[160,1024]{1,0:T(8,128)(2,1)S(1)}, bf16[160,1024]{1,0:T(8,128)(2,1)S(1)}, u32[]{:S(2)}, u32[]{:S(2)}) collective-permute-start(bf16[160,1024]{1,0:T(8,128)(2,1)S(1)} %add_convert_fusion), channel_id=1, source_target_pairs={{0,2},{2,0},{1,3},{3,1},{4,6},{6,4},{5,7},{7,5},{8,10},{10,8},{9,1... | collective-permute-start | bytes 983048 | tf_op jit(solution)/shard_map/ppermute | solution.py:49
  101.3 9.1 %copy-start.19 = (s32[128,2]{0,1:T(2,128)S(1)}, s32[128,2]{0,1:T(2,128)}, u32[]{:S(2)}) copy-start(s32[128,2]{0,1:T(2,128)} %param.9) | copy-start | bytes 3076
  101.3 9.1 %copy-start.20 = (s32[128,2]{0,1:T(2,128)S(1)}, s32[128,2]{0,1:T(2,128)}, u32[]{:S(2)}) copy-start(s32[128,2]{0,1:T(2,128)} %param.10) | copy-start | bytes 3076
  102.3 29.0 %all-to-all-start.1 = ((bf16[64,40,128]{2,1,0:T(8,128)(2,1)}), bf16[64,40,128]{2,1,0:T(8,128)(2,1)S(1)}, u32[]{:S(2)}, u32[]{:S(2)}) async-start(bf16[64,40,128]{2,1,0:T(8,128)(2,1)} %bitcast.9), calls=%async_computation.1 | async-start | bytes 1310720 | tf_op jit(solution)/shard_map/all_to_all | solution.py:191
